TPU v7x, 128 devices: a whole 4x4x4 slice. The times are simulated.
128 devices in a mesh: state: 8 (over x, core), vocab: 16 (over z, y).
Axes of the slice: x: 4, y: 4, z: 4, core: 2. Of those that a mesh axis runs over, the one named last changes fastest.
Arguments:
- state_emb: bfloat16 [8192, 512], P('state', 'vocab'), may hold values from -11 to 11
- tok_emb: bfloat16 [77824, 512], P('vocab', 'state'), may hold values from -0.70710678 to 0.70710678
- counts: bfloat16 [8192, 77824], P('state', 'vocab'), may hold values from 0 to 0.6
Outputs:
- grad_state: bfloat16 [8192, 512], P('state', 'vocab')
- grad_tok: bfloat16 [77824, 512], P('vocab', 'state')
All inputs are finite; a program needn't handle non-finite values.
Results may differ from a plain program's by a relative error of at most 0.02.
Values may be sent and summed in bfloat16 or wider, within the bound.
No kernel may reach another device: no remote copies, remote signals or barrier semaphores. Data moves between devices by JAX's collectives and lax.ppermute only.
A program may use at most 128 MiB of HBM per device.

v0:
```python
import jax
import jax.numpy as jnp
from jax import lax
from jax.sharding import PartitionSpec as P


def body(state_emb, tok_emb, counts):
    states = lax.all_gather(state_emb, "vocab", axis=1, tiled=True)
    tokens = lax.all_gather(tok_emb, "state", axis=1, tiled=True)
    logits = lax.dot_general(
        states, tokens, (((1,), (1,)), ((), ())), preferred_element_type=jnp.float32
    )
    local_top = jnp.max(logits, axis=1, keepdims=True)
    local_counts = jnp.sum(counts, axis=1, keepdims=True, dtype=jnp.float32)
    row_top = lax.pmax(local_top, "vocab")
    weights = jnp.exp(logits - row_top)
    row_total, row_counts = lax.psum(
        (jnp.sum(weights, axis=1, keepdims=True), local_counts), "vocab"
    )
    dlogits = (counts.astype(jnp.float32) - weights / row_total * row_counts).astype(jnp.bfloat16)
    state_part = jnp.dot(dlogits, tokens, preferred_element_type=jnp.float32)
    grad_state = lax.psum_scatter(
        state_part.astype(jnp.bfloat16), "vocab", scatter_dimension=1, tiled=True
    )
    tok_part = lax.dot_general(
        dlogits, states, (((0,), (0,)), ((), ())), preferred_element_type=jnp.float32
    )
    grad_tok = lax.psum_scatter(
        tok_part.astype(jnp.bfloat16), "state", scatter_dimension=1, tiled=True
    )
    return (grad_state, grad_tok)


def solution(mesh):
    return jax.shard_map(
        body,
        mesh=mesh,
        in_specs=(P("state", "vocab"), P("vocab", "state"), P("state", "vocab")),
        out_specs=(P("state", "vocab"), P("vocab", "state")),
        check_vma=False,
    )
```

profile of v0, /device:TPU:0, one launch (start us, length us, event | category | flops | bytes accessed | tf_op | source)
XLA Modules:
  0.0 331.1 jit_solution(11416213607978247288)
XLA Ops:
  7.2 0.0 all-gather.3.cloned.1.call-start
  7.2 0.7 all-gather.3.cloned.1.call-update
  7.9 0.0 all-gather.5.cloned.1.call-start
  7.9 0.7 all-gather.5.cloned.1.call-update
  8.6 0.0 reduce-scatter.3.cloned.1.call-start
  8.7 5.2 %convert_reduce_fusion = f32[1024]{0:T(1024)S(1)} fusion(bf16[1024,4864]{1,0:T(8,128)(2,1)} %param.5), kind=kLoop, calls=%fused_computation.1 | loop fusion | flops 9960448 | bytes 9965568 | tf_op jit(solution)/shard_map/reduce_sum | solution.py:14
  13.9 41.6 %all-gather.3.cloned.1.call-done = bf16[1024,512]{0,1:T(8,128)(2,1)} async-done(((bf16[1024,32]{0,1:T(8,128)(2,1)}), bf16[1024,512]{0,1:T(8,128)(2,1)}) %all-gather.3.cloned.1.call-update) | async-done | bytes 1048592 | tf_op jit(solution)/shard_map/all_gather | solution.py:8
  55.5 36.3 %all-gather.5.cloned.1.call-done = bf16[4864,512]{0,1:T(8,128)(2,1)} async-done(((bf16[4864,64]{0,1:T(8,128)(2,1)}), bf16[4864,512]{0,1:T(8,128)(2,1)}) %all-gather.5.cloned.1.call-update) | async-done | bytes 4980752 | tf_op jit(solution)/shard_map/all_gather | solution.py:9
  91.8 12.2 %fusion.2 = (f32[1024]{0:T(1024)S(1)}, f32[1024,4864]{1,0:T(8,128)}) fusion(bf16[1024,512]{0,1:T(8,128)(2,1)} %all-gather.3.cloned.1.call-done, bf16[4864,512]{0,1:T(8,128)(2,1)} %all-gather.5.cloned.1.call-done), kind=kOutput, calls=%fused_computation.7 | convolution fusion | flops 5105253376 | bytes 25956352 | tf_op jit(solution)/shard_map/dot_general | solution.py:10
  104.1 40.6 %pmax.7 = f32[1024]{0:T(1024)S(1)} all-reduce(f32[1024]{0:T(1024)S(1)} %get-tuple-element.4), channel_id=1, replica_groups=mesh['state'=8,'vocab'=16] {'vocab'}, use_global_device_ids=true, to_apply=%region_1.0 | all-reduce | flops 1024 | bytes 8192 | tf_op jit(solution)/shard_map/pmax | solution.py:15
  144.6 9.5 %fusion.1 = f32[1024]{0:T(1024)S(1)} fusion(f32[1024,4864]{1,0:T(8,128)} %get-tuple-element.5, f32[1024]{0:T(1024)S(1)} %pmax.7), kind=kLoop, calls=%fused_computation.4 | loop fusion | flops 9960448 | bytes 19931136 | tf_op jit(solution)/shard_map/reduce_sum | solution.py:18
  154.1 36.1 %all-reduce = (f32[1024]{0:T(1024)S(1)}, f32[1024]{0:T(1024)S(1)}) all-reduce(f32[1024]{0:T(1024)S(1)} %convert_reduce_fusion, f32[1024]{0:T(1024)S(1)} %fusion.1), channel_id=1, replica_groups=mesh['state'=8,'vocab'=16] {'vocab'}, use_global_device_ids=true, to_apply=%region_5.0 | all-reduce | flops 2048 | bytes 16384 | tf_op jit(solution)/shard_map/psum | solution.py:17
  190.3 0.0 slice-start.1
  190.3 12.9 %fusion = bf16[1024,4864]{1,0:T(8,128)(2,1)S(1)} fusion(bf16[1024,4864]{1,0:T(8,128)(2,1)} %param.5, f32[1024,4864]{1,0:T(8,128)} %get-tuple-element.5, f32[1024]{0:T(1024)S(1)} %get-tuple-element.2, f32[1024]{0:T(1024)S(1)} %get-tuple-element.3, f32[1024]{0:T(1024)S(1)} %pmax.7), kind=kLoop, calls=%fused_computation.2 | loop fusion | flops 29884416 | bytes 39858176 | tf_op jit(solution)/shard_map/convert_element_type | solution.py:20
  203.2 0.0 copy-start
  203.2 3.8 %copy-done = bf16[1024,4864]{1,0:T(8,128)(2,1)} copy-done((bf16[1024,4864]{1,0:T(8,128)(2,1)}, bf16[1024,4864]{1,0:T(8,128)(2,1)S(1)}, u32[]{:S(2)}) %copy-start) | copy-done | bytes 9961496
  207.0 0.0 slice-done.1
  207.0 6.3 %convolution_convert_fusion.1 = bf16[1024,512]{0,1:T(8,128)(2,1)} fusion(bf16[1024,4864]{1,0:T(8,128)(2,1)S(1)} %fusion, bf16[4864,512]{0,1:T(8,128)(2,1)S(1)} %bitcast.7), kind=kOutput, calls=%fused_computation.6 | convolution fusion | flops 5100797952 | bytes 15990784 | tf_op jit(solution)/shard_map/dot_general | solution.py:21
  213.3 0.0 reduce-scatter.3.cloned.1.call-update
  213.4 0.0 reduce-scatter.5.cloned.1.call-start
  213.4 10.8 %convolution_convert_fusion = bf16[4864,512]{0,1:T(8,128)(2,1)} fusion(bf16[1024,512]{0,1:T(8,128)(2,1)S(1)} %copy-done.1, bf16[1024,4864]{1,0:T(8,128)(2,1)} %copy-done), kind=kOutput, calls=%fused_computation.5 | convolution fusion | flops 5102764032 | bytes 15990784 | tf_op jit(solution)/shard_map/dot_general | solution.py:25
  224.3 0.0 reduce-scatter.5.cloned.1.call-update
  224.3 58.8 %reduce-scatter.3.cloned.1.call-done = bf16[1024,32]{0,1:T(8,128)(2,1)} async-done(((bf16[1024,512]{0,1:T(8,128)(2,1)}), bf16[1024,32]{0,1:T(8,128)(2,1)}) %reduce-scatter.3.cloned.1.call-update) | async-done | bytes 65552 | tf_op jit(solution)/shard_map/reduce_scatter | solution.py:22
  283.1 41.5 %reduce-scatter.5.cloned.1.call-done = bf16[4864,64]{0,1:T(8,128)(2,1)} async-done(((bf16[4864,512]{0,1:T(8,128)(2,1)}), bf16[4864,64]{0,1:T(8,128)(2,1)}) %reduce-scatter.5.cloned.1.call-update) | async-done | bytes 622608 | tf_op jit(solution)/shard_map/reduce_scatter | solution.py:28
  (5 shorter events, 0.0 us)
Async XLA Ops:
  7.2 48.4 %all-gather.3.cloned.1.call-start = ((), (), s32[]{:S(2)}) async-start(), calls=%async_computation.2 | async-start | bytes 1114112 | tf_op jit(solution)/shard_map/all_gather | solution.py:8
  7.9 83.9 %all-gather.5.cloned.1.call-start = ((), (), s32[]{:S(2)}) async-start(), calls=%async_computation.3 | async-start | bytes 5603328 | tf_op jit(solution)/shard_map/all_gather | solution.py:9
  8.6 274.5 %reduce-scatter.3.cloned.1.call-start = ((), (), s32[]{:S(2)}) async-start(), calls=%async_computation.4 | async-start | bytes 1114112 | tf_op jit(solution)/shard_map/reduce_scatter | solution.py:22
  144.6 62.4 %slice-start = ((s8[4980736]{0:T(1024)(128)(4,1)}), s8[786432]{0:T(1024)(128)(4,1)S(1)}, s32[]{:S(2)}) async-start(s8[4980736]{0:T(1024)(128)(4,1)} %bitcast.6), calls=%async_computation.6 | async-start | bytes 1572864
  190.3 16.8 %slice-start.1 = ((s8[4980736]{0:T(1024)(128)(4,1)}), s8[4194304]{0:T(1024)(128)(4,1)S(1)}, s32[]{:S(2)}) async-start(s8[4980736]{0:T(1024)(128)(4,1)} %bitcast.6), calls=%async_computation.7 | async-start | bytes 8388608
  203.2 3.8 %copy-start = (bf16[1024,4864]{1,0:T(8,128)(2,1)}, bf16[1024,4864]{1,0:T(8,128)(2,1)S(1)}, u32[]{:S(2)}) copy-start(bf16[1024,4864]{1,0:T(8,128)(2,1)S(1)} %fusion) | copy-start | bytes 29884420
  207.0 6.4 %copy-start.1 = (bf16[1024,512]{0,1:T(8,128)(2,1)S(1)}, bf16[1024,512]{0,1:T(8,128)(2,1)}, u32[]{:S(2)}) copy-start(bf16[1024,512]{0,1:T(8,128)(2,1)} %all-gather.3.cloned.1.call-done) | copy-start | bytes 3145732
  213.4 111.2 %reduce-scatter.5.cloned.1.call-start = ((), (), s32[]{:S(2)}) async-start(), calls=%async_computation.5 | async-start | bytes 5603328 | tf_op jit(solution)/shard_map/reduce_scatter | solution.py:28
Sparse Core Ops, SparseCore 0:
  10.1 45.3 all-gather.2
  57.2 34.5 all-gather.4
  213.5 69.5 reduce-scatter.2
  286.1 38.4 reduce-scatter.4
where the time goes:
time: 331 us
  waiting for transfers between devices  180 us (54%)
  blocking collectives  76.7 us (23%)
  matrix products  29.4 us (9%)
  other arithmetic  27.6 us (8%)
  between operations  13.8 us (4%)
  local copies, waits for them, and re-layouts  3.81 us (1%)
    reduce_scatter x1, waiting for transfers between devices, body(): lax.psum_scatter(state_part.astype(jnp.bfloat16), 'vocab', scatter_dimens...  58.8 us
    all_gather x1, waiting for transfers between devices, body(): states = lax.all_gather(state_emb, 'vocab', axis=1, tiled=True)  41.6 us
    reduce_scatter x1, waiting for transfers between devices, body(): lax.psum_scatter(tok_part.astype(jnp.bfloat16), 'state', scatter_dimensio...  41.5 us
    pmax x1, blocking collectives, body(): row_top = lax.pmax(local_top, 'vocab')  40.6 us
    all_gather x1, waiting for transfers between devices, body(): tokens = lax.all_gather(tok_emb, 'state', axis=1, tiled=True)  36.3 us
    psum x1, blocking collectives, body(): lax.psum((jnp.sum(weights, axis=1, keepdims=True), local_counts), 'vocab')  36.1 us
    convert_element_type x1, other arithmetic, body(): (counts.astype(jnp.float32) - weights / row_total * row_counts).astype(jn...  12.9 us
    dot_general x1, matrix products, body(): lax.dot_general(states, tokens, (((1,), (1,)), ((), ())), preferred_eleme...  12.2 us
  transfers between devices with their start and end apart: 4, of which 4 were waited for; matrix products, arithmetic and copies ran while one was open for 5% of the time, Pallas kernels for 0%

commit v1 on v0

v1 whole, which is shorter than its diff:
```python
import jax
import jax.numpy as jnp
from jax import lax
from jax.experimental import pallas as pl
from jax.experimental.pallas import tpu as pltpu
from jax.sharding import PartitionSpec as P

F32 = jnp.float32
BF16 = jnp.bfloat16
VMEM = pltpu.MemorySpace.VMEM
SMEM = pltpu.MemorySpace.SMEM

E = 512
ROWS = 1024
COLS = 4864
CHUNKS = ((0, 2560), (2560, 2304))
TILE = 256
NX, NY, NZ = 4, 4, 4


def core_swap(a):
    return lax.ppermute(a, "state", [(i, i ^ 1) for i in range(8)])


def x_shift(a, step):
    return lax.ppermute(a, "state", [(i, (i + 2 * step) % 8) for i in range(8)])


def shift(a, stage, step):
    perm = []
    for i in range(8):
        for j in range(16):
            z, y = divmod(j, NY)
            if (i % 2 + stage) % 2 == 0:
                y = (y + step) % NY
            else:
                z = (z + step) % NZ
            perm.append((i * 16 + j, i * 16 + z * NY + y))
    return lax.ppermute(a, ("state", "vocab"), perm)


def run(kernel, outs, *ins, flops=0, smem=0, limit=8, **kw):
    vmem = pl.BlockSpec(memory_space=VMEM)
    specs = [pl.BlockSpec(memory_space=SMEM)] * smem + [vmem] * (len(ins) - smem)
    args = list(ins[:smem]) + [pltpu.with_memory_space_constraint(a, VMEM) for a in ins[smem:]]
    moved = sum(a.size * a.dtype.itemsize for a in ins)
    return pl.pallas_call(
        kernel,
        out_shape=tuple(VMEM(shape, dtype) for shape, dtype in outs),
        in_specs=specs,
        out_specs=tuple([vmem] * len(outs)),
        compiler_params=pltpu.CompilerParams(vmem_limit_bytes=limit * 2**20),
        cost_estimate=pl.CostEstimate(flops=flops, bytes_accessed=moved, transcendentals=0),
        **kw,
    )(*args)


def eye():
    rows = lax.broadcasted_iota(jnp.int32, (128, 128), 0)
    return rows == lax.broadcasted_iota(jnp.int32, (128, 128), 1)


def to_lanes(column):
    return jnp.sum(jnp.where(eye(), jnp.broadcast_to(column, (128, 128)), 0.0), axis=0, keepdims=True)


def to_column(lanes):
    return jnp.sum(jnp.where(eye(), jnp.broadcast_to(lanes, (128, 128)), 0.0), axis=1, keepdims=True)


def assemble_kernel(off, s0, s1, s2, s3, b1, b2, b3, wide, tall):
    def put(slot, rows):
        wide[pl.ds(pl.multiple_of(off[slot], 32), 32), :] = rows

    for k, part in enumerate((s0, s1, s2, s3)):
        put(k, part[...])
    for g, part in enumerate((b1, b2, b3)):
        for k in range(4):
            put(4 * (g + 1) + k, part[32 * k : 32 * k + 32, :])
    tall[...] = wide[...].T


def softmax_kernel(s, *refs):
    parts, (w, stats, tokens), top = refs[:8], refs[8:11], refs[11]
    cols = w.shape[1]
    top[...] = jnp.full(top.shape, -jnp.inf, F32)

    def logits(i, carry):
        at = pl.ds(pl.multiple_of(i * TILE, TILE), TILE)
        tile = jnp.concatenate([p[:, at] for p in parts], axis=0)
        tokens[:, at] = tile
        out = jnp.dot(s[...], tile, preferred_element_type=F32)
        w[:, at] = out
        top[...] = jnp.maximum(top[...], jnp.maximum(out[:, :128], out[:, 128:]))
        return carry

    lax.fori_loop(0, cols // TILE, logits, 0)

    def block(r, carry):
        rows = pl.ds(pl.multiple_of(r * 128, 128), 128)
        row_top = jnp.max(top[rows, :], axis=1, keepdims=True)
        wide_top = jnp.broadcast_to(row_top, (128, 128))

        def weigh(i, acc):
            at = pl.ds(pl.multiple_of(i * 128, 128), 128)
            e = jnp.exp(w[rows, at] - wide_top)
            w[rows, at] = e
            return acc + e

        acc = lax.fori_loop(0, cols // 128, weigh, jnp.zeros((128, 128), F32), unroll=2)
        stats[pl.ds(r, 1), :] = to_lanes(row_top)
        stats[pl.ds(r + 8, 1), :] = to_lanes(jnp.sum(acc, axis=1, keepdims=True))
        return carry

    lax.fori_loop(0, ROWS // 128, block, 0)


def dlogits_kernel(w, counts, factor, s, dl, out):
    f = jnp.concatenate([to_column(factor[r : r + 1, :]) for r in range(ROWS // 128)], axis=0)

    def step(i, carry):
        at = pl.ds(pl.multiple_of(i * TILE, TILE), TILE)
        d = (counts[:, at].astype(F32) - w[:, at] * f).astype(BF16)
        dl[:, at] = d
        out[:, at] = jnp.dot(s[...], d, preferred_element_type=F32).astype(BF16)
        return carry

    lax.fori_loop(0, w.shape[1] // TILE, step, 0)


def tok_kernel(s, dl_a, dl_b, out):
    for dl, (first, width) in zip((dl_a, dl_b), CHUNKS):

        def step(i, carry):
            at = pl.ds(pl.multiple_of(i * TILE, TILE), TILE)
            to = pl.ds(pl.multiple_of(first + i * TILE, TILE), TILE)
            out[:, to] = jnp.dot(s[...], dl[:, at], preferred_element_type=F32).astype(BF16)
            return carry

        lax.fori_loop(0, width // TILE, step, 0)


def state_kernel(off, t_a, t_b, dl_a, dl_b, out, acc):
    dims = (((1,), (1,)), ((), ()))
    for q in range(4):
        rows = slice(256 * q, 256 * q + 256)
        acc[...] = lax.dot_general(t_a[...], dl_a[rows, :], dims, preferred_element_type=F32)
        acc[...] += lax.dot_general(t_b[...], dl_b[rows, :], dims, preferred_element_type=F32)
        for r in range(16):
            part = acc[pl.ds(pl.multiple_of(off[r], 32), 32), :]
            out[32 * r : 32 * r + 32, rows] = part.astype(BF16)


def combine(parts):
    tops = [p[:8] for p in parts]
    top = tops[0]
    for t in tops[1:]:
        top = jnp.maximum(top, t)
    total = sum(p[8:16] * jnp.exp(t - top) for p, t in zip(parts, tops))
    return jnp.concatenate([top, total, sum(p[16:] for p in parts)], axis=0)


def row_offsets():
    i, j = lax.axis_index("state"), lax.axis_index("vocab")
    x, c = i // 2, i % 2
    z, y = j // NY, j % NY
    slot = jnp.arange(16, dtype=jnp.int32)
    a, b = slot % 4, slot // 4
    from_y = jnp.where(c == 0, (y - a) % 4, (y - b) % 4)
    from_z = jnp.where(c == 0, (z - b) % 4, (z - a) % 4)
    k = from_z * NY + from_y
    owner = k // 2
    ahead = (owner // 2 - x) % 4
    place = jnp.where(ahead == 0, 0, jnp.where(ahead == 3, 1, jnp.where(ahead == 1, 2, 3)))
    return 128 * place + 64 * (owner % 2 != c) + 32 * (k % 2)


def add(*parts):
    return sum(p.astype(F32) for p in parts).astype(BF16)


def body(state_emb, tok_emb, counts):
    own = tok_emb.T
    s0 = state_emb.T
    off = row_offsets().astype(jnp.int32)

    halves = []
    for first, width in CHUNKS:
        t0 = own[:, first : first + width]
        halves.append((t0, x_shift(t0, 1), x_shift(t0, -1)))
    chunks = []
    for t0, t2, t4 in halves:
        far = jnp.concatenate([x_shift(t2[:32], 1), x_shift(t4[32:], -1)], axis=0)
        near = [t0, core_swap(t0), t2, core_swap(t2), t4, core_swap(t4), far, core_swap(far)]
        chunks.append(near)

    first_parts = [s0] + [shift(s0, 0, k) for k in (1, 2, 3)]
    block = jnp.concatenate(first_parts, axis=0)
    later = [shift(block, 1, k) for k in (1, 2, 3)]
    wide, tall = run(
        assemble_kernel, [((E, ROWS), BF16), ((ROWS, E), BF16)], off, *first_parts, *later, smem=1
    )

    row_counts = jnp.sum(counts, axis=1, dtype=F32).reshape(8, 128)

    weights, stats, tokens = [], [], []
    for parts, (first, width) in zip(chunks, CHUNKS):
        w, st, tk = run(
            softmax_kernel,
            [((ROWS, width), F32), ((16, 128), F32), ((E, width), BF16)],
            tall,
            *parts,
            flops=2 * ROWS * E * width,
            scratch_shapes=[pltpu.VMEM((ROWS, 128), F32)],
        )
        weights.append(w)
        stats.append(st)
        tokens.append(tk)

    none = jnp.zeros((8, 128), F32)
    total = combine(
        [jnp.concatenate([stats[0], row_counts], axis=0), jnp.concatenate([stats[1], none], axis=0)]
    )
    for stage in range(2):
        total = combine([total] + [shift(total, stage, k) for k in (1, 2, 3)])
    scale = total[16:] / total[8:16]

    dls, far_parts = [], []
    for w, st, (first, width) in zip(weights, stats, CHUNKS):
        factor = jnp.exp(st[:8] - total[:8]) * scale
        dl, part = run(
            dlogits_kernel,
            [((ROWS, width), BF16), ((128, width), BF16)],
            w,
            counts[:, first : first + width],
            factor,
            wide[384:],
            flops=2 * ROWS * 128 * width,
        )
        dls.append(dl)
        far_parts.append(part)
    far = jnp.concatenate(far_parts, axis=1)

    w6 = add(far[:64], core_swap(far[64:]))
    got_low = x_shift(w6[:32], 1)
    got_high = x_shift(w6[32:], -1)
    (mid,) = run(tok_kernel, [((256, COLS), BF16)], wide[128:384], *dls, flops=2 * ROWS * 256 * COLS)
    w2 = add(mid[:64], core_swap(mid[64:128]))
    w4 = add(mid[128:192], core_swap(mid[192:]))
    up_high = x_shift(w4[32:], 1)
    down_low = x_shift(w2[:32], -1)
    up_low = x_shift(add(w4[:32], got_low), 1)
    down_high = x_shift(add(w2[32:], got_high), -1)
    (near,) = run(tok_kernel, [((128, COLS), BF16)], wide[:128], *dls, flops=2 * ROWS * 128 * COLS)
    swapped = core_swap(near[64:])
    grad_tok = jnp.concatenate(
        [add(near[:32], swapped[:32], up_low, down_low), add(near[32:64], swapped[32:], up_high, down_high)],
        axis=0,
    )

    (g,) = run(
        state_kernel,
        [((E, ROWS), BF16)],
        off,
        *tokens,
        *dls,
        smem=1,
        flops=2 * ROWS * E * COLS,
        scratch_shapes=[pltpu.VMEM((E, 256), F32)],
    )
    g = add(g[:128], *[shift(g[128 * k : 128 * k + 128], 1, -k) for k in (1, 2, 3)])
    grad_state = add(g[:32], *[shift(g[32 * k : 32 * k + 32], 0, -k) for k in (1, 2, 3)])
    return grad_state.T, grad_tok.T


def solution(mesh):
    return jax.shard_map(
        body,
        mesh=mesh,
        in_specs=(P("state", "vocab"), P("vocab", "state"), P("state", "vocab")),
        out_specs=(P("state", "vocab"), P("vocab", "state")),
        check_vma=False,
    )
```

time: 331 us -> 168 us (0.51)
  the two profiles are of different devices: /device:TPU:0 before, /device:TPU:32 now
where the time goes in v1:
time: 168 us; the launch traced here: 167 us
  starting transfers between devices  52.4 us (31%)
  waiting for transfers between devices  45.8 us (27%)
  Pallas kernels  43 us (26%)
  local copies, waits for them, and re-layouts  16.9 us (10%)
  other arithmetic  7.91 us (5%)
    pallas_call x8, Pallas kernels, run(): pl.pallas_call(kernel, out_shape=tuple((VMEM(shape, dtype) for shape, dty...  43 us
    ppermute x14, waiting for transfers between devices, x_shift(): return lax.ppermute(a, 'state', [(i, (i + 2 * step) % 8) for i in range(8)])  42.7 us
    ppermute x18, starting transfers between devices, shift(): return lax.ppermute(a, ('state', 'vocab'), perm)  29.7 us
    ppermute x14, starting transfers between devices, x_shift(): return lax.ppermute(a, 'state', [(i, (i + 2 * step) % 8) for i in range(8)])  20 us
    unnamed x17, local copies, waits for them, and re-layouts  8.93 us
    slice x2, local copies, waits for them, and re-layouts, body(): counts[:, first:first + width]  5.47 us
    reduce_sum x1, other arithmetic, body(): row_counts = jnp.sum(counts, axis=1, dtype=F32).reshape(8, 128)  5.2 us
  transfers between devices with their start and end apart: 44, of which 13 were waited for; matrix products, arithmetic and copies ran while one was open for 8% of the time, Pallas kernels for 15%

profile of v1, /device:TPU:32, one launch (start us, length us, event | category | flops | bytes accessed | tf_op | source)
XLA Modules:
  0.0 167.2 jit_solution(4702610555184592455)
XLA Ops:
  4.8 2.9 %collective-permute-start.1 = (bf16[32,1024]{1,0:T(8,128)(2,1)}, bf16[32,1024]{1,0:T(8,128)(2,1)S(1)}, u32[]{:S(2)}, u32[]{:S(2)}) collective-permute-start(bf16[32,1024]{1,0:T(8,128)(2,1)} %bitcast.9), channel_id=1, source_target_pairs={{0,2},{1,3},{2,0},{3,1},{4,6},{5,7},{6,4},{7,5},{8,10},{9,11},{10,... | collective-permute-start | bytes 196616 | tf_op jit(solution)/shard_map/ppermute | solution.py:39
  12.2 3.0 %collective-permute-start.9 = (bf16[64,2560]{1,0:T(8,128)(2,1)S(1)}, bf16[64,2560]{1,0:T(8,128)(2,1)S(1)}, u32[]{:S(2)}, u32[]{:S(2)}) collective-permute-start(bf16[64,2560]{1,0:T(8,128)(2,1)S(1)} %slice.235.refs_0_), channel_id=1, source_target_pairs={{0,96},{16,112},{32,0},{48,16},{64,32},{80,48},{96,64},{112,80},{1... | collective-permute-start | bytes 983048 | tf_op jit(solution)/shard_map/ppermute | solution.py:26
  15.2 5.2 %convert_reduce_fusion = f32[1024]{0:T(1024)S(1)} fusion(bf16[1024,4864]{1,0:T(8,128)(2,1)} %param.5), kind=kLoop, calls=%fused_computation | loop fusion | flops 9960448 | bytes 9965568 | tf_op jit(solution)/shard_map/reduce_sum | solution.py:204
  23.0 3.0 %collective-permute-start.4 = (bf16[128,1024]{1,0:T(8,128)(2,1)S(1)}, bf16[128,1024]{1,0:T(8,128)(2,1)S(1)}, u32[]{:S(2)}, u32[]{:S(2)}) collective-permute-start(bf16[128,1024]{1,0:T(8,128)(2,1)S(1)} %pad_maximum_fusion), channel_id=1, source_target_pairs={{0,8},{1,9},{2,10},{3,11},{4,12},{5,13},{6,14},{7,15},{8,0},{9,1},... | collective-permute-start | bytes 786440 | tf_op jit(solution)/shard_map/ppermute | solution.py:39
  29.8 2.9 %collective-permute-done.20 = bf16[32,2304]{1,0:T(8,128)(2,1)S(1)} collective-permute-done((bf16[32,2304]{1,0:T(8,128)(2,1)S(1)}, bf16[32,2304]{1,0:T(8,128)(2,1)S(1)}, u32[]{:S(2)}, u32[]{:S(2)}) %collective-permute-start.20) | collective-permute-done | bytes 147488 | tf_op jit(solution)/shard_map/ppermute | solution.py:26
  32.9 6.8 %collective-permute-done.11 = bf16[32,2560]{1,0:T(8,128)(2,1)S(1)} collective-permute-done((bf16[32,2560]{1,0:T(8,128)(2,1)S(1)}, bf16[32,2560]{1,0:T(8,128)(2,1)S(1)}, u32[]{:S(2)}, u32[]{:S(2)}) %collective-permute-start.11) | collective-permute-done | bytes 163872 | tf_op jit(solution)/shard_map/ppermute | solution.py:26
  42.3 2.7 %collective-permute-done.12 = bf16[32,2560]{1,0:T(8,128)(2,1)S(1)} collective-permute-done((bf16[32,2560]{1,0:T(8,128)(2,1)S(1)}, bf16[32,2560]{1,0:T(8,128)(2,1)S(1)}, u32[]{:S(2)}, u32[]{:S(2)}) %collective-permute-start.12) | collective-permute-done | bytes 163872 | tf_op jit(solution)/shard_map/ppermute | solution.py:26
  47.3 8.3 %shard_map.52 = (f32[1024,2304]{1,0:T(8,128)S(1)}, f32[16,128]{1,0:T(8,128)S(1)}, bf16[512,2304]{1,0:T(8,128)(2,1)S(1)}) custom-call(bf16[1024,512]{1,0:T(8,128)(2,1)S(1)} %get-tuple-element.14.s, bf16[64,2304]{1,0:T(8,128)(2,1)S(1)} %slice.238.refs_0_, bf16[64,2304]{1,0:T(8,128)(2,1)S(1)} %collective-permute-done.14.refs_1_, ...), custom_call_target="tpu_custom_call" | custom-call | flops 2415919104 | bytes 3407872 | tf_op jit(solution)/shard_map/pallas_call | solution.py:47
  55.5 3.7 %copy-done = f32[1024,2304]{1,0:T(8,128)} copy-done((f32[1024,2304]{1,0:T(8,128)}, f32[1024,2304]{1,0:T(8,128)S(1)}, u32[]{:S(2)}) %copy-start) | copy-done | bytes 9437208
  59.2 9.0 %shard_map.51 = (f32[1024,2560]{1,0:T(8,128)S(1)}, f32[16,128]{1,0:T(8,128)S(1)}, bf16[512,2560]{1,0:T(8,128)(2,1)S(1)}) custom-call(bf16[1024,512]{1,0:T(8,128)(2,1)S(1)} %get-tuple-element.14.s, bf16[64,2560]{1,0:T(8,128)(2,1)S(1)} %slice.235.refs_0_, bf16[64,2560]{1,0:T(8,128)(2,1)S(1)} %collective-permute-done.6.refs_1_, ...), custom_call_target="tpu_custom_call" | custom-call | flops 2684354560 | bytes 3670016 | tf_op jit(solution)/shard_map/pallas_call | solution.py:47
  71.0 2.9 %collective-permute-start.23 = (f32[24,128]{1,0:T(8,128)S(1)}, f32[24,128]{1,0:T(8,128)S(1)}, u32[]{:S(2)}, u32[]{:S(2)}) collective-permute-start(f32[24,128]{1,0:T(8,128)S(1)} %pad_maximum_fusion.1), channel_id=1, source_target_pairs={{0,2},{1,3},{2,0},{3,1},{4,6},{5,7},{6,4},{7,5},{8,10},{9,11},{10,... | collective-permute-start | bytes 36872 | tf_op jit(solution)/shard_map/ppermute | solution.py:39
  77.8 2.8 %slice.183.counts = bf16[1024,2560]{1,0:T(8,128)(2,1)S(1)} slice(bf16[1024,4864]{1,0:T(8,128)(2,1)} %param.5), slice={[0:1024], [0:2560]} | slice | bytes 10485760 | tf_op jit(solution)/shard_map/slice | solution.py:235
  87.6 4.4 %shard_map.53 = (bf16[1024,2560]{1,0:T(8,128)(2,1)S(1)}, bf16[128,2560]{1,0:T(8,128)(2,1)S(1)}) custom-call(f32[1024,2560]{1,0:T(8,128)S(1)} %get-tuple-element.17.w, bf16[1024,2560]{1,0:T(8,128)(2,1)S(1)} %slice.183.counts, f32[8,128]{1,0:T(8,128)S(1)} %exponential_multiply_fusion.1.factor, bf16[128,1024]{1,0:T(8,128)(2,1)S(1)} %get-tuple-element.40.s), custom_call_target="tpu_custom_call" | custom-call | flops 671088640 | bytes 15994880 | tf_op jit(solution)/shard_map/pallas_call | solution.py:47
  92.1 3.7 %copy-done.1 = f32[1024,2304]{1,0:T(8,128)S(1)} copy-done((f32[1024,2304]{1,0:T(8,128)S(1)}, f32[1024,2304]{1,0:T(8,128)}, u32[]{:S(2)}) %copy-start.1) | copy-done | bytes 9437208
  95.7 3.9 %shard_map.54 = (bf16[1024,2304]{1,0:T(8,128)(2,1)S(1)}, bf16[128,2304]{1,0:T(8,128)(2,1)S(1)}) custom-call(f32[1024,2304]{1,0:T(8,128)S(1)} %copy-done.1, bf16[1024,2304]{1,0:T(8,128)(2,1)S(1)} %slice.207.counts, f32[8,128]{1,0:T(8,128)S(1)} %get-tuple-element.26.factor, bf16[128,1024]{1,0:T(8,128)(2,1)S(1)} %get-tuple-element.40.s), custom_call_target="tpu_custom_call" | custom-call | flops 603979776 | bytes 14422016 | tf_op jit(solution)/shard_map/pallas_call | solution.py:47
  99.9 5.9 %shard_map.57 = bf16[256,4864]{1,0:T(8,128)(2,1)S(1)} custom-call(bf16[256,1024]{1,0:T(8,128)(2,1)S(1)} %slice.220.s, bf16[1024,2560]{1,0:T(8,128)(2,1)S(1)} %get-tuple-element.21.dl_a, bf16[1024,2304]{1,0:T(8,128)(2,1)S(1)} %get-tuple-element.23.dl_b), custom_call_target="tpu_custom_call" | custom-call | flops 2550136832 | bytes 10485760 | tf_op jit(solution)/shard_map/pallas_call | solution.py:47
  105.8 6.1 %shard_map.55 = bf16[512,1024]{1,0:T(8,128)(2,1)S(1)} custom-call(s32[16]{0:T(128)S(1)} %fusion.10.off, bf16[512,2560]{1,0:T(8,128)(2,1)S(1)} %copy-done.4, bf16[512,2304]{1,0:T(8,128)(2,1)S(1)} %copy-done.6, bf16[1024,2560]{1,0:T(8,128)(2,1)S(1)} %get-tuple-element.21.dl_a, bf16[1024,2304]{1,0:T(8,128)(2,1)S(1)} %get-tuple-element.23.dl_b), custom_call_target="tpu_custom_call" | custom-call | flops 5100273664 | bytes 14942272 | tf_op jit(solution)/shard_map/pallas_call | solution.py:47
  117.3 4.6 %shard_map.56 = bf16[128,4864]{1,0:T(8,128)(2,1)S(1)} custom-call(bf16[128,1024]{1,0:T(8,128)(2,1)S(1)} %get-tuple-element.39.s, bf16[1024,2560]{1,0:T(8,128)(2,1)S(1)} %get-tuple-element.21.dl_a, bf16[1024,2304]{1,0:T(8,128)(2,1)S(1)} %get-tuple-element.23.dl_b), custom_call_target="tpu_custom_call" | custom-call | flops 1275068416 | bytes 10223616 | tf_op jit(solution)/shard_map/pallas_call | solution.py:47
  126.6 3.4 %collective-permute-start.42 = (bf16[32,4864]{1,0:T(8,128)(2,1)S(1)}, bf16[32,4864]{1,0:T(8,128)(2,1)S(1)}, u32[]{:S(2)}, u32[]{:S(2)}) collective-permute-start(bf16[32,4864]{1,0:T(8,128)(2,1)S(1)} %get-tuple-element.45), channel_id=1, source_target_pairs={{0,96},{16,112},{32,0},{48,16},{64,32},{80,48},{96,64},{112,80},{1... | collective-permute-start | bytes 933896 | tf_op jit(solution)/shard_map/ppermute | solution.py:26
  130.3 7.1 %collective-permute-done.42 = bf16[32,4864]{1,0:T(8,128)(2,1)S(1)} collective-permute-done((bf16[32,4864]{1,0:T(8,128)(2,1)S(1)}, bf16[32,4864]{1,0:T(8,128)(2,1)S(1)}, u32[]{:S(2)}, u32[]{:S(2)}) %collective-permute-start.42) | collective-permute-done | bytes 311328 | tf_op jit(solution)/shard_map/ppermute | solution.py:26
  137.5 10.9 %collective-permute-done.37 = bf16[32,4864]{1,0:T(8,128)(2,1)S(1)} collective-permute-done((bf16[32,4864]{1,0:T(8,128)(2,1)S(1)}, bf16[32,4864]{1,0:T(8,128)(2,1)S(1)}, u32[]{:S(2)}, u32[]{:S(2)}) %collective-permute-start.37) | collective-permute-done | bytes 311328 | tf_op jit(solution)/shard_map/ppermute | solution.py:26
  150.6 3.0 %collective-permute-start.43 = (bf16[32,4864]{1,0:T(8,128)(2,1)S(1)}, bf16[32,4864]{1,0:T(8,128)(2,1)S(1)}, u32[]{:S(2)}, u32[]{:S(2)}) collective-permute-start(bf16[32,4864]{1,0:T(8,128)(2,1)S(1)} %add_convert_fusion.4), channel_id=1, source_target_pairs={{0,96},{16,112},{32,0},{48,16},{64,32},{80,48},{96,64},{112,80},{1... | collective-permute-start | bytes 933896 | tf_op jit(solution)/shard_map/ppermute | solution.py:26
  154.2 4.5 %collective-permute-done.40 = bf16[32,4864]{1,0:T(8,128)(2,1)S(1)} collective-permute-done((bf16[32,4864]{1,0:T(8,128)(2,1)S(1)}, bf16[32,4864]{1,0:T(8,128)(2,1)S(1)}, u32[]{:S(2)}, u32[]{:S(2)}) %collective-permute-start.40) | collective-permute-done | bytes 311328 | tf_op jit(solution)/shard_map/ppermute | solution.py:26
  158.7 3.1 %collective-permute-done.41 = bf16[32,4864]{1,0:T(8,128)(2,1)S(1)} collective-permute-done((bf16[32,4864]{1,0:T(8,128)(2,1)S(1)}, bf16[32,4864]{1,0:T(8,128)(2,1)S(1)}, u32[]{:S(2)}, u32[]{:S(2)}) %collective-permute-start.41) | collective-permute-done | bytes 311328 | tf_op jit(solution)/shard_map/ppermute | solution.py:26
  (127 shorter events, 52.4 us)
Async XLA Ops:
  7.7 12.8 %collective-permute-start.2 = (bf16[32,1024]{1,0:T(8,128)(2,1)}, bf16[32,1024]{1,0:T(8,128)(2,1)S(1)}, u32[]{:S(2)}, u32[]{:S(2)}) collective-permute-start(bf16[32,1024]{1,0:T(8,128)(2,1)} %bitcast.10), channel_id=1, source_target_pairs={{0,3},{1,0},{2,1},{3,2},{4,7},{5,4},{6,5},{7,6},{8,11},{9,8},{10,9... | collective-permute-start | bytes 196616 | tf_op jit(solution)/shard_map/ppermute | solution.py:39
  9.0 11.6 %collective-permute-start.17 = (bf16[64,2304]{1,0:T(8,128)(2,1)S(1)}, bf16[64,2304]{1,0:T(8,128)(2,1)S(1)}, u32[]{:S(2)}, u32[]{:S(2)}) collective-permute-start(bf16[64,2304]{1,0:T(8,128)(2,1)S(1)} %slice.238.refs_0_), channel_id=1, source_target_pairs={{0,96},{16,112},{32,0},{48,16},{64,32},{80,48},{96,64},{112,80},{1... | collective-permute-start | bytes 884744 | tf_op jit(solution)/shard_map/ppermute | solution.py:26
  11.8 11.3 %collective-permute-start.7 = (bf16[64,2560]{1,0:T(8,128)(2,1)S(1)}, bf16[64,2560]{1,0:T(8,128)(2,1)S(1)}, u32[]{:S(2)}, u32[]{:S(2)}) collective-permute-start(bf16[64,2560]{1,0:T(8,128)(2,1)S(1)} %slice.235.refs_0_), channel_id=1, source_target_pairs={{0,32},{16,48},{32,64},{48,80},{64,96},{80,112},{96,0},{112,16},{1... | collective-permute-start | bytes 983048 | tf_op jit(solution)/shard_map/ppermute | solution.py:26
  12.2 13.9 %collective-permute-start.9 = (bf16[64,2560]{1,0:T(8,128)(2,1)S(1)}, bf16[64,2560]{1,0:T(8,128)(2,1)S(1)}, u32[]{:S(2)}, u32[]{:S(2)}) collective-permute-start(bf16[64,2560]{1,0:T(8,128)(2,1)S(1)} %slice.235.refs_0_), channel_id=1, source_target_pairs={{0,96},{16,112},{32,0},{48,16},{64,32},{80,48},{96,64},{112,80},{1... | collective-permute-start | bytes 983048 | tf_op jit(solution)/shard_map/ppermute | solution.py:26
  15.2 11.9 %collective-permute-start.19 = (bf16[32,2304]{1,0:T(8,128)(2,1)S(1)}, bf16[32,2304]{1,0:T(8,128)(2,1)S(1)}, u32[]{:S(2)}, u32[]{:S(2)}) collective-permute-start(bf16[32,2304]{1,0:T(8,128)(2,1)S(1)} %slice.239), channel_id=1, source_target_pairs={{0,32},{16,48},{32,64},{48,80},{64,96},{80,112},{96,0},{112,16},{1... | collective-permute-start | bytes 442376 | tf_op jit(solution)/shard_map/ppermute | solution.py:26
  20.4 21.3 %collective-permute-start.14 = (bf16[64,2304]{1,0:T(8,128)(2,1)S(1)}, bf16[64,2304]{1,0:T(8,128)(2,1)S(1)}, u32[]{:S(2)}, u32[]{:S(2)}) collective-permute-start(bf16[64,2304]{1,0:T(8,128)(2,1)S(1)} %slice.238.refs_0_), channel_id=1, source_target_pairs={{0,16},{16,0},{32,48},{48,32},{64,80},{80,64},{96,112},{112,96},{1... | collective-permute-start | bytes 884744 | tf_op jit(solution)/shard_map/ppermute | solution.py:22
  20.6 21.3 %collective-permute-start.3 = (bf16[128,1024]{1,0:T(8,128)(2,1)S(1)}, bf16[128,1024]{1,0:T(8,128)(2,1)S(1)}, u32[]{:S(2)}, u32[]{:S(2)}) collective-permute-start(bf16[128,1024]{1,0:T(8,128)(2,1)S(1)} %pad_maximum_fusion), channel_id=1, source_target_pairs={{0,4},{1,5},{2,6},{3,7},{4,8},{5,9},{6,10},{7,11},{8,12},{9,13},{1... | collective-permute-start | bytes 786440 | tf_op jit(solution)/shard_map/ppermute | solution.py:39
  23.0 22.0 %collective-permute-start.4 = (bf16[128,1024]{1,0:T(8,128)(2,1)S(1)}, bf16[128,1024]{1,0:T(8,128)(2,1)S(1)}, u32[]{:S(2)}, u32[]{:S(2)}) collective-permute-start(bf16[128,1024]{1,0:T(8,128)(2,1)S(1)} %pad_maximum_fusion), channel_id=1, source_target_pairs={{0,8},{1,9},{2,10},{3,11},{4,12},{5,13},{6,14},{7,15},{8,0},{9,1},... | collective-permute-start | bytes 786440 | tf_op jit(solution)/shard_map/ppermute | solution.py:39
  26.0 19.6 %collective-permute-start.5 = (bf16[128,1024]{1,0:T(8,128)(2,1)S(1)}, bf16[128,1024]{1,0:T(8,128)(2,1)S(1)}, u32[]{:S(2)}, u32[]{:S(2)}) collective-permute-start(bf16[128,1024]{1,0:T(8,128)(2,1)S(1)} %pad_maximum_fusion), channel_id=1, source_target_pairs={{0,12},{1,13},{2,14},{3,15},{4,0},{5,1},{6,2},{7,3},{8,4},{9,5},{1... | collective-permute-start | bytes 786440 | tf_op jit(solution)/shard_map/ppermute | solution.py:39
  45.1 14.1 %collective-permute-start.6 = (bf16[64,2560]{1,0:T(8,128)(2,1)S(1)}, bf16[64,2560]{1,0:T(8,128)(2,1)S(1)}, u32[]{:S(2)}, u32[]{:S(2)}) collective-permute-start(bf16[64,2560]{1,0:T(8,128)(2,1)S(1)} %slice.235.refs_0_), channel_id=1, source_target_pairs={{0,16},{16,0},{32,48},{48,32},{64,80},{80,64},{96,112},{112,96},{1... | collective-permute-start | bytes 983048 | tf_op jit(solution)/shard_map/ppermute | solution.py:22
  45.6 13.6 %collective-permute-start.10 = (bf16[64,2560]{1,0:T(8,128)(2,1)S(1)}, bf16[64,2560]{1,0:T(8,128)(2,1)S(1)}, u32[]{:S(2)}, u32[]{:S(2)}) collective-permute-start(bf16[64,2560]{1,0:T(8,128)(2,1)S(1)} %collective-permute-done.9.refs_4_), channel_id=1, source_target_pairs={{0,16},{16,0},{32,48},{48,32},{64,80},{80,64},{96,112},{112,96},{1... | collective-permute-start | bytes 983048 | tf_op jit(solution)/shard_map/ppermute | solution.py:22
  45.7 13.5 %collective-permute-start.8 = (bf16[64,2560]{1,0:T(8,128)(2,1)S(1)}, bf16[64,2560]{1,0:T(8,128)(2,1)S(1)}, u32[]{:S(2)}, u32[]{:S(2)}) collective-permute-start(bf16[64,2560]{1,0:T(8,128)(2,1)S(1)} %collective-permute-done.7.refs_2_), channel_id=1, source_target_pairs={{0,16},{16,0},{32,48},{48,32},{64,80},{80,64},{96,112},{112,96},{1... | collective-permute-start | bytes 983048 | tf_op jit(solution)/shard_map/ppermute | solution.py:22
  46.2 13.1 %collective-permute-start.13 = (bf16[64,2560]{1,0:T(8,128)(2,1)S(1)}, bf16[64,2560]{1,0:T(8,128)(2,1)S(1)}, u32[]{:S(2)}, u32[]{:S(2)}) collective-permute-start(bf16[64,2560]{1,0:T(8,128)(2,1)S(1)} %constant_dynamic-update-slice_fusion.refs_6_), channel_id=1, source_target_pairs={{0,16},{16,0},{32,48},{48,32},{64,80},{80,64},{96,112},{112,96},{1... | collective-permute-start | bytes 983048 | tf_op jit(solution)/shard_map/ppermute | solution.py:22
  69.8 10.9 %collective-permute-start.22 = (f32[24,128]{1,0:T(8,128)S(1)}, f32[24,128]{1,0:T(8,128)S(1)}, u32[]{:S(2)}, u32[]{:S(2)}) collective-permute-start(f32[24,128]{1,0:T(8,128)S(1)} %pad_maximum_fusion.1), channel_id=1, source_target_pairs={{0,1},{1,2},{2,3},{3,0},{4,5},{5,6},{6,7},{7,4},{8,9},{9,10},{10,1... | collective-permute-start | bytes 36872 | tf_op jit(solution)/shard_map/ppermute | solution.py:39
  99.8 24.6 %collective-permute-start.36 = (bf16[64,4864]{1,0:T(8,128)(2,1)S(1)}, bf16[64,4864]{1,0:T(8,128)(2,1)S(1)}, u32[]{:S(2)}, u32[]{:S(2)}) collective-permute-start(bf16[64,4864]{1,0:T(8,128)(2,1)S(1)} %slice.274), channel_id=1, source_target_pairs={{0,16},{16,0},{32,48},{48,32},{64,80},{80,64},{96,112},{112,96},{1... | collective-permute-start | bytes 1867784 | tf_op jit(solution)/shard_map/ppermute | solution.py:22
  122.5 31.7 %collective-permute-start.34 = (bf16[64,4864]{1,0:T(8,128)(2,1)S(1)}, bf16[64,4864]{1,0:T(8,128)(2,1)S(1)}, u32[]{:S(2)}, u32[]{:S(2)}) collective-permute-start(bf16[64,4864]{1,0:T(8,128)(2,1)S(1)} %slice.268), channel_id=1, source_target_pairs={{0,16},{16,0},{32,48},{48,32},{64,80},{80,64},{96,112},{112,96},{1... | collective-permute-start | bytes 1867784 | tf_op jit(solution)/shard_map/ppermute | solution.py:22
  123.4 26.8 %collective-permute-start.31 = (bf16[32,1024]{1,0:T(8,128)(2,1)S(1)}, bf16[32,1024]{1,0:T(8,128)(2,1)S(1)}, u32[]{:S(2)}, u32[]{:S(2)}) collective-permute-start(bf16[32,1024]{1,0:T(8,128)(2,1)S(1)} %get-tuple-element.46), channel_id=1, source_target_pairs={{0,3},{1,0},{2,1},{3,2},{4,7},{5,4},{6,5},{7,6},{8,11},{9,8},{10,9... | collective-permute-start | bytes 196616 | tf_op jit(solution)/shard_map/ppermute | solution.py:39
  124.4 26.2 %collective-permute-start.32 = (bf16[32,1024]{1,0:T(8,128)(2,1)S(1)}, bf16[32,1024]{1,0:T(8,128)(2,1)S(1)}, u32[]{:S(2)}, u32[]{:S(2)}) collective-permute-start(bf16[32,1024]{1,0:T(8,128)(2,1)S(1)} %get-tuple-element.48), channel_id=1, source_target_pairs={{0,2},{1,3},{2,0},{3,1},{4,6},{5,7},{6,4},{7,5},{8,10},{9,11},{10,... | collective-permute-start | bytes 196616 | tf_op jit(solution)/shard_map/ppermute | solution.py:39
  126.5 27.1 %collective-permute-start.33 = (bf16[32,1024]{1,0:T(8,128)(2,1)S(1)}, bf16[32,1024]{1,0:T(8,128)(2,1)S(1)}, u32[]{:S(2)}, u32[]{:S(2)}) collective-permute-start(bf16[32,1024]{1,0:T(8,128)(2,1)S(1)} %get-tuple-element.47), channel_id=1, source_target_pairs={{0,1},{1,2},{2,3},{3,0},{4,5},{5,6},{6,7},{7,4},{8,9},{9,10},{10,1... | collective-permute-start | bytes 196616 | tf_op jit(solution)/shard_map/ppermute | solution.py:39
  126.6 10.9 %collective-permute-start.42 = (bf16[32,4864]{1,0:T(8,128)(2,1)S(1)}, bf16[32,4864]{1,0:T(8,128)(2,1)S(1)}, u32[]{:S(2)}, u32[]{:S(2)}) collective-permute-start(bf16[32,4864]{1,0:T(8,128)(2,1)S(1)} %get-tuple-element.45), channel_id=1, source_target_pairs={{0,96},{16,112},{32,0},{48,16},{64,32},{80,48},{96,64},{112,80},{1... | collective-permute-start | bytes 933896 | tf_op jit(solution)/shard_map/ppermute | solution.py:26
  137.4 11.0 %collective-permute-start.37 = (bf16[32,4864]{1,0:T(8,128)(2,1)S(1)}, bf16[32,4864]{1,0:T(8,128)(2,1)S(1)}, u32[]{:S(2)}, u32[]{:S(2)}) collective-permute-start(bf16[32,4864]{1,0:T(8,128)(2,1)S(1)} %get-tuple-element.44), channel_id=1, source_target_pairs={{0,32},{16,48},{32,64},{48,80},{64,96},{80,112},{96,0},{112,16},{1... | collective-permute-start | bytes 933896 | tf_op jit(solution)/shard_map/ppermute | solution.py:26
  150.2 11.6 %collective-permute-start.41 = (bf16[32,4864]{1,0:T(8,128)(2,1)S(1)}, bf16[32,4864]{1,0:T(8,128)(2,1)S(1)}, u32[]{:S(2)}, u32[]{:S(2)}) collective-permute-start(bf16[32,4864]{1,0:T(8,128)(2,1)S(1)} %slice.281), channel_id=1, source_target_pairs={{0,32},{16,48},{32,64},{48,80},{64,96},{80,112},{96,0},{112,16},{1... | collective-permute-start | bytes 933896 | tf_op jit(solution)/shard_map/ppermute | solution.py:26
  150.6 13.0 %collective-permute-start.43 = (bf16[32,4864]{1,0:T(8,128)(2,1)S(1)}, bf16[32,4864]{1,0:T(8,128)(2,1)S(1)}, u32[]{:S(2)}, u32[]{:S(2)}) collective-permute-start(bf16[32,4864]{1,0:T(8,128)(2,1)S(1)} %add_convert_fusion.4), channel_id=1, source_target_pairs={{0,96},{16,112},{32,0},{48,16},{64,32},{80,48},{96,64},{112,80},{1... | collective-permute-start | bytes 933896 | tf_op jit(solution)/shard_map/ppermute | solution.py:26
  153.5 12.5 %collective-permute-start.38 = (bf16[32,4864]{1,0:T(8,128)(2,1)S(1)}, bf16[32,4864]{1,0:T(8,128)(2,1)S(1)}, u32[]{:S(2)}, u32[]{:S(2)}) collective-permute-start(bf16[32,4864]{1,0:T(8,128)(2,1)S(1)} %add_convert_fusion.6), channel_id=1, source_target_pairs={{0,32},{16,48},{32,64},{48,80},{64,96},{80,112},{96,0},{112,16},{1... | collective-permute-start | bytes 933896 | tf_op jit(solution)/shard_map/ppermute | solution.py:26
  (27 other events, 178.1 us)

commit v2 on v0

v2 whole, which is shorter than its diff:
```python
import functools

import jax
import jax.numpy as jnp
from jax import lax
from jax.experimental import pallas as pl
from jax.experimental.pallas import tpu as pltpu
from jax.sharding import PartitionSpec as P

F32 = jnp.float32
BF16 = jnp.bfloat16
VMEM = pltpu.MemorySpace.VMEM
SMEM = pltpu.MemorySpace.SMEM
HBM = pltpu.MemorySpace.HBM

E = 512
ROWS = 1024
COLS = 4864
HALF = COLS // 2
HALVES = (slice(0, HALF), slice(HALF, COLS))
NX, NY, NZ = 4, 4, 4
GATHER = 2**31


def core_swap(a):
    return lax.ppermute(a, "state", [(i, i ^ 1) for i in range(8)])


def x_shift(a, step):
    return lax.ppermute(a, "state", [(i, (i + 2 * step) % 8) for i in range(8)])


def shift(a, stage, step):
    perm = []
    for i in range(8):
        for j in range(16):
            z, y = divmod(j, NY)
            if (i % 2 + stage) % 2 == 0:
                y = (y + step) % NY
            else:
                z = (z + step) % NZ
            perm.append((i * 16 + j, i * 16 + z * NY + y))
    return lax.ppermute(a, ("state", "vocab"), perm)


def run(kernel, outs, *ins, flops=64, smem=0, hbm=0, wait=(), limit=8, **kw):
    plain = smem + hbm
    vmem = pl.BlockSpec(memory_space=VMEM)
    anywhere = pl.BlockSpec(memory_space=pl.ANY)
    specs = [pl.BlockSpec(memory_space=SMEM)] * smem + [pl.BlockSpec(memory_space=HBM)] * hbm + [vmem] * (len(ins) - plain)
    args = list(ins[:smem]) + [pltpu.with_memory_space_constraint(a, HBM) for a in ins[smem:plain]]
    args += [pltpu.with_memory_space_constraint(a, VMEM) for a in ins[plain:]]

    def wrapped(*refs):
        kernel(*refs[: len(ins)], *refs[len(ins) + len(wait) :])

    return pl.pallas_call(
        wrapped,
        out_shape=tuple((space[0] if space else VMEM)(shape, dtype) for shape, dtype, *space in outs),
        in_specs=specs + [anywhere] * len(wait),
        out_specs=tuple(pl.BlockSpec(memory_space=o[2]) if o[2:] else vmem for o in outs),
        compiler_params=pltpu.CompilerParams(vmem_limit_bytes=limit * 2**20),
        cost_estimate=pl.CostEstimate(flops=flops, bytes_accessed=64, transcendentals=0),
        **kw,
    )(*args, *wait)


def eye():
    rows = lax.broadcasted_iota(jnp.int32, (128, 128), 0)
    return rows == lax.broadcasted_iota(jnp.int32, (128, 128), 1)


def to_lanes(column):
    return jnp.sum(jnp.where(eye(), jnp.broadcast_to(column, (128, 128)), 0.0), axis=0, keepdims=True)


def to_column(lanes):
    return jnp.sum(jnp.where(eye(), jnp.broadcast_to(lanes, (128, 128)), 0.0), axis=1, keepdims=True)


def hold_kernel(*refs):
    for a, out in zip(refs[:2], refs[2:]):
        out[...] = a[...]


def row_offset(slot):
    i, j = lax.axis_index("state"), lax.axis_index("vocab")
    x, c = lax.div(i, 2), lax.rem(i, 2)
    z, y = lax.div(j, NY), lax.rem(j, NY)
    b, a = divmod(slot, 4)
    y = lax.rem(y + 4 - jnp.where(c == 0, a, b), 4)
    z = lax.rem(z + 4 - jnp.where(c == 0, b, a), 4)
    k = z * NY + y
    owner = lax.div(k, 2)
    ahead = lax.rem(lax.div(owner, 2) + 4 - x, 4)
    place = jnp.where(ahead == 0, 0, jnp.where(ahead == 3, 1, jnp.where(ahead == 1, 2, 3)))
    other = jnp.where(lax.rem(owner, 2) == c, 0, 64)
    return pl.multiple_of(128 * place + other + 32 * lax.rem(k, 2), 32)


def assemble_kernel(s0, s1, s2, s3, b1, b2, b3, wide, tall):
    def put(slot, rows):
        wide[pl.ds(row_offset(slot), 32), :] = rows

    for k, part in enumerate((s0, s1, s2, s3)):
        put(k, part[...])
    for g, part in enumerate((b1, b2, b3)):
        for k in range(4):
            put(4 * (g + 1) + k, part[32 * k : 32 * k + 32, :])
    tall[...] = wide[...].T


def gather_kernel(counts, *refs):
    parts, (sums, t_a, t_b, held, sems) = refs[:6], refs[6:]

    def fetch(r):
        rows = pl.ds(128 * r, 128)
        return pltpu.make_async_copy(counts.at[rows, :], held.at[r % 4], sems.at[r % 4])

    for r in range(4):
        fetch(r).start()
    for t, cols in zip((t_a, t_b), HALVES):
        for p, part in enumerate(parts):
            t[64 * p : 64 * p + 64, :] = part[:, cols]
    for r in range(ROWS // 128):
        fetch(r).wait()
        sums[r : r + 1, :] = to_lanes(jnp.sum(held[r % 4].astype(F32), axis=1, keepdims=True))
        if r + 4 < ROWS // 128:
            fetch(r + 4).start()


def join_kernel(low, high, *outs):
    for out, cols in zip(outs, HALVES):
        out[:32, :] = low[:, cols]
        out[32:, :] = high[:, cols]


def far_kernel(*refs):
    (mine_a, theirs_a, mine_b, theirs_b), (low, high) = refs[:4], refs[4:]
    for mine, theirs, cols in ((mine_a, theirs_a, HALVES[0]), (mine_b, theirs_b, HALVES[1])):
        both = (mine[...].astype(F32) + theirs[...].astype(F32)).astype(BF16)
        low[:, cols] = both[:32]
        high[:, cols] = both[32:]


def pair_kernel(mine, theirs_down, theirs_up, low, high, up, down):
    up[:32, :] = (mine[128:160, :].astype(F32) + theirs_up[:32, :].astype(F32) + low[...].astype(F32)).astype(BF16)
    up[32:, :] = (mine[160:, :].astype(F32) + theirs_up[32:, :].astype(F32)).astype(BF16)
    down[:32, :] = (mine[64:96, :].astype(F32) + theirs_down[:32, :].astype(F32)).astype(BF16)
    down[32:, :] = (
        mine[96:128, :].astype(F32) + theirs_down[32:, :].astype(F32) + high[...].astype(F32)
    ).astype(BF16)


def final_kernel(mine, theirs, up, down, out):
    parts = (mine, theirs, up, down)
    out[...] = sum(p[:64, :].astype(F32) for p in parts).astype(BF16)


def softmax_kernel(near, s, mine, theirs, w, stats, tokens, kept, sem, ring=None, sems=None):
    def spill(r):
        return pltpu.make_async_copy(ring.at[r % 4], w.at[pl.ds(128 * r, 128), :], sems.at[r % 4])

    tokens[384:448, :] = mine[...]
    tokens[448:, :] = theirs[...]
    keep = pltpu.make_async_copy(tokens, kept, sem)
    keep.start()
    for r in range(ROWS // 128):
        rows = slice(128 * r, 128 * r + 128)
        logits = jnp.dot(s[rows, :], tokens[...], preferred_element_type=F32)
        top = jnp.max(logits, axis=1, keepdims=True)
        e = jnp.exp(logits - top)
        if ring is None:
            w[rows, :] = e
        else:
            if r >= 4:
                spill(r - 4).wait()
            ring[r % 4] = e
            spill(r).start()
        stats[r : r + 1, :] = to_lanes(top)
        stats[r + 8 : r + 9, :] = to_lanes(jnp.sum(e, axis=1, keepdims=True))
    if ring is not None:
        for r in range(ROWS // 128 - 4, ROWS // 128):
            spill(r).wait()
    keep.wait()


def dlogits_kernel(cols, w, counts, factor, s, dl, mine, theirs):
    for r in range(ROWS // 128):
        rows = slice(128 * r, 128 * r + 128)
        f = to_column(factor[r : r + 1, :])
        dl[rows, :] = (counts[rows, cols].astype(F32) - w[rows, :] * f).astype(BF16)
    out = jnp.dot(s[384:, :], dl[...], preferred_element_type=F32).astype(BF16)
    mine[...] = out[:64]
    theirs[...] = out[64:]


def tok_kernel(s, dl_a, dl_b, mine, *theirs):
    for dl, cols in zip((dl_a, dl_b), HALVES):
        out = jnp.dot(s[:384, :], dl[...], preferred_element_type=F32).astype(BF16)
        for b in range(3):
            rows = slice(64 * b, 64 * b + 64)
            mine[rows, cols] = out[128 * b : 128 * b + 64]
            theirs[b][:, cols] = out[128 * b + 64 : 128 * b + 128]


def state_kernel(t_a, t_b, dl_a, dl_b, out, acc):
    dims = (((1,), (1,)), ((), ()))
    offsets = [row_offset(slot) for slot in range(16)]
    for q in range(4):
        rows = slice(256 * q, 256 * q + 256)
        one = lax.dot_general(t_a[...], dl_a[rows, :], dims, preferred_element_type=F32)
        two = lax.dot_general(t_b[...], dl_b[rows, :], dims, preferred_element_type=F32)
        acc[...] = one + two
        for r in range(16):
            part = acc[pl.ds(offsets[r], 32), :]
            out[32 * r : 32 * r + 32, rows] = part.astype(BF16)


def combine(parts):
    tops = [p[:8] for p in parts]
    top = tops[0]
    for t in tops[1:]:
        top = jnp.maximum(top, t)
    total = sum(p[8:16] * jnp.exp(t - top) for p, t in zip(parts, tops))
    return jnp.concatenate([top, total, sum(p[16:] for p in parts)], axis=0)


def add(*parts):
    return sum(p.astype(F32) for p in parts).astype(BF16)


def body(state_emb, tok_emb, counts):
    own = tok_emb.T

    t2, t4 = x_shift(own, 1), x_shift(own, -1)
    s0 = state_emb.T
    first_parts = [s0] + [shift(s0, 0, k) for k in (1, 2, 3)]
    block = jnp.concatenate(first_parts, axis=0)
    later = [shift(block, 1, k) for k in (1, 2, 3)]
    t1 = core_swap(own)
    t2, t4 = run(hold_kernel, [((64, COLS), BF16)] * 2, t2, t4, wait=(later[0], later[2], t1))

    row_counts, *near = run(
        gather_kernel,
        [((8, 128), F32)] + [((E, HALF), BF16)] * 2,
        counts,
        own,
        t1,
        t2,
        core_swap(t2),
        t4,
        core_swap(t4),
        hbm=1,
        flops=GATHER,
        scratch_shapes=[pltpu.VMEM((4, 128, COLS), BF16), pltpu.SemaphoreType.DMA((4,))],
    )
    wide, tall = run(
        assemble_kernel, [((E, ROWS), BF16), ((ROWS, E), BF16)], *first_parts, *later, wait=(row_counts,)
    )
    mine = run(
        join_kernel,
        [((64, HALF), BF16)] * 2,
        x_shift(t2[:32], 1),
        x_shift(t4[32:], -1),
        wait=(row_counts, wide),
    )
    weights, stats, tokens = [], [], []
    ring = [pltpu.VMEM((4, 128, HALF), F32), pltpu.SemaphoreType.DMA((4,))]
    for t, far in zip(near, mine):
        w, st, _, tk = run(
            softmax_kernel,
            [
                ((ROWS, HALF), F32, HBM) if weights else ((ROWS, HALF), F32),
                ((16, 128), F32),
                ((E, HALF), BF16),
                ((E, HALF), BF16, HBM),
            ],
            t,
            tall,
            far,
            core_swap(far),
            wait=weights,
            flops=2 * ROWS * E * HALF,
            input_output_aliases={0: 2},
            limit=12 if weights else 8,
            scratch_shapes=[pltpu.SemaphoreType.DMA] + (ring if weights else []),
        )
        weights.append(w)
        stats.append(st)
        tokens.append(tk)

    none = jnp.zeros((8, 128), F32)
    total = combine(
        [jnp.concatenate([stats[0], row_counts], axis=0), jnp.concatenate([stats[1], none], axis=0)]
    )
    for stage in range(2):
        total = combine([total] + [shift(total, stage, k) for k in (1, 2, 3)])
    scale = total[16:] / total[8:16]

    dls, sums = [], []
    for w, st, cols in zip(weights, stats, HALVES):
        dl, mine, theirs = run(
            functools.partial(dlogits_kernel, cols),
            [((ROWS, HALF), BF16), ((64, HALF), BF16), ((64, HALF), BF16)],
            w,
            counts,
            jnp.exp(st[:8] - total[:8]) * scale,
            wide,
            wait=dls,
            flops=2 * ROWS * 256 * HALF,
        )
        dls.append(dl)
        sums += [mine, core_swap(theirs)]

    low, high = run(far_kernel, [((32, COLS), BF16)] * 2, *sums)
    from_low, from_high = x_shift(low, 1), x_shift(high, -1)
    mine, *theirs = run(
        tok_kernel,
        [((192, COLS), BF16)] + [((64, COLS), BF16)] * 3,
        wide,
        *dls,
        wait=(low,),
        flops=2 * ROWS * 384 * COLS,
    )
    theirs = [core_swap(t) for t in theirs]
    up, down = run(
        pair_kernel, [((64, COLS), BF16)] * 2, mine, theirs[1], theirs[2], from_low, from_high
    )
    from_up, from_down = x_shift(up, 1), x_shift(down, -1)
    (grad_tok,) = run(final_kernel, [((64, COLS), BF16)], mine, theirs[0], from_up, from_down)

    (g,) = run(
        state_kernel,
        [((E, ROWS), BF16)],
        *tokens,
        *dls,
        wait=(mine,),
        flops=2 * ROWS * E * COLS,
        scratch_shapes=[pltpu.VMEM((E, 256), F32)],
    )
    g = add(g[:128], *[shift(g[128 * k : 128 * k + 128], 1, -k) for k in (1, 2, 3)])
    grad_state = add(g[:32], *[shift(g[32 * k : 32 * k + 32], 0, -k) for k in (1, 2, 3)])
    return grad_state.T, grad_tok.T


def solution(mesh):
    return jax.shard_map(
        body,
        mesh=mesh,
        in_specs=(P("state", "vocab"), P("vocab", "state"), P("state", "vocab")),
        out_specs=(P("state", "vocab"), P("vocab", "state")),
        check_vma=False,
    )
```

time: 331 us -> 113 us (0.34)
  waiting for transfers between devices: 180 us -> 42.4 us
  blocking collectives: 76.7 us -> 0 us
  starting transfers between devices: 0.16 us -> 34.5 us
  Pallas kernels: 0 us -> 30.4 us
  matrix products: 29.4 us -> 0 us
  other arithmetic: 27.6 us -> 1.75 us
  between operations: 13.8 us -> 1 us
    reduce_scatter x2 -> x0, waiting for transfers between devices: 100 us -> none  [the longest x1 58.8 us: body(): lax.psum_scatter(state_part.astype(jnp.bfloat16), 'vocab', scatter_dimens...]
    all_gather x2 -> x0, waiting for transfers between devices: 77.9 us -> none  [the longest x1 41.6 us: body(): states = lax.all_gather(state_emb, 'vocab', axis=1, tiled=True)]
    ppermute x0 -> x36, waiting for transfers between devices: none -> 42.4 us  [the longest x18 37.9 us: shift(): return lax.ppermute(a, ('state', 'vocab'), perm)]
    pmax x1 -> x0, blocking collectives: 40.6 us -> none  [body(): row_top = lax.pmax(local_top, 'vocab')]
    psum x1 -> x0, blocking collectives: 36.1 us -> none  [body(): lax.psum((jnp.sum(weights, axis=1, keepdims=True), local_counts), 'vocab')]
    ppermute x0 -> x36, starting transfers between devices: none -> 34.5 us  [the longest x18 21.5 us: shift(): return lax.ppermute(a, ('state', 'vocab'), perm)]
    pallas_call x0 -> x13, Pallas kernels: none -> 30.4 us  [run(): pl.pallas_call(wrapped, out_shape=tuple(((space[0] if space else VMEM)(sh...]
    dot_general x3 -> x0, matrix products: 29.4 us -> none  [the longest x1 12.2 us: body(): lax.dot_general(states, tokens, (((1,), (1,)), ((), ())), preferred_eleme...]
  transfers between devices with their start and end apart: 4 -> 36, of which waited for: 4 -> 19; matrix products, arithmetic and copies ran while one was open for 5% -> 2% of each run, Pallas kernels for 0% -> 19%
where the time goes in v2:
time: 113 us
  waiting for transfers between devices  42.4 us (38%)
  starting transfers between devices  34.5 us (31%)
  Pallas kernels  30.4 us (27%)
  local copies, waits for them, and re-layouts  2.78 us (2%)
  other arithmetic  1.75 us (2%)
    ppermute x18, waiting for transfers between devices, shift(): return lax.ppermute(a, ('state', 'vocab'), perm)  37.9 us
    pallas_call x13, Pallas kernels, run(): pl.pallas_call(wrapped, out_shape=tuple(((space[0] if space else VMEM)(sh...  30.4 us
    ppermute x18, starting transfers between devices, shift(): return lax.ppermute(a, ('state', 'vocab'), perm)  21.5 us
    ppermute x8, starting transfers between devices, x_shift(): return lax.ppermute(a, 'state', [(i, (i + 2 * step) % 8) for i in range(8)])  11.1 us
    ppermute x10, waiting for transfers between devices, core_swap(): return lax.ppermute(a, 'state', [(i, i ^ 1) for i in range(8)])  2.7 us
    unnamed x21, local copies, waits for them, and re-layouts  2.67 us
  transfers between devices with their start and end apart: 36, of which 19 were waited for; matrix products, arithmetic and copies ran while one was open for 2% of the time, Pallas kernels for 19%

profile of v2, /device:TPU:0, one launch (start us, length us, event | category | flops | bytes accessed | tf_op | source)
XLA Modules:
  0.0 112.8 jit_solution(12830269021281333010)
XLA Ops:
  0.6 2.9 %collective-permute-start.2 = (bf16[64,4864]{1,0:T(8,128)(2,1)}, bf16[64,4864]{1,0:T(8,128)(2,1)S(1)}, u32[]{:S(2)}, u32[]{:S(2)}) collective-permute-start(bf16[64,4864]{1,0:T(8,128)(2,1)} %bitcast.10), channel_id=1, source_target_pairs={{0,96},{16,112},{32,0},{48,16},{64,32},{80,48},{96,64},{112,80},{1... | collective-permute-start | bytes 1867784 | tf_op jit(solution)/shard_map/ppermute | solution.py:30
  3.6 3.0 %collective-permute-start.5 = (bf16[32,1024]{1,0:T(8,128)(2,1)}, bf16[32,1024]{1,0:T(8,128)(2,1)S(1)}, u32[]{:S(2)}, u32[]{:S(2)}) collective-permute-start(bf16[32,1024]{1,0:T(8,128)(2,1)} %bitcast.14), channel_id=1, source_target_pairs={{0,3},{1,0},{2,1},{3,2},{4,7},{5,4},{6,5},{7,6},{8,11},{9,8},{10,9... | collective-permute-start | bytes 196616 | tf_op jit(solution)/shard_map/ppermute | solution.py:43
  9.6 2.9 %collective-permute-done.4.refs_2_ = bf16[32,1024]{1,0:T(8,128)(2,1)S(1)} collective-permute-done((bf16[32,1024]{1,0:T(8,128)(2,1)}, bf16[32,1024]{1,0:T(8,128)(2,1)S(1)}, u32[]{:S(2)}, u32[]{:S(2)}) %collective-permute-start.4) | collective-permute-done | bytes 65568 | tf_op jit(solution)/shard_map/ppermute | solution.py:43
  12.6 2.2 %collective-permute-done.3.refs_1_ = bf16[32,1024]{1,0:T(8,128)(2,1)S(1)} collective-permute-done((bf16[32,1024]{1,0:T(8,128)(2,1)}, bf16[32,1024]{1,0:T(8,128)(2,1)S(1)}, u32[]{:S(2)}, u32[]{:S(2)}) %collective-permute-start.3) | collective-permute-done | bytes 65568 | tf_op jit(solution)/shard_map/ppermute | solution.py:43
  15.6 4.1 %collective-permute-start.7 = (bf16[128,1024]{1,0:T(8,128)(2,1)S(1)}, bf16[128,1024]{1,0:T(8,128)(2,1)S(1)}, u32[]{:S(2)}, u32[]{:S(2)}) collective-permute-start(bf16[128,1024]{1,0:T(8,128)(2,1)S(1)} %pad_maximum_fusion), channel_id=1, source_target_pairs={{0,12},{1,13},{2,14},{3,15},{4,0},{5,1},{6,2},{7,3},{8,4},{9,5},{1... | collective-permute-start | bytes 786440 | tf_op jit(solution)/shard_map/ppermute | solution.py:43
  19.7 3.9 %collective-permute-done.7.refs_3_.refs_6_ = bf16[128,1024]{1,0:T(8,128)(2,1)S(1)} collective-permute-done((bf16[128,1024]{1,0:T(8,128)(2,1)S(1)}, bf16[128,1024]{1,0:T(8,128)(2,1)S(1)}, u32[]{:S(2)}, u32[]{:S(2)}) %collective-permute-start.7) | collective-permute-done | bytes 262176 | tf_op jit(solution)/shard_map/ppermute | solution.py:43
  23.6 3.7 %collective-permute-done.6.refs_2_.refs_4_ = bf16[128,1024]{1,0:T(8,128)(2,1)S(1)} collective-permute-done((bf16[128,1024]{1,0:T(8,128)(2,1)S(1)}, bf16[128,1024]{1,0:T(8,128)(2,1)S(1)}, u32[]{:S(2)}, u32[]{:S(2)}) %collective-permute-start.6) | collective-permute-done | bytes 262176 | tf_op jit(solution)/shard_map/ppermute | solution.py:43
  28.0 3.3 %collective-permute-start.12 = (bf16[32,4864]{1,0:T(8,128)(2,1)S(1)}, bf16[32,4864]{1,0:T(8,128)(2,1)S(1)}, u32[]{:S(2)}, u32[]{:S(2)}) collective-permute-start(bf16[32,4864]{1,0:T(8,128)(2,1)S(1)} %slice.99), channel_id=1, source_target_pairs={{0,96},{16,112},{32,0},{48,16},{64,32},{80,48},{96,64},{112,80},{1... | collective-permute-start | bytes 933896 | tf_op jit(solution)/shard_map/ppermute | solution.py:30
  31.4 4.4 %shard_map.51 = (f32[8,128]{1,0:T(8,128)S(1)}, bf16[512,2432]{1,0:T(8,128)(2,1)S(1)}, bf16[512,2432]{1,0:T(8,128)(2,1)S(1)}) custom-call(bf16[1024,4864]{1,0:T(8,128)(2,1)} %refs_1_.3, bf16[64,4864]{1,0:T(8,128)(2,1)S(1)} %bitcast.13, bf16[64,4864]{1,0:T(8,128)(2,1)S(1)} %collective-permute-done.refs_4_.refs_2_, ...), custom_call_target="tpu_custom_call" | custom-call | flops 2147483648 | bytes 64 | tf_op jit(solution)/shard_map/pallas_call | solution.py:57
  35.8 3.4 %collective-permute-done.10.refs_5_ = bf16[128,1024]{1,0:T(8,128)(2,1)S(1)} collective-permute-done((bf16[128,1024]{1,0:T(8,128)(2,1)S(1)}, bf16[128,1024]{1,0:T(8,128)(2,1)S(1)}, u32[]{:S(2)}, u32[]{:S(2)}) %collective-permute-start.10) | collective-permute-done | bytes 262176 | tf_op jit(solution)/shard_map/ppermute | solution.py:43
  43.4 4.1 %shard_map.54 = (f32[1024,2432]{1,0:T(8,128)S(1)}, f32[16,128]{1,0:T(8,128)S(1)}, bf16[512,2432]{1,0:T(8,128)(2,1)S(1)}, bf16[512,2432]{1,0:T(8,128)(2,1)}) custom-call(bf16[512,2432]{1,0:T(8,128)(2,1)S(1)} %get-tuple-element.33.refs_0_, bf16[1024,512]{1,0:T(8,128)(2,1)S(1)} %get-tuple-element.35.refs_1_, ...), custom_call_target="tpu_custom_call", output_to_operand_aliasing={{2}: (0, {})} | custom-call | flops 2550136832 | bytes 64 | tf_op jit(solution)/shard_map/pallas_call | solution.py:57
  47.5 6.3 %shard_map.55 = (f32[1024,2432]{1,0:T(8,128)}, f32[16,128]{1,0:T(8,128)S(1)}, bf16[512,2432]{1,0:T(8,128)(2,1)S(1)}, bf16[512,2432]{1,0:T(8,128)(2,1)}) custom-call(bf16[512,2432]{1,0:T(8,128)(2,1)S(1)} %get-tuple-element.39.refs_0_, bf16[1024,512]{1,0:T(8,128)(2,1)S(1)} %get-tuple-element.35.refs_1_, ...), custom_call_target="tpu_custom_call", output_to_operand_aliasing={{2}: (0, {})} | custom-call | flops 2550136832 | bytes 64 | tf_op jit(solution)/shard_map/pallas_call | solution.py:57
  53.8 2.1 %collective-permute-start.17 = (f32[24,128]{1,0:T(8,128)S(1)}, f32[24,128]{1,0:T(8,128)S(1)}, u32[]{:S(2)}, u32[]{:S(2)}) collective-permute-start(f32[24,128]{1,0:T(8,128)S(1)} %pad_maximum_fusion.1), channel_id=1, source_target_pairs={{0,3},{1,0},{2,1},{3,2},{4,7},{5,4},{6,5},{7,6},{8,11},{9,8},{10,9... | collective-permute-start | bytes 36872 | tf_op jit(solution)/shard_map/ppermute | solution.py:43
  57.6 3.5 %collective-permute-done.16 = f32[24,128]{1,0:T(8,128)S(1)} collective-permute-done((f32[24,128]{1,0:T(8,128)S(1)}, f32[24,128]{1,0:T(8,128)S(1)}, u32[]{:S(2)}, u32[]{:S(2)}) %collective-permute-start.16) | collective-permute-done | bytes 12320 | tf_op jit(solution)/shard_map/ppermute | solution.py:43
  71.5 2.0 %shard_map.57 = (bf16[1024,2432]{1,0:T(8,128)(2,1)S(1)}, bf16[64,2432]{1,0:T(8,128)(2,1)S(1)}, bf16[64,2432]{1,0:T(8,128)(2,1)S(1)}) custom-call(f32[1024,2432]{1,0:T(8,128)S(1)} %bitcast.9, bf16[1024,4864]{1,0:T(8,128)(2,1)S(1)} %bitcast.7, f32[8,128]{1,0:T(8,128)S(1)} %get-tuple-element.60.refs_2_, ...), custom_call_target="tpu_custom_call" | custom-call | flops 1275068416 | bytes 64 | tf_op jit(solution)/shard_map/pallas_call | solution.py:57
  77.5 4.3 %shard_map.59 = (bf16[192,4864]{1,0:T(8,128)(2,1)S(1)}, bf16[64,4864]{1,0:T(8,128)(2,1)S(1)}, bf16[64,4864]{1,0:T(8,128)(2,1)S(1)}, bf16[64,4864]{1,0:T(8,128)(2,1)S(1)}) custom-call(bf16[512,1024]{1,0:T(8,128)(2,1)S(1)} %get-tuple-element.36.refs_3_.refs_0_, bf16[1024,2432]{1,0:T(8,128)(2,1)S(1)} %get-tuple-element.45.refs_4_.refs_1_.refs_2_, ...), custom_call_target="tpu_custom_call" | custom-call | flops 3825205248 | bytes 64 | tf_op jit(solution)/shard_map/pallas_call | solution.py:57
  82.3 5.8 %shard_map.60 = bf16[512,1024]{1,0:T(8,128)(2,1)S(1)} custom-call(bf16[512,2432]{1,0:T(8,128)(2,1)S(1)} %copy-done.3, bf16[512,2432]{1,0:T(8,128)(2,1)S(1)} %copy-done.2, bf16[1024,2432]{1,0:T(8,128)(2,1)S(1)} %get-tuple-element.45.refs_4_.refs_1_.refs_2_, bf16[1024,2432]{1,0:T(8,128)(2,1)S(1)} %get-tuple-element.47.refs_2_.refs_3_, ...), custom_call_target="tpu_custom_call" | custom-call | flops 5100273664 | bytes 64 | tf_op jit(solution)/shard_map/pallas_call | solution.py:57
  88.2 2.1 %collective-permute-start.23 = (bf16[128,1024]{1,0:T(8,128)(2,1)S(1)}, bf16[128,1024]{1,0:T(8,128)(2,1)S(1)}, u32[]{:S(2)}, u32[]{:S(2)}) collective-permute-start(bf16[128,1024]{1,0:T(8,128)(2,1)S(1)} %get-tuple-element.67), channel_id=1, source_target_pairs={{0,12},{1,13},{2,14},{3,15},{4,0},{5,1},{6,2},{7,3},{8,4},{9,5},{1... | collective-permute-start | bytes 786440 | tf_op jit(solution)/shard_map/ppermute | solution.py:43
  92.3 2.3 %collective-permute-done.23 = bf16[128,1024]{1,0:T(8,128)(2,1)S(1)} collective-permute-done((bf16[128,1024]{1,0:T(8,128)(2,1)S(1)}, bf16[128,1024]{1,0:T(8,128)(2,1)S(1)}, u32[]{:S(2)}, u32[]{:S(2)}) %collective-permute-start.23) | collective-permute-done | bytes 262176 | tf_op jit(solution)/shard_map/ppermute | solution.py:43
  94.7 2.7 %collective-permute-start.35 = (bf16[64,4864]{1,0:T(8,128)(2,1)S(1)}, bf16[64,4864]{1,0:T(8,128)(2,1)S(1)}, u32[]{:S(2)}, u32[]{:S(2)}) collective-permute-start(bf16[64,4864]{1,0:T(8,128)(2,1)S(1)} %get-tuple-element.59), channel_id=1, source_target_pairs={{0,96},{16,112},{32,0},{48,16},{64,32},{80,48},{96,64},{112,80},{1... | collective-permute-start | bytes 1867784 | tf_op jit(solution)/shard_map/ppermute | solution.py:30
  97.4 3.3 %collective-permute-done.25 = bf16[128,1024]{1,0:T(8,128)(2,1)S(1)} collective-permute-done((bf16[128,1024]{1,0:T(8,128)(2,1)S(1)}, bf16[128,1024]{1,0:T(8,128)(2,1)S(1)}, u32[]{:S(2)}, u32[]{:S(2)}) %collective-permute-start.25) | collective-permute-done | bytes 262176 | tf_op jit(solution)/shard_map/ppermute | solution.py:43
  103.0 2.2 %collective-permute-done.26 = bf16[32,1024]{1,0:T(8,128)(2,1)S(1)} collective-permute-done((bf16[32,1024]{1,0:T(8,128)(2,1)S(1)}, bf16[32,1024]{1,0:T(8,128)(2,1)S(1)}, u32[]{:S(2)}, u32[]{:S(2)}) %collective-permute-start.26) | collective-permute-done | bytes 65568 | tf_op jit(solution)/shard_map/ppermute | solution.py:43
  105.2 2.0 %collective-permute-start.27 = (bf16[32,1024]{1,0:T(8,128)(2,1)S(1)}, bf16[32,1024]{1,0:T(8,128)(2,1)S(1)}, u32[]{:S(2)}, u32[]{:S(2)}) collective-permute-start(bf16[32,1024]{1,0:T(8,128)(2,1)S(1)} %get-tuple-element.72), channel_id=1, source_target_pairs={{0,2},{1,3},{2,0},{3,1},{4,6},{5,7},{6,4},{7,5},{8,10},{9,11},{10,... | collective-permute-start | bytes 196616 | tf_op jit(solution)/shard_map/ppermute | solution.py:43
  107.6 3.4 %collective-permute-done.27 = bf16[32,1024]{1,0:T(8,128)(2,1)S(1)} collective-permute-done((bf16[32,1024]{1,0:T(8,128)(2,1)S(1)}, bf16[32,1024]{1,0:T(8,128)(2,1)S(1)}, u32[]{:S(2)}, u32[]{:S(2)}) %collective-permute-start.27) | collective-permute-done | bytes 65568 | tf_op jit(solution)/shard_map/ppermute | solution.py:43
  (97 shorter events, 31.8 us)
Async XLA Ops:
  0.6 26.6 %collective-permute-start.2 = (bf16[64,4864]{1,0:T(8,128)(2,1)}, bf16[64,4864]{1,0:T(8,128)(2,1)S(1)}, u32[]{:S(2)}, u32[]{:S(2)}) collective-permute-start(bf16[64,4864]{1,0:T(8,128)(2,1)} %bitcast.10), channel_id=1, source_target_pairs={{0,96},{16,112},{32,0},{48,16},{64,32},{80,48},{96,64},{112,80},{1... | collective-permute-start | bytes 1867784 | tf_op jit(solution)/shard_map/ppermute | solution.py:30
  3.5 23.7 %collective-permute-start.1 = (bf16[64,4864]{1,0:T(8,128)(2,1)}, bf16[64,4864]{1,0:T(8,128)(2,1)S(1)}, u32[]{:S(2)}, u32[]{:S(2)}) collective-permute-start(bf16[64,4864]{1,0:T(8,128)(2,1)} %bitcast.11), channel_id=1, source_target_pairs={{0,32},{16,48},{32,64},{48,80},{64,96},{80,112},{96,0},{112,16},{1... | collective-permute-start | bytes 1867784 | tf_op jit(solution)/shard_map/ppermute | solution.py:30
  3.6 23.7 %collective-permute-start = (bf16[64,4864]{1,0:T(8,128)(2,1)}, bf16[64,4864]{1,0:T(8,128)(2,1)S(1)}, u32[]{:S(2)}, u32[]{:S(2)}) collective-permute-start(bf16[64,4864]{1,0:T(8,128)(2,1)} %bitcast.12), channel_id=1, source_target_pairs={{0,16},{16,0},{32,48},{48,32},{64,80},{80,64},{96,112},{112,96},{1... | collective-permute-start | bytes 1867784 | tf_op jit(solution)/shard_map/ppermute | solution.py:26
  6.6 6.0 %collective-permute-start.4 = (bf16[32,1024]{1,0:T(8,128)(2,1)}, bf16[32,1024]{1,0:T(8,128)(2,1)S(1)}, u32[]{:S(2)}, u32[]{:S(2)}) collective-permute-start(bf16[32,1024]{1,0:T(8,128)(2,1)} %bitcast.15), channel_id=1, source_target_pairs={{0,2},{1,3},{2,0},{3,1},{4,6},{5,7},{6,4},{7,5},{8,10},{9,11},{10,... | collective-permute-start | bytes 196616 | tf_op jit(solution)/shard_map/ppermute | solution.py:43
  8.8 5.9 %collective-permute-start.3 = (bf16[32,1024]{1,0:T(8,128)(2,1)}, bf16[32,1024]{1,0:T(8,128)(2,1)S(1)}, u32[]{:S(2)}, u32[]{:S(2)}) collective-permute-start(bf16[32,1024]{1,0:T(8,128)(2,1)} %bitcast.16), channel_id=1, source_target_pairs={{0,1},{1,2},{2,3},{3,0},{4,5},{5,6},{6,7},{7,4},{8,9},{9,10},{10,1... | collective-permute-start | bytes 196616 | tf_op jit(solution)/shard_map/ppermute | solution.py:43
  15.6 8.0 %collective-permute-start.7 = (bf16[128,1024]{1,0:T(8,128)(2,1)S(1)}, bf16[128,1024]{1,0:T(8,128)(2,1)S(1)}, u32[]{:S(2)}, u32[]{:S(2)}) collective-permute-start(bf16[128,1024]{1,0:T(8,128)(2,1)S(1)} %pad_maximum_fusion), channel_id=1, source_target_pairs={{0,12},{1,13},{2,14},{3,15},{4,0},{5,1},{6,2},{7,3},{8,4},{9,5},{1... | collective-permute-start | bytes 786440 | tf_op jit(solution)/shard_map/ppermute | solution.py:43
  19.7 7.6 %collective-permute-start.6 = (bf16[128,1024]{1,0:T(8,128)(2,1)S(1)}, bf16[128,1024]{1,0:T(8,128)(2,1)S(1)}, u32[]{:S(2)}, u32[]{:S(2)}) collective-permute-start(bf16[128,1024]{1,0:T(8,128)(2,1)S(1)} %pad_maximum_fusion), channel_id=1, source_target_pairs={{0,4},{1,5},{2,6},{3,7},{4,8},{5,9},{6,10},{7,11},{8,12},{9,13},{1... | collective-permute-start | bytes 786440 | tf_op jit(solution)/shard_map/ppermute | solution.py:43
  28.0 11.8 %collective-permute-start.12 = (bf16[32,4864]{1,0:T(8,128)(2,1)S(1)}, bf16[32,4864]{1,0:T(8,128)(2,1)S(1)}, u32[]{:S(2)}, u32[]{:S(2)}) collective-permute-start(bf16[32,4864]{1,0:T(8,128)(2,1)S(1)} %slice.99), channel_id=1, source_target_pairs={{0,96},{16,112},{32,0},{48,16},{64,32},{80,48},{96,64},{112,80},{1... | collective-permute-start | bytes 933896 | tf_op jit(solution)/shard_map/ppermute | solution.py:30
  31.3 10.3 %collective-permute-start.11 = (bf16[32,4864]{1,0:T(8,128)(2,1)S(1)}, bf16[32,4864]{1,0:T(8,128)(2,1)S(1)}, u32[]{:S(2)}, u32[]{:S(2)}) collective-permute-start(bf16[32,4864]{1,0:T(8,128)(2,1)S(1)} %slice.98), channel_id=1, source_target_pairs={{0,32},{16,48},{32,64},{48,80},{64,96},{80,112},{96,0},{112,16},{1... | collective-permute-start | bytes 933896 | tf_op jit(solution)/shard_map/ppermute | solution.py:30
  31.3 7.9 %collective-permute-start.10 = (bf16[128,1024]{1,0:T(8,128)(2,1)S(1)}, bf16[128,1024]{1,0:T(8,128)(2,1)S(1)}, u32[]{:S(2)}, u32[]{:S(2)}) collective-permute-start(bf16[128,1024]{1,0:T(8,128)(2,1)S(1)} %pad_maximum_fusion), channel_id=1, source_target_pairs={{0,8},{1,9},{2,10},{3,11},{4,12},{5,13},{6,14},{7,15},{8,0},{9,1},... | collective-permute-start | bytes 786440 | tf_op jit(solution)/shard_map/ppermute | solution.py:43
  41.8 5.7 %collective-permute-start.14 = (bf16[64,2432]{1,0:T(8,128)(2,1)S(1)}, bf16[64,2432]{1,0:T(8,128)(2,1)S(1)}, u32[]{:S(2)}, u32[]{:S(2)}) collective-permute-start(bf16[64,2432]{1,0:T(8,128)(2,1)S(1)} %get-tuple-element.40.refs_2_), channel_id=1, source_target_pairs={{0,16},{16,0},{32,48},{48,32},{64,80},{80,64},{96,112},{112,96},{1... | collective-permute-start | bytes 933896 | tf_op jit(solution)/shard_map/ppermute | solution.py:26
  62.1 5.5 %collective-permute-start.18 = (f32[24,128]{1,0:T(8,128)S(1)}, f32[24,128]{1,0:T(8,128)S(1)}, u32[]{:S(2)}, u32[]{:S(2)}) collective-permute-start(f32[24,128]{1,0:T(8,128)S(1)} %pad_maximum_fusion.2), channel_id=1, source_target_pairs={{0,4},{1,5},{2,6},{3,7},{4,8},{5,9},{6,10},{7,11},{8,12},{9,13},{1... | collective-permute-start | bytes 36872 | tf_op jit(solution)/shard_map/ppermute | solution.py:43
  75.4 14.9 %collective-permute-start.33 = (bf16[32,4864]{1,0:T(8,128)(2,1)S(1)}, bf16[32,4864]{1,0:T(8,128)(2,1)S(1)}, u32[]{:S(2)}, u32[]{:S(2)}) collective-permute-start(bf16[32,4864]{1,0:T(8,128)(2,1)S(1)} %get-tuple-element.57), channel_id=1, source_target_pairs={{0,96},{16,112},{32,0},{48,16},{64,32},{80,48},{96,64},{112,80},{1... | collective-permute-start | bytes 933896 | tf_op jit(solution)/shard_map/ppermute | solution.py:30
  76.9 13.4 %collective-permute-start.32 = (bf16[32,4864]{1,0:T(8,128)(2,1)S(1)}, bf16[32,4864]{1,0:T(8,128)(2,1)S(1)}, u32[]{:S(2)}, u32[]{:S(2)}) collective-permute-start(bf16[32,4864]{1,0:T(8,128)(2,1)S(1)} %get-tuple-element.52.refs_3_), channel_id=1, source_target_pairs={{0,32},{16,48},{32,64},{48,80},{64,96},{80,112},{96,0},{112,16},{1... | collective-permute-start | bytes 933896 | tf_op jit(solution)/shard_map/ppermute | solution.py:30
  81.7 10.1 %collective-permute-start.30 = (bf16[64,4864]{1,0:T(8,128)(2,1)S(1)}, bf16[64,4864]{1,0:T(8,128)(2,1)S(1)}, u32[]{:S(2)}, u32[]{:S(2)}) collective-permute-start(bf16[64,4864]{1,0:T(8,128)(2,1)S(1)} %get-tuple-element.55), channel_id=1, source_target_pairs={{0,16},{16,0},{32,48},{48,32},{64,80},{80,64},{96,112},{112,96},{1... | collective-permute-start | bytes 1867784 | tf_op jit(solution)/shard_map/ppermute | solution.py:26
  81.8 10.0 %collective-permute-start.31 = (bf16[64,4864]{1,0:T(8,128)(2,1)S(1)}, bf16[64,4864]{1,0:T(8,128)(2,1)S(1)}, u32[]{:S(2)}, u32[]{:S(2)}) collective-permute-start(bf16[64,4864]{1,0:T(8,128)(2,1)S(1)} %get-tuple-element.56), channel_id=1, source_target_pairs={{0,16},{16,0},{32,48},{48,32},{64,80},{80,64},{96,112},{112,96},{1... | collective-permute-start | bytes 1867784 | tf_op jit(solution)/shard_map/ppermute | solution.py:26
  88.2 6.4 %collective-permute-start.23 = (bf16[128,1024]{1,0:T(8,128)(2,1)S(1)}, bf16[128,1024]{1,0:T(8,128)(2,1)S(1)}, u32[]{:S(2)}, u32[]{:S(2)}) collective-permute-start(bf16[128,1024]{1,0:T(8,128)(2,1)S(1)} %get-tuple-element.67), channel_id=1, source_target_pairs={{0,12},{1,13},{2,14},{3,15},{4,0},{5,1},{6,2},{7,3},{8,4},{9,5},{1... | collective-permute-start | bytes 786440 | tf_op jit(solution)/shard_map/ppermute | solution.py:43
  90.3 10.4 %collective-permute-start.25 = (bf16[128,1024]{1,0:T(8,128)(2,1)S(1)}, bf16[128,1024]{1,0:T(8,128)(2,1)S(1)}, u32[]{:S(2)}, u32[]{:S(2)}) collective-permute-start(bf16[128,1024]{1,0:T(8,128)(2,1)S(1)} %get-tuple-element.68), channel_id=1, source_target_pairs={{0,4},{1,5},{2,6},{3,7},{4,8},{5,9},{6,10},{7,11},{8,12},{9,13},{1... | collective-permute-start | bytes 786440 | tf_op jit(solution)/shard_map/ppermute | solution.py:43
  90.3 10.4 %collective-permute-start.24 = (bf16[128,1024]{1,0:T(8,128)(2,1)S(1)}, bf16[128,1024]{1,0:T(8,128)(2,1)S(1)}, u32[]{:S(2)}, u32[]{:S(2)}) collective-permute-start(bf16[128,1024]{1,0:T(8,128)(2,1)S(1)} %get-tuple-element.69), channel_id=1, source_target_pairs={{0,8},{1,9},{2,10},{3,11},{4,12},{5,13},{6,14},{7,15},{8,0},{9,1},... | collective-permute-start | bytes 786440 | tf_op jit(solution)/shard_map/ppermute | solution.py:43
  91.9 19.8 %collective-permute-start.29 = (bf16[64,4864]{1,0:T(8,128)(2,1)S(1)}, bf16[64,4864]{1,0:T(8,128)(2,1)S(1)}, u32[]{:S(2)}, u32[]{:S(2)}) collective-permute-start(bf16[64,4864]{1,0:T(8,128)(2,1)S(1)} %get-tuple-element.54), channel_id=1, source_target_pairs={{0,16},{16,0},{32,48},{48,32},{64,80},{80,64},{96,112},{112,96},{1... | collective-permute-start | bytes 1867784 | tf_op jit(solution)/shard_map/ppermute | solution.py:26
  92.3 19.4 %collective-permute-start.34 = (bf16[64,4864]{1,0:T(8,128)(2,1)S(1)}, bf16[64,4864]{1,0:T(8,128)(2,1)S(1)}, u32[]{:S(2)}, u32[]{:S(2)}) collective-permute-start(bf16[64,4864]{1,0:T(8,128)(2,1)S(1)} %get-tuple-element.58), channel_id=1, source_target_pairs={{0,32},{16,48},{32,64},{48,80},{64,96},{80,112},{96,0},{112,16},{1... | collective-permute-start | bytes 1867784 | tf_op jit(solution)/shard_map/ppermute | solution.py:30
  94.7 17.0 %collective-permute-start.35 = (bf16[64,4864]{1,0:T(8,128)(2,1)S(1)}, bf16[64,4864]{1,0:T(8,128)(2,1)S(1)}, u32[]{:S(2)}, u32[]{:S(2)}) collective-permute-start(bf16[64,4864]{1,0:T(8,128)(2,1)S(1)} %get-tuple-element.59), channel_id=1, source_target_pairs={{0,96},{16,112},{32,0},{48,16},{64,32},{80,48},{96,64},{112,80},{1... | collective-permute-start | bytes 1867784 | tf_op jit(solution)/shard_map/ppermute | solution.py:30
  102.1 5.5 %collective-permute-start.28 = (bf16[32,1024]{1,0:T(8,128)(2,1)S(1)}, bf16[32,1024]{1,0:T(8,128)(2,1)S(1)}, u32[]{:S(2)}, u32[]{:S(2)}) collective-permute-start(bf16[32,1024]{1,0:T(8,128)(2,1)S(1)} %get-tuple-element.71), channel_id=1, source_target_pairs={{0,1},{1,2},{2,3},{3,0},{4,5},{5,6},{6,7},{7,4},{8,9},{9,10},{10,1... | collective-permute-start | bytes 196616 | tf_op jit(solution)/shard_map/ppermute | solution.py:43
  105.2 5.8 %collective-permute-start.27 = (bf16[32,1024]{1,0:T(8,128)(2,1)S(1)}, bf16[32,1024]{1,0:T(8,128)(2,1)S(1)}, u32[]{:S(2)}, u32[]{:S(2)}) collective-permute-start(bf16[32,1024]{1,0:T(8,128)(2,1)S(1)} %get-tuple-element.72), channel_id=1, source_target_pairs={{0,2},{1,3},{2,0},{3,1},{4,6},{5,7},{6,4},{7,5},{8,10},{9,11},{10,... | collective-permute-start | bytes 196616 | tf_op jit(solution)/shard_map/ppermute | solution.py:43
  (22 other events, 177.1 us)

commit v3 on v2

--- a/solution.py
+++ b/solution.py
@@ -152,44 +152,48 @@
     ).astype(BF16)
 
 
-def final_kernel(mine, theirs, up, down, out):
-    parts = (mine, theirs, up, down)
-    out[...] = sum(p[:64, :].astype(F32) for p in parts).astype(BF16)
-
-
-def softmax_kernel(near, s, mine, theirs, w, stats, tokens, kept, sem, ring=None, sems=None):
-    def spill(r):
-        return pltpu.make_async_copy(ring.at[r % 4], w.at[pl.ds(128 * r, 128), :], sems.at[r % 4])
-
+def final_kernel(mine, theirs, up, down, out, held, sems):
+    copies = []
+    for n, rows in enumerate((slice(0, 32), slice(32, 64))):
+        held[rows, :] = sum(p[rows, :].astype(F32) for p in (mine, theirs, up, down)).astype(BF16)
+        copies.append(pltpu.make_async_copy(held.at[rows, :], out.at[rows, :], sems.at[n]))
+        copies[n].start()
+    for copy in copies:
+        copy.wait()
+
+
+def softmax_kernel(spilled, near, s, mine, theirs, w_top, w_low, stats, tokens, kept, sem, *spill):
     tokens[384:448, :] = mine[...]
     tokens[448:, :] = theirs[...]
     keep = pltpu.make_async_copy(tokens, kept, sem)
     keep.start()
+    copies = []
     for r in range(ROWS // 128):
         rows = slice(128 * r, 128 * r + 128)
         logits = jnp.dot(s[rows, :], tokens[...], preferred_element_type=F32)
         top = jnp.max(logits, axis=1, keepdims=True)
         e = jnp.exp(logits - top)
-        if ring is None:
-            w[rows, :] = e
+        if r >= 4:
+            w_low[128 * r - 512 : 128 * r - 384, :] = e
+        elif spilled:
+            held, sems = spill
+            held[rows, :] = e
+            copies.append(pltpu.make_async_copy(held.at[rows, :], w_top.at[rows, :], sems.at[r]))
+            copies[r].start()
         else:
-            if r >= 4:
-                spill(r - 4).wait()
-            ring[r % 4] = e
-            spill(r).start()
+            w_top[rows, :] = e
         stats[r : r + 1, :] = to_lanes(top)
         stats[r + 8 : r + 9, :] = to_lanes(jnp.sum(e, axis=1, keepdims=True))
-    if ring is not None:
-        for r in range(ROWS // 128 - 4, ROWS // 128):
-            spill(r).wait()
-    keep.wait()
-
-
-def dlogits_kernel(cols, w, counts, factor, s, dl, mine, theirs):
+    for copy in copies + [keep]:
+        copy.wait()
+
+
+def dlogits_kernel(cols, w_top, w_low, counts, factor, s, dl, mine, theirs):
     for r in range(ROWS // 128):
         rows = slice(128 * r, 128 * r + 128)
         f = to_column(factor[r : r + 1, :])
-        dl[rows, :] = (counts[rows, cols].astype(F32) - w[rows, :] * f).astype(BF16)
+        w = w_top[rows, :] if r < 4 else w_low[128 * r - 512 : 128 * r - 384, :]
+        dl[rows, :] = (counts[rows, cols].astype(F32) - w * f).astype(BF16)
     out = jnp.dot(s[384:, :], dl[...], preferred_element_type=F32).astype(BF16)
     mine[...] = out[:64]
     theirs[...] = out[64:]
@@ -266,12 +270,13 @@
         wait=(row_counts, wide),
     )
     weights, stats, tokens = [], [], []
-    ring = [pltpu.VMEM((4, 128, HALF), F32), pltpu.SemaphoreType.DMA((4,))]
-    for t, far in zip(near, mine):
-        w, st, _, tk = run(
-            softmax_kernel,
+    for spilled, (t, far) in enumerate(zip(near, mine)):
+        spill = [pltpu.VMEM((ROWS // 2, HALF), F32), pltpu.SemaphoreType.DMA((4,))]
+        top, low, st, _, tk = run(
+            functools.partial(softmax_kernel, spilled),
             [
-                ((ROWS, HALF), F32, HBM) if weights else ((ROWS, HALF), F32),
+                ((ROWS // 2, HALF), F32, HBM) if spilled else ((ROWS // 2, HALF), F32),
+                ((ROWS // 2, HALF), F32),
                 ((16, 128), F32),
                 ((E, HALF), BF16),
                 ((E, HALF), BF16, HBM),
@@ -280,13 +285,13 @@
             tall,
             far,
             core_swap(far),
-            wait=weights,
+            wait=weights[0] if spilled else (),
             flops=2 * ROWS * E * HALF,
-            input_output_aliases={0: 2},
-            limit=12 if weights else 8,
-            scratch_shapes=[pltpu.SemaphoreType.DMA] + (ring if weights else []),
+            input_output_aliases={0: 3},
+            limit=12 if spilled else 8,
+            scratch_shapes=[pltpu.SemaphoreType.DMA] + (spill if spilled else []),
         )
-        weights.append(w)
+        weights.append((top, low))
         stats.append(st)
         tokens.append(tk)
 
@@ -303,7 +308,7 @@
         dl, mine, theirs = run(
             functools.partial(dlogits_kernel, cols),
             [((ROWS, HALF), BF16), ((64, HALF), BF16), ((64, HALF), BF16)],
-            w,
+            *w,
             counts,
             jnp.exp(st[:8] - total[:8]) * scale,
             wide,
@@ -325,10 +330,25 @@
     )
     theirs = [core_swap(t) for t in theirs]
     up, down = run(
-        pair_kernel, [((64, COLS), BF16)] * 2, mine, theirs[1], theirs[2], from_low, from_high
+        pair_kernel,
+        [((64, COLS), BF16)] * 2,
+        mine,
+        theirs[1],
+        theirs[2],
+        from_low,
+        from_high,
+        wait=(theirs[0],),
     )
     from_up, from_down = x_shift(up, 1), x_shift(down, -1)
-    (grad_tok,) = run(final_kernel, [((64, COLS), BF16)], mine, theirs[0], from_up, from_down)
+    (grad_tok,) = run(
+        final_kernel,
+        [((64, COLS), BF16, HBM)],
+        mine,
+        theirs[0],
+        from_up,
+        from_down,
+        scratch_shapes=[pltpu.VMEM((64, COLS), BF16), pltpu.SemaphoreType.DMA((2,))],
+    )
 
     (g,) = run(
         state_kernel,

time: 113 us -> 108 us (0.956)
  waiting for transfers between devices: 42.4 us -> 38.3 us
  local copies, waits for them, and re-layouts: 2.78 us -> 1.22 us
  starting transfers between devices: 34.5 us -> 35.8 us
    ppermute x18, waiting for transfers between devices: 37.9 us -> 34.1 us  [shift(): return lax.ppermute(a, ('state', 'vocab'), perm)]
    unnamed x21 -> x18, local copies, waits for them, and re-layouts: 2.67 us -> 1.11 us
  transfers between devices with their start and end apart: 36 -> 36, of which waited for: 19 -> 19; matrix products, arithmetic and copies ran while one was open for 2% -> 2% of each run, Pallas kernels for 19% -> 20%
where the time goes in v3:
time: 108 us
  waiting for transfers between devices  38.3 us (35%)
  starting transfers between devices  35.8 us (33%)
  Pallas kernels  29.7 us (28%)
  other arithmetic  1.75 us (2%)
  local copies, waits for them, and re-layouts  1.22 us (1%)
  between operations  1.16 us (1%)
    ppermute x18, waiting for transfers between devices, shift(): return lax.ppermute(a, ('state', 'vocab'), perm)  34.1 us
    pallas_call x13, Pallas kernels, run(): pl.pallas_call(wrapped, out_shape=tuple(((space[0] if space else VMEM)(sh...  29.7 us
    ppermute x18, starting transfers between devices, shift(): return lax.ppermute(a, ('state', 'vocab'), perm)  21.5 us
    ppermute x8, starting transfers between devices, x_shift(): return lax.ppermute(a, 'state', [(i, (i + 2 * step) % 8) for i in range(8)])  11.6 us
    ppermute x10, starting transfers between devices, core_swap(): return lax.ppermute(a, 'state', [(i, i ^ 1) for i in range(8)])  2.7 us
    ppermute x10, waiting for transfers between devices, core_swap(): return lax.ppermute(a, 'state', [(i, i ^ 1) for i in range(8)])  2.34 us
  transfers between devices with their start and end apart: 36, of which 19 were waited for; matrix products, arithmetic and copies ran while one was open for 2% of the time, Pallas kernels for 20%

profile of v3, /device:TPU:0, one launch (start us, length us, event | category | flops | bytes accessed | tf_op | source)
XLA Modules:
  0.0 108.0 jit_solution(3348518792245344881)
XLA Ops:
  0.6 2.9 %collective-permute-start.2 = (bf16[64,4864]{1,0:T(8,128)(2,1)}, bf16[64,4864]{1,0:T(8,128)(2,1)S(1)}, u32[]{:S(2)}, u32[]{:S(2)}) collective-permute-start(bf16[64,4864]{1,0:T(8,128)(2,1)} %bitcast.9), channel_id=1, source_target_pairs={{0,96},{16,112},{32,0},{48,16},{64,32},{80,48},{96,64},{112,80},{1... | collective-permute-start | bytes 1867784 | tf_op jit(solution)/shard_map/ppermute | solution.py:30
  3.5 3.0 %collective-permute-start.5 = (bf16[32,1024]{1,0:T(8,128)(2,1)}, bf16[32,1024]{1,0:T(8,128)(2,1)S(1)}, u32[]{:S(2)}, u32[]{:S(2)}) collective-permute-start(bf16[32,1024]{1,0:T(8,128)(2,1)} %bitcast.13), channel_id=1, source_target_pairs={{0,3},{1,0},{2,1},{3,2},{4,7},{5,4},{6,5},{7,6},{8,11},{9,8},{10,9... | collective-permute-start | bytes 196616 | tf_op jit(solution)/shard_map/ppermute | solution.py:43
  9.6 2.9 %collective-permute-done.4.refs_2_ = bf16[32,1024]{1,0:T(8,128)(2,1)S(1)} collective-permute-done((bf16[32,1024]{1,0:T(8,128)(2,1)}, bf16[32,1024]{1,0:T(8,128)(2,1)S(1)}, u32[]{:S(2)}, u32[]{:S(2)}) %collective-permute-start.4) | collective-permute-done | bytes 65568 | tf_op jit(solution)/shard_map/ppermute | solution.py:43
  12.5 2.2 %collective-permute-done.3.refs_1_ = bf16[32,1024]{1,0:T(8,128)(2,1)S(1)} collective-permute-done((bf16[32,1024]{1,0:T(8,128)(2,1)}, bf16[32,1024]{1,0:T(8,128)(2,1)S(1)}, u32[]{:S(2)}, u32[]{:S(2)}) %collective-permute-start.3) | collective-permute-done | bytes 65568 | tf_op jit(solution)/shard_map/ppermute | solution.py:43
  15.6 4.1 %collective-permute-start.7 = (bf16[128,1024]{1,0:T(8,128)(2,1)S(1)}, bf16[128,1024]{1,0:T(8,128)(2,1)S(1)}, u32[]{:S(2)}, u32[]{:S(2)}) collective-permute-start(bf16[128,1024]{1,0:T(8,128)(2,1)S(1)} %pad_maximum_fusion), channel_id=1, source_target_pairs={{0,12},{1,13},{2,14},{3,15},{4,0},{5,1},{6,2},{7,3},{8,4},{9,5},{1... | collective-permute-start | bytes 786440 | tf_op jit(solution)/shard_map/ppermute | solution.py:43
  19.7 3.9 %collective-permute-done.7.refs_3_.refs_6_ = bf16[128,1024]{1,0:T(8,128)(2,1)S(1)} collective-permute-done((bf16[128,1024]{1,0:T(8,128)(2,1)S(1)}, bf16[128,1024]{1,0:T(8,128)(2,1)S(1)}, u32[]{:S(2)}, u32[]{:S(2)}) %collective-permute-start.7) | collective-permute-done | bytes 262176 | tf_op jit(solution)/shard_map/ppermute | solution.py:43
  23.6 3.7 %collective-permute-done.6.refs_2_.refs_4_ = bf16[128,1024]{1,0:T(8,128)(2,1)S(1)} collective-permute-done((bf16[128,1024]{1,0:T(8,128)(2,1)S(1)}, bf16[128,1024]{1,0:T(8,128)(2,1)S(1)}, u32[]{:S(2)}, u32[]{:S(2)}) %collective-permute-start.6) | collective-permute-done | bytes 262176 | tf_op jit(solution)/shard_map/ppermute | solution.py:43
  28.0 3.3 %collective-permute-start.12 = (bf16[32,4864]{1,0:T(8,128)(2,1)S(1)}, bf16[32,4864]{1,0:T(8,128)(2,1)S(1)}, u32[]{:S(2)}, u32[]{:S(2)}) collective-permute-start(bf16[32,4864]{1,0:T(8,128)(2,1)S(1)} %slice.99), channel_id=1, source_target_pairs={{0,96},{16,112},{32,0},{48,16},{64,32},{80,48},{96,64},{112,80},{1... | collective-permute-start | bytes 933896 | tf_op jit(solution)/shard_map/ppermute | solution.py:30
  32.4 4.4 %shard_map.51 = (f32[8,128]{1,0:T(8,128)S(1)}, bf16[512,2432]{1,0:T(8,128)(2,1)S(1)}, bf16[512,2432]{1,0:T(8,128)(2,1)S(1)}) custom-call(bf16[1024,4864]{1,0:T(8,128)(2,1)} %refs_2_.3, bf16[64,4864]{1,0:T(8,128)(2,1)S(1)} %bitcast.12, bf16[64,4864]{1,0:T(8,128)(2,1)S(1)} %collective-permute-done.refs_4_.refs_2_, ...), custom_call_target="tpu_custom_call" | custom-call | flops 2147483648 | bytes 64 | tf_op jit(solution)/shard_map/pallas_call | solution.py:57
  36.8 2.3 %collective-permute-done.10.refs_5_ = bf16[128,1024]{1,0:T(8,128)(2,1)S(1)} collective-permute-done((bf16[128,1024]{1,0:T(8,128)(2,1)S(1)}, bf16[128,1024]{1,0:T(8,128)(2,1)S(1)}, u32[]{:S(2)}, u32[]{:S(2)}) %collective-permute-start.10) | collective-permute-done | bytes 262176 | tf_op jit(solution)/shard_map/ppermute | solution.py:43
  39.8 1.8 %collective-permute-done.11.refs_0_ = bf16[32,4864]{1,0:T(8,128)(2,1)S(1)} collective-permute-done((bf16[32,4864]{1,0:T(8,128)(2,1)S(1)}, bf16[32,4864]{1,0:T(8,128)(2,1)S(1)}, u32[]{:S(2)}, u32[]{:S(2)}) %collective-permute-start.11) | collective-permute-done | bytes 311328 | tf_op jit(solution)/shard_map/ppermute | solution.py:30
  43.3 4.3 %shard_map.54 = (f32[512,2432]{1,0:T(8,128)S(1)}, f32[512,2432]{1,0:T(8,128)S(1)}, f32[16,128]{1,0:T(8,128)S(1)}, bf16[512,2432]{1,0:T(8,128)(2,1)S(1)}, bf16[512,2432]{1,0:T(8,128)(2,1)}) custom-call(bf16[512,2432]{1,0:T(8,128)(2,1)S(1)} %get-tuple-element.35.refs_0_, ...), custom_call_target="tpu_custom_call", output_to_operand_aliasing={{3}: (0, {})} | custom-call | flops 2550136832 | bytes 64 | tf_op jit(solution)/shard_map/pallas_call | solution.py:57
  47.7 4.7 %shard_map.55 = (f32[512,2432]{1,0:T(8,128)}, f32[512,2432]{1,0:T(8,128)S(1)}, f32[16,128]{1,0:T(8,128)S(1)}, bf16[512,2432]{1,0:T(8,128)(2,1)S(1)}, bf16[512,2432]{1,0:T(8,128)(2,1)}) custom-call(bf16[512,2432]{1,0:T(8,128)(2,1)S(1)} %get-tuple-element.41.refs_0_, bf16[1024,512]{1,0:T(8,128)(2,1)S(1)} %get-tuple-element.37.refs_1_, ...), custom_call_target="tpu_custom_call", output_to_operand_aliasing={{3}: (0, {})} | custom-call | flops 2550136832 | bytes 64 | tf_op jit(solution)/shard_map/pallas_call | solution.py:57
  52.5 2.1 %collective-permute-start.17 = (f32[24,128]{1,0:T(8,128)S(1)}, f32[24,128]{1,0:T(8,128)S(1)}, u32[]{:S(2)}, u32[]{:S(2)}) collective-permute-start(f32[24,128]{1,0:T(8,128)S(1)} %pad_maximum_fusion.1), channel_id=1, source_target_pairs={{0,3},{1,0},{2,1},{3,2},{4,7},{5,4},{6,5},{7,6},{8,11},{9,8},{10,9... | collective-permute-start | bytes 36872 | tf_op jit(solution)/shard_map/ppermute | solution.py:43
  56.2 3.5 %collective-permute-done.16 = f32[24,128]{1,0:T(8,128)S(1)} collective-permute-done((f32[24,128]{1,0:T(8,128)S(1)}, f32[24,128]{1,0:T(8,128)S(1)}, u32[]{:S(2)}, u32[]{:S(2)}) %collective-permute-start.16) | collective-permute-done | bytes 12320 | tf_op jit(solution)/shard_map/ppermute | solution.py:43
  66.3 1.9 %shard_map.56 = (bf16[1024,2432]{1,0:T(8,128)(2,1)S(1)}, bf16[64,2432]{1,0:T(8,128)(2,1)S(1)}, bf16[64,2432]{1,0:T(8,128)(2,1)S(1)}) custom-call(f32[512,2432]{1,0:T(8,128)S(1)} %get-tuple-element.43.refs_4_.refs_0_, f32[512,2432]{1,0:T(8,128)S(1)} %get-tuple-element.44.refs_5_.refs_1_, bf16[1024,4864]{1,0:T(8,128)(2,1)S(1)} %bitcast.6, ...), custom_call_target="tpu_custom_call" | custom-call | flops 1275068416 | bytes 64 | tf_op jit(solution)/shard_map/pallas_call | solution.py:57
  68.6 2.0 %shard_map.57 = (bf16[1024,2432]{1,0:T(8,128)(2,1)S(1)}, bf16[64,2432]{1,0:T(8,128)(2,1)S(1)}, bf16[64,2432]{1,0:T(8,128)(2,1)S(1)}) custom-call(f32[512,2432]{1,0:T(8,128)S(1)} %bitcast.8, f32[512,2432]{1,0:T(8,128)S(1)} %get-tuple-element.50.refs_1_, bf16[1024,4864]{1,0:T(8,128)(2,1)S(1)} %bitcast.6, f32[8,128]{1,0:T(8,128)S(1)} %get-tuple-element.64.refs_3_, ...), custom_call_target="tpu_custom_call" | custom-call | flops 1275068416 | bytes 64 | tf_op jit(solution)/shard_map/pallas_call | solution.py:57
  74.6 4.3 %shard_map.59 = (bf16[192,4864]{1,0:T(8,128)(2,1)S(1)}, bf16[64,4864]{1,0:T(8,128)(2,1)S(1)}, bf16[64,4864]{1,0:T(8,128)(2,1)S(1)}, bf16[64,4864]{1,0:T(8,128)(2,1)S(1)}) custom-call(bf16[512,1024]{1,0:T(8,128)(2,1)S(1)} %get-tuple-element.38.refs_3_.refs_4_.refs_0_, bf16[1024,2432]{1,0:T(8,128)(2,1)S(1)} %get-tuple-element.48.refs_5_.refs_1_.refs_2_, ...), custom_call_target="tpu_custom_call" | custom-call | flops 3825205248 | bytes 64 | tf_op jit(solution)/shard_map/pallas_call | solution.py:57
  79.6 5.8 %shard_map.60 = bf16[512,1024]{1,0:T(8,128)(2,1)S(1)} custom-call(bf16[512,2432]{1,0:T(8,128)(2,1)S(1)} %copy-done.3, bf16[512,2432]{1,0:T(8,128)(2,1)S(1)} %copy-done.2, bf16[1024,2432]{1,0:T(8,128)(2,1)S(1)} %get-tuple-element.48.refs_5_.refs_1_.refs_2_, bf16[1024,2432]{1,0:T(8,128)(2,1)S(1)} %get-tuple-element.51.refs_2_.refs_3_, ...), custom_call_target="tpu_custom_call" | custom-call | flops 5100273664 | bytes 64 | tf_op jit(solution)/shard_map/pallas_call | solution.py:57
  85.5 2.1 %collective-permute-start.23 = (bf16[128,1024]{1,0:T(8,128)(2,1)S(1)}, bf16[128,1024]{1,0:T(8,128)(2,1)S(1)}, u32[]{:S(2)}, u32[]{:S(2)}) collective-permute-start(bf16[128,1024]{1,0:T(8,128)(2,1)S(1)} %get-tuple-element.71), channel_id=1, source_target_pairs={{0,12},{1,13},{2,14},{3,15},{4,0},{5,1},{6,2},{7,3},{8,4},{9,5},{1... | collective-permute-start | bytes 786440 | tf_op jit(solution)/shard_map/ppermute | solution.py:43
  89.6 3.2 %collective-permute-start.35 = (bf16[64,4864]{1,0:T(8,128)(2,1)S(1)}, bf16[64,4864]{1,0:T(8,128)(2,1)S(1)}, u32[]{:S(2)}, u32[]{:S(2)}) collective-permute-start(bf16[64,4864]{1,0:T(8,128)(2,1)S(1)} %get-tuple-element.63), channel_id=1, source_target_pairs={{0,96},{16,112},{32,0},{48,16},{64,32},{80,48},{96,64},{112,80},{1... | collective-permute-start | bytes 1867784 | tf_op jit(solution)/shard_map/ppermute | solution.py:30
  92.8 5.2 %collective-permute-done.25 = bf16[128,1024]{1,0:T(8,128)(2,1)S(1)} collective-permute-done((bf16[128,1024]{1,0:T(8,128)(2,1)S(1)}, bf16[128,1024]{1,0:T(8,128)(2,1)S(1)}, u32[]{:S(2)}, u32[]{:S(2)}) %collective-permute-start.25) | collective-permute-done | bytes 262176 | tf_op jit(solution)/shard_map/ppermute | solution.py:43
  100.3 2.0 %collective-permute-start.27 = (bf16[32,1024]{1,0:T(8,128)(2,1)S(1)}, bf16[32,1024]{1,0:T(8,128)(2,1)S(1)}, u32[]{:S(2)}, u32[]{:S(2)}) collective-permute-start(bf16[32,1024]{1,0:T(8,128)(2,1)S(1)} %get-tuple-element.76), channel_id=1, source_target_pairs={{0,2},{1,3},{2,0},{3,1},{4,6},{5,7},{6,4},{7,5},{8,10},{9,11},{10,... | collective-permute-start | bytes 196616 | tf_op jit(solution)/shard_map/ppermute | solution.py:43
  102.5 2.4 %collective-permute-done.28 = bf16[32,1024]{1,0:T(8,128)(2,1)S(1)} collective-permute-done((bf16[32,1024]{1,0:T(8,128)(2,1)S(1)}, bf16[32,1024]{1,0:T(8,128)(2,1)S(1)}, u32[]{:S(2)}, u32[]{:S(2)}) %collective-permute-start.28) | collective-permute-done | bytes 65568 | tf_op jit(solution)/shard_map/ppermute | solution.py:43
  (94 shorter events, 28.8 us)
Async XLA Ops:
  0.6 26.6 %collective-permute-start.2 = (bf16[64,4864]{1,0:T(8,128)(2,1)}, bf16[64,4864]{1,0:T(8,128)(2,1)S(1)}, u32[]{:S(2)}, u32[]{:S(2)}) collective-permute-start(bf16[64,4864]{1,0:T(8,128)(2,1)} %bitcast.9), channel_id=1, source_target_pairs={{0,96},{16,112},{32,0},{48,16},{64,32},{80,48},{96,64},{112,80},{1... | collective-permute-start | bytes 1867784 | tf_op jit(solution)/shard_map/ppermute | solution.py:30
  3.5 23.7 %collective-permute-start.1 = (bf16[64,4864]{1,0:T(8,128)(2,1)}, bf16[64,4864]{1,0:T(8,128)(2,1)S(1)}, u32[]{:S(2)}, u32[]{:S(2)}) collective-permute-start(bf16[64,4864]{1,0:T(8,128)(2,1)} %bitcast.10), channel_id=1, source_target_pairs={{0,32},{16,48},{32,64},{48,80},{64,96},{80,112},{96,0},{112,16},{1... | collective-permute-start | bytes 1867784 | tf_op jit(solution)/shard_map/ppermute | solution.py:30
  3.5 23.7 %collective-permute-start = (bf16[64,4864]{1,0:T(8,128)(2,1)}, bf16[64,4864]{1,0:T(8,128)(2,1)S(1)}, u32[]{:S(2)}, u32[]{:S(2)}) collective-permute-start(bf16[64,4864]{1,0:T(8,128)(2,1)} %bitcast.11), channel_id=1, source_target_pairs={{0,16},{16,0},{32,48},{48,32},{64,80},{80,64},{96,112},{112,96},{1... | collective-permute-start | bytes 1867784 | tf_op jit(solution)/shard_map/ppermute | solution.py:26
  6.6 6.0 %collective-permute-start.4 = (bf16[32,1024]{1,0:T(8,128)(2,1)}, bf16[32,1024]{1,0:T(8,128)(2,1)S(1)}, u32[]{:S(2)}, u32[]{:S(2)}) collective-permute-start(bf16[32,1024]{1,0:T(8,128)(2,1)} %bitcast.14), channel_id=1, source_target_pairs={{0,2},{1,3},{2,0},{3,1},{4,6},{5,7},{6,4},{7,5},{8,10},{9,11},{10,... | collective-permute-start | bytes 196616 | tf_op jit(solution)/shard_map/ppermute | solution.py:43
  8.8 5.9 %collective-permute-start.3 = (bf16[32,1024]{1,0:T(8,128)(2,1)}, bf16[32,1024]{1,0:T(8,128)(2,1)S(1)}, u32[]{:S(2)}, u32[]{:S(2)}) collective-permute-start(bf16[32,1024]{1,0:T(8,128)(2,1)} %bitcast.15), channel_id=1, source_target_pairs={{0,1},{1,2},{2,3},{3,0},{4,5},{5,6},{6,7},{7,4},{8,9},{9,10},{10,1... | collective-permute-start | bytes 196616 | tf_op jit(solution)/shard_map/ppermute | solution.py:43
  15.6 8.0 %collective-permute-start.7 = (bf16[128,1024]{1,0:T(8,128)(2,1)S(1)}, bf16[128,1024]{1,0:T(8,128)(2,1)S(1)}, u32[]{:S(2)}, u32[]{:S(2)}) collective-permute-start(bf16[128,1024]{1,0:T(8,128)(2,1)S(1)} %pad_maximum_fusion), channel_id=1, source_target_pairs={{0,12},{1,13},{2,14},{3,15},{4,0},{5,1},{6,2},{7,3},{8,4},{9,5},{1... | collective-permute-start | bytes 786440 | tf_op jit(solution)/shard_map/ppermute | solution.py:43
  19.7 7.6 %collective-permute-start.6 = (bf16[128,1024]{1,0:T(8,128)(2,1)S(1)}, bf16[128,1024]{1,0:T(8,128)(2,1)S(1)}, u32[]{:S(2)}, u32[]{:S(2)}) collective-permute-start(bf16[128,1024]{1,0:T(8,128)(2,1)S(1)} %pad_maximum_fusion), channel_id=1, source_target_pairs={{0,4},{1,5},{2,6},{3,7},{4,8},{5,9},{6,10},{7,11},{8,12},{9,13},{1... | collective-permute-start | bytes 786440 | tf_op jit(solution)/shard_map/ppermute | solution.py:43
  28.0 11.8 %collective-permute-start.12 = (bf16[32,4864]{1,0:T(8,128)(2,1)S(1)}, bf16[32,4864]{1,0:T(8,128)(2,1)S(1)}, u32[]{:S(2)}, u32[]{:S(2)}) collective-permute-start(bf16[32,4864]{1,0:T(8,128)(2,1)S(1)} %slice.99), channel_id=1, source_target_pairs={{0,96},{16,112},{32,0},{48,16},{64,32},{80,48},{96,64},{112,80},{1... | collective-permute-start | bytes 933896 | tf_op jit(solution)/shard_map/ppermute | solution.py:30
  31.3 10.3 %collective-permute-start.11 = (bf16[32,4864]{1,0:T(8,128)(2,1)S(1)}, bf16[32,4864]{1,0:T(8,128)(2,1)S(1)}, u32[]{:S(2)}, u32[]{:S(2)}) collective-permute-start(bf16[32,4864]{1,0:T(8,128)(2,1)S(1)} %slice.98), channel_id=1, source_target_pairs={{0,32},{16,48},{32,64},{48,80},{64,96},{80,112},{96,0},{112,16},{1... | collective-permute-start | bytes 933896 | tf_op jit(solution)/shard_map/ppermute | solution.py:30
  31.3 7.9 %collective-permute-start.10 = (bf16[128,1024]{1,0:T(8,128)(2,1)S(1)}, bf16[128,1024]{1,0:T(8,128)(2,1)S(1)}, u32[]{:S(2)}, u32[]{:S(2)}) collective-permute-start(bf16[128,1024]{1,0:T(8,128)(2,1)S(1)} %pad_maximum_fusion), channel_id=1, source_target_pairs={{0,8},{1,9},{2,10},{3,11},{4,12},{5,13},{6,14},{7,15},{8,0},{9,1},... | collective-permute-start | bytes 786440 | tf_op jit(solution)/shard_map/ppermute | solution.py:43
  41.7 5.9 %collective-permute-start.14 = (bf16[64,2432]{1,0:T(8,128)(2,1)S(1)}, bf16[64,2432]{1,0:T(8,128)(2,1)S(1)}, u32[]{:S(2)}, u32[]{:S(2)}) collective-permute-start(bf16[64,2432]{1,0:T(8,128)(2,1)S(1)} %get-tuple-element.42.refs_2_), channel_id=1, source_target_pairs={{0,16},{16,0},{32,48},{48,32},{64,80},{80,64},{96,112},{112,96},{1... | collective-permute-start | bytes 933896 | tf_op jit(solution)/shard_map/ppermute | solution.py:26
  60.7 5.5 %collective-permute-start.18 = (f32[24,128]{1,0:T(8,128)S(1)}, f32[24,128]{1,0:T(8,128)S(1)}, u32[]{:S(2)}, u32[]{:S(2)}) collective-permute-start(f32[24,128]{1,0:T(8,128)S(1)} %pad_maximum_fusion.2), channel_id=1, source_target_pairs={{0,4},{1,5},{2,6},{3,7},{4,8},{5,9},{6,10},{7,11},{8,12},{9,13},{1... | collective-permute-start | bytes 36872 | tf_op jit(solution)/shard_map/ppermute | solution.py:43
  72.5 13.0 %collective-permute-start.33 = (bf16[32,4864]{1,0:T(8,128)(2,1)S(1)}, bf16[32,4864]{1,0:T(8,128)(2,1)S(1)}, u32[]{:S(2)}, u32[]{:S(2)}) collective-permute-start(bf16[32,4864]{1,0:T(8,128)(2,1)S(1)} %get-tuple-element.61), channel_id=1, source_target_pairs={{0,96},{16,112},{32,0},{48,16},{64,32},{80,48},{96,64},{112,80},{1... | collective-permute-start | bytes 933896 | tf_op jit(solution)/shard_map/ppermute | solution.py:30
  74.1 13.5 %collective-permute-start.32 = (bf16[32,4864]{1,0:T(8,128)(2,1)S(1)}, bf16[32,4864]{1,0:T(8,128)(2,1)S(1)}, u32[]{:S(2)}, u32[]{:S(2)}) collective-permute-start(bf16[32,4864]{1,0:T(8,128)(2,1)S(1)} %get-tuple-element.56.refs_3_), channel_id=1, source_target_pairs={{0,32},{16,48},{32,64},{48,80},{64,96},{80,112},{96,0},{112,16},{1... | collective-permute-start | bytes 933896 | tf_op jit(solution)/shard_map/ppermute | solution.py:30
  78.9 8.7 %collective-permute-start.29 = (bf16[64,4864]{1,0:T(8,128)(2,1)S(1)}, bf16[64,4864]{1,0:T(8,128)(2,1)S(1)}, u32[]{:S(2)}, u32[]{:S(2)}) collective-permute-start(bf16[64,4864]{1,0:T(8,128)(2,1)S(1)} %get-tuple-element.58), channel_id=1, source_target_pairs={{0,16},{16,0},{32,48},{48,32},{64,80},{80,64},{96,112},{112,96},{1... | collective-permute-start | bytes 1867784 | tf_op jit(solution)/shard_map/ppermute | solution.py:26
  79.0 10.1 %collective-permute-start.30 = (bf16[64,4864]{1,0:T(8,128)(2,1)S(1)}, bf16[64,4864]{1,0:T(8,128)(2,1)S(1)}, u32[]{:S(2)}, u32[]{:S(2)}) collective-permute-start(bf16[64,4864]{1,0:T(8,128)(2,1)S(1)} %get-tuple-element.59), channel_id=1, source_target_pairs={{0,16},{16,0},{32,48},{48,32},{64,80},{80,64},{96,112},{112,96},{1... | collective-permute-start | bytes 1867784 | tf_op jit(solution)/shard_map/ppermute | solution.py:26
  79.5 9.6 %collective-permute-start.31 = (bf16[64,4864]{1,0:T(8,128)(2,1)S(1)}, bf16[64,4864]{1,0:T(8,128)(2,1)S(1)}, u32[]{:S(2)}, u32[]{:S(2)}) collective-permute-start(bf16[64,4864]{1,0:T(8,128)(2,1)S(1)} %get-tuple-element.60), channel_id=1, source_target_pairs={{0,16},{16,0},{32,48},{48,32},{64,80},{80,64},{96,112},{112,96},{1... | collective-permute-start | bytes 1867784 | tf_op jit(solution)/shard_map/ppermute | solution.py:26
  85.5 7.3 %collective-permute-start.23 = (bf16[128,1024]{1,0:T(8,128)(2,1)S(1)}, bf16[128,1024]{1,0:T(8,128)(2,1)S(1)}, u32[]{:S(2)}, u32[]{:S(2)}) collective-permute-start(bf16[128,1024]{1,0:T(8,128)(2,1)S(1)} %get-tuple-element.71), channel_id=1, source_target_pairs={{0,12},{1,13},{2,14},{3,15},{4,0},{5,1},{6,2},{7,3},{8,4},{9,5},{1... | collective-permute-start | bytes 786440 | tf_op jit(solution)/shard_map/ppermute | solution.py:43
  87.6 10.4 %collective-permute-start.25 = (bf16[128,1024]{1,0:T(8,128)(2,1)S(1)}, bf16[128,1024]{1,0:T(8,128)(2,1)S(1)}, u32[]{:S(2)}, u32[]{:S(2)}) collective-permute-start(bf16[128,1024]{1,0:T(8,128)(2,1)S(1)} %get-tuple-element.72), channel_id=1, source_target_pairs={{0,4},{1,5},{2,6},{3,7},{4,8},{5,9},{6,10},{7,11},{8,12},{9,13},{1... | collective-permute-start | bytes 786440 | tf_op jit(solution)/shard_map/ppermute | solution.py:43
  87.6 10.4 %collective-permute-start.24 = (bf16[128,1024]{1,0:T(8,128)(2,1)S(1)}, bf16[128,1024]{1,0:T(8,128)(2,1)S(1)}, u32[]{:S(2)}, u32[]{:S(2)}) collective-permute-start(bf16[128,1024]{1,0:T(8,128)(2,1)S(1)} %get-tuple-element.73), channel_id=1, source_target_pairs={{0,8},{1,9},{2,10},{3,11},{4,12},{5,13},{6,14},{7,15},{8,0},{9,1},... | collective-permute-start | bytes 786440 | tf_op jit(solution)/shard_map/ppermute | solution.py:43
  89.5 17.3 %collective-permute-start.34 = (bf16[64,4864]{1,0:T(8,128)(2,1)S(1)}, bf16[64,4864]{1,0:T(8,128)(2,1)S(1)}, u32[]{:S(2)}, u32[]{:S(2)}) collective-permute-start(bf16[64,4864]{1,0:T(8,128)(2,1)S(1)} %get-tuple-element.62), channel_id=1, source_target_pairs={{0,32},{16,48},{32,64},{48,80},{64,96},{80,112},{96,0},{112,16},{1... | collective-permute-start | bytes 1867784 | tf_op jit(solution)/shard_map/ppermute | solution.py:30
  89.6 17.2 %collective-permute-start.35 = (bf16[64,4864]{1,0:T(8,128)(2,1)S(1)}, bf16[64,4864]{1,0:T(8,128)(2,1)S(1)}, u32[]{:S(2)}, u32[]{:S(2)}) collective-permute-start(bf16[64,4864]{1,0:T(8,128)(2,1)S(1)} %get-tuple-element.63), channel_id=1, source_target_pairs={{0,96},{16,112},{32,0},{48,16},{64,32},{80,48},{96,64},{112,80},{1... | collective-permute-start | bytes 1867784 | tf_op jit(solution)/shard_map/ppermute | solution.py:30
  99.4 5.5 %collective-permute-start.28 = (bf16[32,1024]{1,0:T(8,128)(2,1)S(1)}, bf16[32,1024]{1,0:T(8,128)(2,1)S(1)}, u32[]{:S(2)}, u32[]{:S(2)}) collective-permute-start(bf16[32,1024]{1,0:T(8,128)(2,1)S(1)} %get-tuple-element.75), channel_id=1, source_target_pairs={{0,1},{1,2},{2,3},{3,0},{4,5},{5,6},{6,7},{7,4},{8,9},{9,10},{10,1... | collective-permute-start | bytes 196616 | tf_op jit(solution)/shard_map/ppermute | solution.py:43
  100.3 5.8 %collective-permute-start.27 = (bf16[32,1024]{1,0:T(8,128)(2,1)S(1)}, bf16[32,1024]{1,0:T(8,128)(2,1)S(1)}, u32[]{:S(2)}, u32[]{:S(2)}) collective-permute-start(bf16[32,1024]{1,0:T(8,128)(2,1)S(1)} %get-tuple-element.76), channel_id=1, source_target_pairs={{0,2},{1,3},{2,0},{3,1},{4,6},{5,7},{6,4},{7,5},{8,10},{9,11},{10,... | collective-permute-start | bytes 196616 | tf_op jit(solution)/shard_map/ppermute | solution.py:43
  (21 other events, 152.1 us)

commit v4 on v3

--- a/solution.py
+++ b/solution.py
@@ -243,7 +243,7 @@
     block = jnp.concatenate(first_parts, axis=0)
     later = [shift(block, 1, k) for k in (1, 2, 3)]
     t1 = core_swap(own)
-    t2, t4 = run(hold_kernel, [((64, COLS), BF16)] * 2, t2, t4, wait=(later[0], later[2], t1))
+    t2, t4 = run(hold_kernel, [((64, COLS), BF16)] * 2, t2, t4, wait=(later[0], later[2]))
 
     row_counts, *near = run(
         gather_kernel,

time: 108 us -> 107 us (level)
  waiting for transfers between devices: 38.3 us -> 36.9 us
    ppermute x18, waiting for transfers between devices: 34.1 us -> 32.8 us  [shift(): return lax.ppermute(a, ('state', 'vocab'), perm)]
  transfers between devices with their start and end apart: 36 -> 36, of which waited for: 19 -> 18; matrix products, arithmetic and copies ran while one was open for 2% -> 2% of each run, Pallas kernels for 20% -> 21%
where the time goes in v4:
time: 107 us; the launch traced here: 106 us
  waiting for transfers between devices  36.9 us (34%)
  starting transfers between devices  35.2 us (33%)
  Pallas kernels  29.7 us (28%)
  other arithmetic  1.75 us (2%)
  local copies, waits for them, and re-layouts  1.22 us (1%)
  between operations  1.16 us (1%)
    ppermute x18, waiting for transfers between devices, shift(): return lax.ppermute(a, ('state', 'vocab'), perm)  32.8 us
    pallas_call x13, Pallas kernels, run(): pl.pallas_call(wrapped, out_shape=tuple(((space[0] if space else VMEM)(sh...  29.7 us
    ppermute x18, starting transfers between devices, shift(): return lax.ppermute(a, ('state', 'vocab'), perm)  20.9 us
    ppermute x8, starting transfers between devices, x_shift(): return lax.ppermute(a, 'state', [(i, (i + 2 * step) % 8) for i in range(8)])  11.6 us
    ppermute x10, starting transfers between devices, core_swap(): return lax.ppermute(a, 'state', [(i, i ^ 1) for i in range(8)])  2.7 us
    ppermute x10, waiting for transfers between devices, core_swap(): return lax.ppermute(a, 'state', [(i, i ^ 1) for i in range(8)])  2.34 us
  transfers between devices with their start and end apart: 36, of which 18 were waited for; matrix products, arithmetic and copies ran while one was open for 2% of the time, Pallas kernels for 21%

profile of v4, /device:TPU:0, one launch (start us, length us, event | category | flops | bytes accessed | tf_op | source)
XLA Modules:
  0.0 106.0 jit_solution(7546071805716949900)
XLA Ops:
  0.6 2.9 %collective-permute-start.2 = (bf16[64,4864]{1,0:T(8,128)(2,1)}, bf16[64,4864]{1,0:T(8,128)(2,1)S(1)}, u32[]{:S(2)}, u32[]{:S(2)}) collective-permute-start(bf16[64,4864]{1,0:T(8,128)(2,1)} %bitcast.9), channel_id=1, source_target_pairs={{0,96},{16,112},{32,0},{48,16},{64,32},{80,48},{96,64},{112,80},{1... | collective-permute-start | bytes 1867784 | tf_op jit(solution)/shard_map/ppermute | solution.py:30
  3.5 3.0 %collective-permute-start.5 = (bf16[32,1024]{1,0:T(8,128)(2,1)}, bf16[32,1024]{1,0:T(8,128)(2,1)S(1)}, u32[]{:S(2)}, u32[]{:S(2)}) collective-permute-start(bf16[32,1024]{1,0:T(8,128)(2,1)} %bitcast.13), channel_id=1, source_target_pairs={{0,3},{1,0},{2,1},{3,2},{4,7},{5,4},{6,5},{7,6},{8,11},{9,8},{10,9... | collective-permute-start | bytes 196616 | tf_op jit(solution)/shard_map/ppermute | solution.py:43
  8.8 3.8 %collective-permute-done.4.refs_2_ = bf16[32,1024]{1,0:T(8,128)(2,1)S(1)} collective-permute-done((bf16[32,1024]{1,0:T(8,128)(2,1)}, bf16[32,1024]{1,0:T(8,128)(2,1)S(1)}, u32[]{:S(2)}, u32[]{:S(2)}) %collective-permute-start.4) | collective-permute-done | bytes 65568 | tf_op jit(solution)/shard_map/ppermute | solution.py:43
  14.1 4.1 %collective-permute-start.7 = (bf16[128,1024]{1,0:T(8,128)(2,1)S(1)}, bf16[128,1024]{1,0:T(8,128)(2,1)S(1)}, u32[]{:S(2)}, u32[]{:S(2)}) collective-permute-start(bf16[128,1024]{1,0:T(8,128)(2,1)S(1)} %pad_maximum_fusion), channel_id=1, source_target_pairs={{0,12},{1,13},{2,14},{3,15},{4,0},{5,1},{6,2},{7,3},{8,4},{9,5},{1... | collective-permute-start | bytes 786440 | tf_op jit(solution)/shard_map/ppermute | solution.py:43
  18.2 3.9 %collective-permute-done.7.refs_3_.refs_6_ = bf16[128,1024]{1,0:T(8,128)(2,1)S(1)} collective-permute-done((bf16[128,1024]{1,0:T(8,128)(2,1)S(1)}, bf16[128,1024]{1,0:T(8,128)(2,1)S(1)}, u32[]{:S(2)}, u32[]{:S(2)}) %collective-permute-start.7) | collective-permute-done | bytes 262176 | tf_op jit(solution)/shard_map/ppermute | solution.py:43
  22.1 3.7 %collective-permute-done.6.refs_2_.refs_4_ = bf16[128,1024]{1,0:T(8,128)(2,1)S(1)} collective-permute-done((bf16[128,1024]{1,0:T(8,128)(2,1)S(1)}, bf16[128,1024]{1,0:T(8,128)(2,1)S(1)}, u32[]{:S(2)}, u32[]{:S(2)}) %collective-permute-start.6) | collective-permute-done | bytes 262176 | tf_op jit(solution)/shard_map/ppermute | solution.py:43
  26.5 3.3 %collective-permute-start.12 = (bf16[32,4864]{1,0:T(8,128)(2,1)S(1)}, bf16[32,4864]{1,0:T(8,128)(2,1)S(1)}, u32[]{:S(2)}, u32[]{:S(2)}) collective-permute-start(bf16[32,4864]{1,0:T(8,128)(2,1)S(1)} %slice.99), channel_id=1, source_target_pairs={{0,96},{16,112},{32,0},{48,16},{64,32},{80,48},{96,64},{112,80},{1... | collective-permute-start | bytes 933896 | tf_op jit(solution)/shard_map/ppermute | solution.py:30
  31.0 4.4 %shard_map.51 = (f32[8,128]{1,0:T(8,128)S(1)}, bf16[512,2432]{1,0:T(8,128)(2,1)S(1)}, bf16[512,2432]{1,0:T(8,128)(2,1)S(1)}) custom-call(bf16[1024,4864]{1,0:T(8,128)(2,1)} %refs_2_.3, bf16[64,4864]{1,0:T(8,128)(2,1)S(1)} %bitcast.12, bf16[64,4864]{1,0:T(8,128)(2,1)S(1)} %collective-permute-done.refs_2_, bf16[64,4864]{1,0:T(8,128)(2,1)S(1)} %get-tuple-element.33.refs_3_, ...), custom_call_target="tpu_custom_call" | custom-call | flops 2147483648 | bytes 64 | tf_op jit(solution)/shard_map/pallas_call | solution.py:57
  35.4 2.3 %collective-permute-done.10.refs_5_ = bf16[128,1024]{1,0:T(8,128)(2,1)S(1)} collective-permute-done((bf16[128,1024]{1,0:T(8,128)(2,1)S(1)}, bf16[128,1024]{1,0:T(8,128)(2,1)S(1)}, u32[]{:S(2)}, u32[]{:S(2)}) %collective-permute-start.10) | collective-permute-done | bytes 262176 | tf_op jit(solution)/shard_map/ppermute | solution.py:43
  38.3 1.8 %collective-permute-done.11.refs_0_ = bf16[32,4864]{1,0:T(8,128)(2,1)S(1)} collective-permute-done((bf16[32,4864]{1,0:T(8,128)(2,1)S(1)}, bf16[32,4864]{1,0:T(8,128)(2,1)S(1)}, u32[]{:S(2)}, u32[]{:S(2)}) %collective-permute-start.11) | collective-permute-done | bytes 311328 | tf_op jit(solution)/shard_map/ppermute | solution.py:30
  41.9 4.3 %shard_map.54 = (f32[512,2432]{1,0:T(8,128)S(1)}, f32[512,2432]{1,0:T(8,128)S(1)}, f32[16,128]{1,0:T(8,128)S(1)}, bf16[512,2432]{1,0:T(8,128)(2,1)S(1)}, bf16[512,2432]{1,0:T(8,128)(2,1)}) custom-call(bf16[512,2432]{1,0:T(8,128)(2,1)S(1)} %get-tuple-element.35.refs_0_, ...), custom_call_target="tpu_custom_call", output_to_operand_aliasing={{3}: (0, {})} | custom-call | flops 2550136832 | bytes 64 | tf_op jit(solution)/shard_map/pallas_call | solution.py:57
  46.2 4.7 %shard_map.55 = (f32[512,2432]{1,0:T(8,128)}, f32[512,2432]{1,0:T(8,128)S(1)}, f32[16,128]{1,0:T(8,128)S(1)}, bf16[512,2432]{1,0:T(8,128)(2,1)S(1)}, bf16[512,2432]{1,0:T(8,128)(2,1)}) custom-call(bf16[512,2432]{1,0:T(8,128)(2,1)S(1)} %get-tuple-element.41.refs_0_, bf16[1024,512]{1,0:T(8,128)(2,1)S(1)} %get-tuple-element.37.refs_1_, ...), custom_call_target="tpu_custom_call", output_to_operand_aliasing={{3}: (0, {})} | custom-call | flops 2550136832 | bytes 64 | tf_op jit(solution)/shard_map/pallas_call | solution.py:57
  54.8 2.1 %collective-permute-done.16 = f32[24,128]{1,0:T(8,128)S(1)} collective-permute-done((f32[24,128]{1,0:T(8,128)S(1)}, f32[24,128]{1,0:T(8,128)S(1)}, u32[]{:S(2)}, u32[]{:S(2)}) %collective-permute-start.16) | collective-permute-done | bytes 12320 | tf_op jit(solution)/shard_map/ppermute | solution.py:43
  59.6 1.7 %collective-permute-done.20 = f32[24,128]{1,0:T(8,128)S(1)} collective-permute-done((f32[24,128]{1,0:T(8,128)S(1)}, f32[24,128]{1,0:T(8,128)S(1)}, u32[]{:S(2)}, u32[]{:S(2)}) %collective-permute-start.20) | collective-permute-done | bytes 12320 | tf_op jit(solution)/shard_map/ppermute | solution.py:43
  61.2 1.6 %collective-permute-done.19 = f32[24,128]{1,0:T(8,128)S(1)} collective-permute-done((f32[24,128]{1,0:T(8,128)S(1)}, f32[24,128]{1,0:T(8,128)S(1)}, u32[]{:S(2)}, u32[]{:S(2)}) %collective-permute-start.19) | collective-permute-done | bytes 12320 | tf_op jit(solution)/shard_map/ppermute | solution.py:43
  64.0 1.9 %shard_map.56 = (bf16[1024,2432]{1,0:T(8,128)(2,1)S(1)}, bf16[64,2432]{1,0:T(8,128)(2,1)S(1)}, bf16[64,2432]{1,0:T(8,128)(2,1)S(1)}) custom-call(f32[512,2432]{1,0:T(8,128)S(1)} %get-tuple-element.43.refs_4_.refs_0_, f32[512,2432]{1,0:T(8,128)S(1)} %get-tuple-element.44.refs_5_.refs_1_, bf16[1024,4864]{1,0:T(8,128)(2,1)S(1)} %bitcast.6, ...), custom_call_target="tpu_custom_call" | custom-call | flops 1275068416 | bytes 64 | tf_op jit(solution)/shard_map/pallas_call | solution.py:57
  66.3 2.0 %shard_map.57 = (bf16[1024,2432]{1,0:T(8,128)(2,1)S(1)}, bf16[64,2432]{1,0:T(8,128)(2,1)S(1)}, bf16[64,2432]{1,0:T(8,128)(2,1)S(1)}) custom-call(f32[512,2432]{1,0:T(8,128)S(1)} %bitcast.8, f32[512,2432]{1,0:T(8,128)S(1)} %get-tuple-element.50.refs_1_, bf16[1024,4864]{1,0:T(8,128)(2,1)S(1)} %bitcast.6, f32[8,128]{1,0:T(8,128)S(1)} %get-tuple-element.64.refs_3_, ...), custom_call_target="tpu_custom_call" | custom-call | flops 1275068416 | bytes 64 | tf_op jit(solution)/shard_map/pallas_call | solution.py:57
  72.3 4.3 %shard_map.59 = (bf16[192,4864]{1,0:T(8,128)(2,1)S(1)}, bf16[64,4864]{1,0:T(8,128)(2,1)S(1)}, bf16[64,4864]{1,0:T(8,128)(2,1)S(1)}, bf16[64,4864]{1,0:T(8,128)(2,1)S(1)}) custom-call(bf16[512,1024]{1,0:T(8,128)(2,1)S(1)} %get-tuple-element.38.refs_3_.refs_4_.refs_0_, bf16[1024,2432]{1,0:T(8,128)(2,1)S(1)} %get-tuple-element.48.refs_5_.refs_1_.refs_2_, ...), custom_call_target="tpu_custom_call" | custom-call | flops 3825205248 | bytes 64 | tf_op jit(solution)/shard_map/pallas_call | solution.py:57
  77.3 5.8 %shard_map.60 = bf16[512,1024]{1,0:T(8,128)(2,1)S(1)} custom-call(bf16[512,2432]{1,0:T(8,128)(2,1)S(1)} %copy-done.3, bf16[512,2432]{1,0:T(8,128)(2,1)S(1)} %copy-done.2, bf16[1024,2432]{1,0:T(8,128)(2,1)S(1)} %get-tuple-element.48.refs_5_.refs_1_.refs_2_, bf16[1024,2432]{1,0:T(8,128)(2,1)S(1)} %get-tuple-element.51.refs_2_.refs_3_, ...), custom_call_target="tpu_custom_call" | custom-call | flops 5100273664 | bytes 64 | tf_op jit(solution)/shard_map/pallas_call | solution.py:57
  83.2 2.1 %collective-permute-start.23 = (bf16[128,1024]{1,0:T(8,128)(2,1)S(1)}, bf16[128,1024]{1,0:T(8,128)(2,1)S(1)}, u32[]{:S(2)}, u32[]{:S(2)}) collective-permute-start(bf16[128,1024]{1,0:T(8,128)(2,1)S(1)} %get-tuple-element.71), channel_id=1, source_target_pairs={{0,12},{1,13},{2,14},{3,15},{4,0},{5,1},{6,2},{7,3},{8,4},{9,5},{1... | collective-permute-start | bytes 786440 | tf_op jit(solution)/shard_map/ppermute | solution.py:43
  87.3 3.2 %collective-permute-start.35 = (bf16[64,4864]{1,0:T(8,128)(2,1)S(1)}, bf16[64,4864]{1,0:T(8,128)(2,1)S(1)}, u32[]{:S(2)}, u32[]{:S(2)}) collective-permute-start(bf16[64,4864]{1,0:T(8,128)(2,1)S(1)} %get-tuple-element.63), channel_id=1, source_target_pairs={{0,96},{16,112},{32,0},{48,16},{64,32},{80,48},{96,64},{112,80},{1... | collective-permute-start | bytes 1867784 | tf_op jit(solution)/shard_map/ppermute | solution.py:30
  90.5 5.2 %collective-permute-done.25 = bf16[128,1024]{1,0:T(8,128)(2,1)S(1)} collective-permute-done((bf16[128,1024]{1,0:T(8,128)(2,1)S(1)}, bf16[128,1024]{1,0:T(8,128)(2,1)S(1)}, u32[]{:S(2)}, u32[]{:S(2)}) %collective-permute-start.25) | collective-permute-done | bytes 262176 | tf_op jit(solution)/shard_map/ppermute | solution.py:43
  95.9 2.1 %collective-permute-start.26 = (bf16[32,1024]{1,0:T(8,128)(2,1)S(1)}, bf16[32,1024]{1,0:T(8,128)(2,1)S(1)}, u32[]{:S(2)}, u32[]{:S(2)}) collective-permute-start(bf16[32,1024]{1,0:T(8,128)(2,1)S(1)} %get-tuple-element.74), channel_id=1, source_target_pairs={{0,3},{1,0},{2,1},{3,2},{4,7},{5,4},{6,5},{7,6},{8,11},{9,8},{10,9... | collective-permute-start | bytes 196616 | tf_op jit(solution)/shard_map/ppermute | solution.py:43
  100.2 3.9 %collective-permute-done.28 = bf16[32,1024]{1,0:T(8,128)(2,1)S(1)} collective-permute-done((bf16[32,1024]{1,0:T(8,128)(2,1)S(1)}, bf16[32,1024]{1,0:T(8,128)(2,1)S(1)}, u32[]{:S(2)}, u32[]{:S(2)}) %collective-permute-start.28) | collective-permute-done | bytes 65568 | tf_op jit(solution)/shard_map/ppermute | solution.py:43
  (94 shorter events, 26.8 us)
Async XLA Ops:
  0.6 25.2 %collective-permute-start.2 = (bf16[64,4864]{1,0:T(8,128)(2,1)}, bf16[64,4864]{1,0:T(8,128)(2,1)S(1)}, u32[]{:S(2)}, u32[]{:S(2)}) collective-permute-start(bf16[64,4864]{1,0:T(8,128)(2,1)} %bitcast.9), channel_id=1, source_target_pairs={{0,96},{16,112},{32,0},{48,16},{64,32},{80,48},{96,64},{112,80},{1... | collective-permute-start | bytes 1867784 | tf_op jit(solution)/shard_map/ppermute | solution.py:30
  3.5 22.3 %collective-permute-start.1 = (bf16[64,4864]{1,0:T(8,128)(2,1)}, bf16[64,4864]{1,0:T(8,128)(2,1)S(1)}, u32[]{:S(2)}, u32[]{:S(2)}) collective-permute-start(bf16[64,4864]{1,0:T(8,128)(2,1)} %bitcast.10), channel_id=1, source_target_pairs={{0,32},{16,48},{32,64},{48,80},{64,96},{80,112},{96,0},{112,16},{1... | collective-permute-start | bytes 1867784 | tf_op jit(solution)/shard_map/ppermute | solution.py:30
  6.6 6.0 %collective-permute-start.4 = (bf16[32,1024]{1,0:T(8,128)(2,1)}, bf16[32,1024]{1,0:T(8,128)(2,1)S(1)}, u32[]{:S(2)}, u32[]{:S(2)}) collective-permute-start(bf16[32,1024]{1,0:T(8,128)(2,1)} %bitcast.14), channel_id=1, source_target_pairs={{0,2},{1,3},{2,0},{3,1},{4,6},{5,7},{6,4},{7,5},{8,10},{9,11},{10,... | collective-permute-start | bytes 196616 | tf_op jit(solution)/shard_map/ppermute | solution.py:43
  7.2 6.1 %collective-permute-start.3 = (bf16[32,1024]{1,0:T(8,128)(2,1)}, bf16[32,1024]{1,0:T(8,128)(2,1)S(1)}, u32[]{:S(2)}, u32[]{:S(2)}) collective-permute-start(bf16[32,1024]{1,0:T(8,128)(2,1)} %bitcast.15), channel_id=1, source_target_pairs={{0,1},{1,2},{2,3},{3,0},{4,5},{5,6},{6,7},{7,4},{8,9},{9,10},{10,1... | collective-permute-start | bytes 196616 | tf_op jit(solution)/shard_map/ppermute | solution.py:43
  14.1 8.0 %collective-permute-start.7 = (bf16[128,1024]{1,0:T(8,128)(2,1)S(1)}, bf16[128,1024]{1,0:T(8,128)(2,1)S(1)}, u32[]{:S(2)}, u32[]{:S(2)}) collective-permute-start(bf16[128,1024]{1,0:T(8,128)(2,1)S(1)} %pad_maximum_fusion), channel_id=1, source_target_pairs={{0,12},{1,13},{2,14},{3,15},{4,0},{5,1},{6,2},{7,3},{8,4},{9,5},{1... | collective-permute-start | bytes 786440 | tf_op jit(solution)/shard_map/ppermute | solution.py:43
  18.2 7.6 %collective-permute-start.6 = (bf16[128,1024]{1,0:T(8,128)(2,1)S(1)}, bf16[128,1024]{1,0:T(8,128)(2,1)S(1)}, u32[]{:S(2)}, u32[]{:S(2)}) collective-permute-start(bf16[128,1024]{1,0:T(8,128)(2,1)S(1)} %pad_maximum_fusion), channel_id=1, source_target_pairs={{0,4},{1,5},{2,6},{3,7},{4,8},{5,9},{6,10},{7,11},{8,12},{9,13},{1... | collective-permute-start | bytes 786440 | tf_op jit(solution)/shard_map/ppermute | solution.py:43
  18.2 11.6 %collective-permute-start = (bf16[64,4864]{1,0:T(8,128)(2,1)}, bf16[64,4864]{1,0:T(8,128)(2,1)S(1)}, u32[]{:S(2)}, u32[]{:S(2)}) collective-permute-start(bf16[64,4864]{1,0:T(8,128)(2,1)} %bitcast.11), channel_id=1, source_target_pairs={{0,16},{16,0},{32,48},{48,32},{64,80},{80,64},{96,112},{112,96},{1... | collective-permute-start | bytes 1867784 | tf_op jit(solution)/shard_map/ppermute | solution.py:26
  26.5 11.8 %collective-permute-start.12 = (bf16[32,4864]{1,0:T(8,128)(2,1)S(1)}, bf16[32,4864]{1,0:T(8,128)(2,1)S(1)}, u32[]{:S(2)}, u32[]{:S(2)}) collective-permute-start(bf16[32,4864]{1,0:T(8,128)(2,1)S(1)} %slice.99), channel_id=1, source_target_pairs={{0,96},{16,112},{32,0},{48,16},{64,32},{80,48},{96,64},{112,80},{1... | collective-permute-start | bytes 933896 | tf_op jit(solution)/shard_map/ppermute | solution.py:30
  29.8 10.3 %collective-permute-start.11 = (bf16[32,4864]{1,0:T(8,128)(2,1)S(1)}, bf16[32,4864]{1,0:T(8,128)(2,1)S(1)}, u32[]{:S(2)}, u32[]{:S(2)}) collective-permute-start(bf16[32,4864]{1,0:T(8,128)(2,1)S(1)} %slice.98), channel_id=1, source_target_pairs={{0,32},{16,48},{32,64},{48,80},{64,96},{80,112},{96,0},{112,16},{1... | collective-permute-start | bytes 933896 | tf_op jit(solution)/shard_map/ppermute | solution.py:30
  29.8 7.9 %collective-permute-start.10 = (bf16[128,1024]{1,0:T(8,128)(2,1)S(1)}, bf16[128,1024]{1,0:T(8,128)(2,1)S(1)}, u32[]{:S(2)}, u32[]{:S(2)}) collective-permute-start(bf16[128,1024]{1,0:T(8,128)(2,1)S(1)} %pad_maximum_fusion), channel_id=1, source_target_pairs={{0,8},{1,9},{2,10},{3,11},{4,12},{5,13},{6,14},{7,15},{8,0},{9,1},... | collective-permute-start | bytes 786440 | tf_op jit(solution)/shard_map/ppermute | solution.py:43
  40.3 6.0 %collective-permute-start.14 = (bf16[64,2432]{1,0:T(8,128)(2,1)S(1)}, bf16[64,2432]{1,0:T(8,128)(2,1)S(1)}, u32[]{:S(2)}, u32[]{:S(2)}) collective-permute-start(bf16[64,2432]{1,0:T(8,128)(2,1)S(1)} %get-tuple-element.42.refs_2_), channel_id=1, source_target_pairs={{0,16},{16,0},{32,48},{48,32},{64,80},{80,64},{96,112},{112,96},{1... | collective-permute-start | bytes 933896 | tf_op jit(solution)/shard_map/ppermute | solution.py:26
  58.4 5.5 %collective-permute-start.18 = (f32[24,128]{1,0:T(8,128)S(1)}, f32[24,128]{1,0:T(8,128)S(1)}, u32[]{:S(2)}, u32[]{:S(2)}) collective-permute-start(f32[24,128]{1,0:T(8,128)S(1)} %pad_maximum_fusion.2), channel_id=1, source_target_pairs={{0,4},{1,5},{2,6},{3,7},{4,8},{5,9},{6,10},{7,11},{8,12},{9,13},{1... | collective-permute-start | bytes 36872 | tf_op jit(solution)/shard_map/ppermute | solution.py:43
  70.2 13.0 %collective-permute-start.33 = (bf16[32,4864]{1,0:T(8,128)(2,1)S(1)}, bf16[32,4864]{1,0:T(8,128)(2,1)S(1)}, u32[]{:S(2)}, u32[]{:S(2)}) collective-permute-start(bf16[32,4864]{1,0:T(8,128)(2,1)S(1)} %get-tuple-element.61), channel_id=1, source_target_pairs={{0,96},{16,112},{32,0},{48,16},{64,32},{80,48},{96,64},{112,80},{1... | collective-permute-start | bytes 933896 | tf_op jit(solution)/shard_map/ppermute | solution.py:30
  71.7 13.5 %collective-permute-start.32 = (bf16[32,4864]{1,0:T(8,128)(2,1)S(1)}, bf16[32,4864]{1,0:T(8,128)(2,1)S(1)}, u32[]{:S(2)}, u32[]{:S(2)}) collective-permute-start(bf16[32,4864]{1,0:T(8,128)(2,1)S(1)} %get-tuple-element.56.refs_3_), channel_id=1, source_target_pairs={{0,32},{16,48},{32,64},{48,80},{64,96},{80,112},{96,0},{112,16},{1... | collective-permute-start | bytes 933896 | tf_op jit(solution)/shard_map/ppermute | solution.py:30
  76.6 8.7 %collective-permute-start.29 = (bf16[64,4864]{1,0:T(8,128)(2,1)S(1)}, bf16[64,4864]{1,0:T(8,128)(2,1)S(1)}, u32[]{:S(2)}, u32[]{:S(2)}) collective-permute-start(bf16[64,4864]{1,0:T(8,128)(2,1)S(1)} %get-tuple-element.58), channel_id=1, source_target_pairs={{0,16},{16,0},{32,48},{48,32},{64,80},{80,64},{96,112},{112,96},{1... | collective-permute-start | bytes 1867784 | tf_op jit(solution)/shard_map/ppermute | solution.py:26
  76.7 10.1 %collective-permute-start.30 = (bf16[64,4864]{1,0:T(8,128)(2,1)S(1)}, bf16[64,4864]{1,0:T(8,128)(2,1)S(1)}, u32[]{:S(2)}, u32[]{:S(2)}) collective-permute-start(bf16[64,4864]{1,0:T(8,128)(2,1)S(1)} %get-tuple-element.59), channel_id=1, source_target_pairs={{0,16},{16,0},{32,48},{48,32},{64,80},{80,64},{96,112},{112,96},{1... | collective-permute-start | bytes 1867784 | tf_op jit(solution)/shard_map/ppermute | solution.py:26
  77.2 9.6 %collective-permute-start.31 = (bf16[64,4864]{1,0:T(8,128)(2,1)S(1)}, bf16[64,4864]{1,0:T(8,128)(2,1)S(1)}, u32[]{:S(2)}, u32[]{:S(2)}) collective-permute-start(bf16[64,4864]{1,0:T(8,128)(2,1)S(1)} %get-tuple-element.60), channel_id=1, source_target_pairs={{0,16},{16,0},{32,48},{48,32},{64,80},{80,64},{96,112},{112,96},{1... | collective-permute-start | bytes 1867784 | tf_op jit(solution)/shard_map/ppermute | solution.py:26
  83.2 7.3 %collective-permute-start.23 = (bf16[128,1024]{1,0:T(8,128)(2,1)S(1)}, bf16[128,1024]{1,0:T(8,128)(2,1)S(1)}, u32[]{:S(2)}, u32[]{:S(2)}) collective-permute-start(bf16[128,1024]{1,0:T(8,128)(2,1)S(1)} %get-tuple-element.71), channel_id=1, source_target_pairs={{0,12},{1,13},{2,14},{3,15},{4,0},{5,1},{6,2},{7,3},{8,4},{9,5},{1... | collective-permute-start | bytes 786440 | tf_op jit(solution)/shard_map/ppermute | solution.py:43
  85.3 10.4 %collective-permute-start.25 = (bf16[128,1024]{1,0:T(8,128)(2,1)S(1)}, bf16[128,1024]{1,0:T(8,128)(2,1)S(1)}, u32[]{:S(2)}, u32[]{:S(2)}) collective-permute-start(bf16[128,1024]{1,0:T(8,128)(2,1)S(1)} %get-tuple-element.72), channel_id=1, source_target_pairs={{0,4},{1,5},{2,6},{3,7},{4,8},{5,9},{6,10},{7,11},{8,12},{9,13},{1... | collective-permute-start | bytes 786440 | tf_op jit(solution)/shard_map/ppermute | solution.py:43
  85.3 10.4 %collective-permute-start.24 = (bf16[128,1024]{1,0:T(8,128)(2,1)S(1)}, bf16[128,1024]{1,0:T(8,128)(2,1)S(1)}, u32[]{:S(2)}, u32[]{:S(2)}) collective-permute-start(bf16[128,1024]{1,0:T(8,128)(2,1)S(1)} %get-tuple-element.73), channel_id=1, source_target_pairs={{0,8},{1,9},{2,10},{3,11},{4,12},{5,13},{6,14},{7,15},{8,0},{9,1},... | collective-permute-start | bytes 786440 | tf_op jit(solution)/shard_map/ppermute | solution.py:43
  87.2 17.6 %collective-permute-start.34 = (bf16[64,4864]{1,0:T(8,128)(2,1)S(1)}, bf16[64,4864]{1,0:T(8,128)(2,1)S(1)}, u32[]{:S(2)}, u32[]{:S(2)}) collective-permute-start(bf16[64,4864]{1,0:T(8,128)(2,1)S(1)} %get-tuple-element.62), channel_id=1, source_target_pairs={{0,32},{16,48},{32,64},{48,80},{64,96},{80,112},{96,0},{112,16},{1... | collective-permute-start | bytes 1867784 | tf_op jit(solution)/shard_map/ppermute | solution.py:30
  87.3 17.5 %collective-permute-start.35 = (bf16[64,4864]{1,0:T(8,128)(2,1)S(1)}, bf16[64,4864]{1,0:T(8,128)(2,1)S(1)}, u32[]{:S(2)}, u32[]{:S(2)}) collective-permute-start(bf16[64,4864]{1,0:T(8,128)(2,1)S(1)} %get-tuple-element.63), channel_id=1, source_target_pairs={{0,96},{16,112},{32,0},{48,16},{64,32},{80,48},{96,64},{112,80},{1... | collective-permute-start | bytes 1867784 | tf_op jit(solution)/shard_map/ppermute | solution.py:30
  97.9 6.2 %collective-permute-start.28 = (bf16[32,1024]{1,0:T(8,128)(2,1)S(1)}, bf16[32,1024]{1,0:T(8,128)(2,1)S(1)}, u32[]{:S(2)}, u32[]{:S(2)}) collective-permute-start(bf16[32,1024]{1,0:T(8,128)(2,1)S(1)} %get-tuple-element.75), channel_id=1, source_target_pairs={{0,1},{1,2},{2,3},{3,0},{4,5},{5,6},{6,7},{7,4},{8,9},{9,10},{10,1... | collective-permute-start | bytes 196616 | tf_op jit(solution)/shard_map/ppermute | solution.py:43
  97.9 6.2 %collective-permute-start.27 = (bf16[32,1024]{1,0:T(8,128)(2,1)S(1)}, bf16[32,1024]{1,0:T(8,128)(2,1)S(1)}, u32[]{:S(2)}, u32[]{:S(2)}) collective-permute-start(bf16[32,1024]{1,0:T(8,128)(2,1)S(1)} %get-tuple-element.76), channel_id=1, source_target_pairs={{0,2},{1,3},{2,0},{3,1},{4,6},{5,7},{6,4},{7,5},{8,10},{9,11},{10,... | collective-permute-start | bytes 196616 | tf_op jit(solution)/shard_map/ppermute | solution.py:43
  (21 other events, 148.5 us)

commit v5 on v4

--- a/solution.py
+++ b/solution.py
@@ -243,7 +243,7 @@
     block = jnp.concatenate(first_parts, axis=0)
     later = [shift(block, 1, k) for k in (1, 2, 3)]
     t1 = core_swap(own)
-    t2, t4 = run(hold_kernel, [((64, COLS), BF16)] * 2, t2, t4, wait=(later[0], later[2]))
+    t2, t4 = run(hold_kernel, [((64, COLS), BF16)] * 2, t2, t4, wait=(later[0],))
 
     row_counts, *near = run(
         gather_kernel,

time: 107 us -> 107 us (level)
  waiting for transfers between devices: 36.9 us -> 33.4 us
  starting transfers between devices: 35.2 us -> 38 us
    ppermute x18, waiting for transfers between devices: 32.8 us -> 30.1 us  [shift(): return lax.ppermute(a, ('state', 'vocab'), perm)]
    ppermute x18, starting transfers between devices: 20.9 us -> 23.3 us  [shift(): return lax.ppermute(a, ('state', 'vocab'), perm)]
where the time goes in v5:
time: 107 us; the launch traced here: 105 us
  starting transfers between devices  38 us (36%)
  waiting for transfers between devices  33.4 us (31%)
  Pallas kernels  29.7 us (28%)
  other arithmetic  1.75 us (2%)
  local copies, waits for them, and re-layouts  1.22 us (1%)
  between operations  1.15 us (1%)
    ppermute x18, waiting for transfers between devices, shift(): return lax.ppermute(a, ('state', 'vocab'), perm)  30.1 us
    pallas_call x13, Pallas kernels, run(): pl.pallas_call(wrapped, out_shape=tuple(((space[0] if space else VMEM)(sh...  29.7 us
    ppermute x18, starting transfers between devices, shift(): return lax.ppermute(a, ('state', 'vocab'), perm)  23.3 us
    ppermute x8, starting transfers between devices, x_shift(): return lax.ppermute(a, 'state', [(i, (i + 2 * step) % 8) for i in range(8)])  12 us
    ppermute x10, starting transfers between devices, core_swap(): return lax.ppermute(a, 'state', [(i, i ^ 1) for i in range(8)])  2.71 us
    ppermute x10, waiting for transfers between devices, core_swap(): return lax.ppermute(a, 'state', [(i, i ^ 1) for i in range(8)])  2.34 us
  transfers between devices with their start and end apart: 36, of which 18 were waited for; matrix products, arithmetic and copies ran while one was open for 2% of the time, Pallas kernels for 21%

profile of v5, /device:TPU:0, one launch (start us, length us, event | category | flops | bytes accessed | tf_op | source)
XLA Modules:
  0.0 105.3 jit_solution(7328911561842145697)
XLA Ops:
  0.6 2.9 %collective-permute-start.2 = (bf16[64,4864]{1,0:T(8,128)(2,1)}, bf16[64,4864]{1,0:T(8,128)(2,1)S(1)}, u32[]{:S(2)}, u32[]{:S(2)}) collective-permute-start(bf16[64,4864]{1,0:T(8,128)(2,1)} %bitcast.9), channel_id=1, source_target_pairs={{0,96},{16,112},{32,0},{48,16},{64,32},{80,48},{96,64},{112,80},{1... | collective-permute-start | bytes 1867784 | tf_op jit(solution)/shard_map/ppermute | solution.py:30
  3.5 3.0 %collective-permute-start.5 = (bf16[32,1024]{1,0:T(8,128)(2,1)}, bf16[32,1024]{1,0:T(8,128)(2,1)S(1)}, u32[]{:S(2)}, u32[]{:S(2)}) collective-permute-start(bf16[32,1024]{1,0:T(8,128)(2,1)} %bitcast.13), channel_id=1, source_target_pairs={{0,3},{1,0},{2,1},{3,2},{4,7},{5,4},{6,5},{7,6},{8,11},{9,8},{10,9... | collective-permute-start | bytes 196616 | tf_op jit(solution)/shard_map/ppermute | solution.py:43
  8.8 3.8 %collective-permute-done.4.refs_2_ = bf16[32,1024]{1,0:T(8,128)(2,1)S(1)} collective-permute-done((bf16[32,1024]{1,0:T(8,128)(2,1)}, bf16[32,1024]{1,0:T(8,128)(2,1)S(1)}, u32[]{:S(2)}, u32[]{:S(2)}) %collective-permute-start.4) | collective-permute-done | bytes 65568 | tf_op jit(solution)/shard_map/ppermute | solution.py:43
  14.1 2.0 %collective-permute-start.6 = (bf16[128,1024]{1,0:T(8,128)(2,1)S(1)}, bf16[128,1024]{1,0:T(8,128)(2,1)S(1)}, u32[]{:S(2)}, u32[]{:S(2)}) collective-permute-start(bf16[128,1024]{1,0:T(8,128)(2,1)S(1)} %pad_maximum_fusion), channel_id=1, source_target_pairs={{0,4},{1,5},{2,6},{3,7},{4,8},{5,9},{6,10},{7,11},{8,12},{9,13},{1... | collective-permute-start | bytes 786440 | tf_op jit(solution)/shard_map/ppermute | solution.py:43
  16.1 6.5 %collective-permute-done.6.refs_2_.refs_4_ = bf16[128,1024]{1,0:T(8,128)(2,1)S(1)} collective-permute-done((bf16[128,1024]{1,0:T(8,128)(2,1)S(1)}, bf16[128,1024]{1,0:T(8,128)(2,1)S(1)}, u32[]{:S(2)}, u32[]{:S(2)}) %collective-permute-start.6) | collective-permute-done | bytes 262176 | tf_op jit(solution)/shard_map/ppermute | solution.py:43
  23.3 3.3 %collective-permute-start.12 = (bf16[32,4864]{1,0:T(8,128)(2,1)S(1)}, bf16[32,4864]{1,0:T(8,128)(2,1)S(1)}, u32[]{:S(2)}, u32[]{:S(2)}) collective-permute-start(bf16[32,4864]{1,0:T(8,128)(2,1)S(1)} %slice.99), channel_id=1, source_target_pairs={{0,96},{16,112},{32,0},{48,16},{64,32},{80,48},{96,64},{112,80},{1... | collective-permute-start | bytes 933896 | tf_op jit(solution)/shard_map/ppermute | solution.py:30
  26.6 2.0 %collective-permute-start.10 = (bf16[128,1024]{1,0:T(8,128)(2,1)S(1)}, bf16[128,1024]{1,0:T(8,128)(2,1)S(1)}, u32[]{:S(2)}, u32[]{:S(2)}) collective-permute-start(bf16[128,1024]{1,0:T(8,128)(2,1)S(1)} %pad_maximum_fusion), channel_id=1, source_target_pairs={{0,12},{1,13},{2,14},{3,15},{4,0},{5,1},{6,2},{7,3},{8,4},{9,5},{1... | collective-permute-start | bytes 786440 | tf_op jit(solution)/shard_map/ppermute | solution.py:43
  29.7 4.4 %shard_map.51 = (f32[8,128]{1,0:T(8,128)S(1)}, bf16[512,2432]{1,0:T(8,128)(2,1)S(1)}, bf16[512,2432]{1,0:T(8,128)(2,1)S(1)}) custom-call(bf16[1024,4864]{1,0:T(8,128)(2,1)} %refs_2_.3, bf16[64,4864]{1,0:T(8,128)(2,1)S(1)} %bitcast.12, bf16[64,4864]{1,0:T(8,128)(2,1)S(1)} %collective-permute-done.refs_2_, bf16[64,4864]{1,0:T(8,128)(2,1)S(1)} %get-tuple-element.33.refs_3_, ...), custom_call_target="tpu_custom_call" | custom-call | flops 2147483648 | bytes 64 | tf_op jit(solution)/shard_map/pallas_call | solution.py:57
  38.9 4.3 %shard_map.54 = (f32[512,2432]{1,0:T(8,128)S(1)}, f32[512,2432]{1,0:T(8,128)S(1)}, f32[16,128]{1,0:T(8,128)S(1)}, bf16[512,2432]{1,0:T(8,128)(2,1)S(1)}, bf16[512,2432]{1,0:T(8,128)(2,1)}) custom-call(bf16[512,2432]{1,0:T(8,128)(2,1)S(1)} %get-tuple-element.35.refs_0_, ...), custom_call_target="tpu_custom_call", output_to_operand_aliasing={{3}: (0, {})} | custom-call | flops 2550136832 | bytes 64 | tf_op jit(solution)/shard_map/pallas_call | solution.py:57
  43.3 4.7 %shard_map.55 = (f32[512,2432]{1,0:T(8,128)}, f32[512,2432]{1,0:T(8,128)S(1)}, f32[16,128]{1,0:T(8,128)S(1)}, bf16[512,2432]{1,0:T(8,128)(2,1)S(1)}, bf16[512,2432]{1,0:T(8,128)(2,1)}) custom-call(bf16[512,2432]{1,0:T(8,128)(2,1)S(1)} %get-tuple-element.41.refs_0_, bf16[1024,512]{1,0:T(8,128)(2,1)S(1)} %get-tuple-element.37.refs_1_, ...), custom_call_target="tpu_custom_call", output_to_operand_aliasing={{3}: (0, {})} | custom-call | flops 2550136832 | bytes 64 | tf_op jit(solution)/shard_map/pallas_call | solution.py:57
  48.0 1.7 %collective-permute-start.17 = (f32[24,128]{1,0:T(8,128)S(1)}, f32[24,128]{1,0:T(8,128)S(1)}, u32[]{:S(2)}, u32[]{:S(2)}) collective-permute-start(f32[24,128]{1,0:T(8,128)S(1)} %pad_maximum_fusion.1), channel_id=1, source_target_pairs={{0,3},{1,0},{2,1},{3,2},{4,7},{5,4},{6,5},{7,6},{8,11},{9,8},{10,9... | collective-permute-start | bytes 36872 | tf_op jit(solution)/shard_map/ppermute | solution.py:43
  51.8 3.2 %collective-permute-done.16 = f32[24,128]{1,0:T(8,128)S(1)} collective-permute-done((f32[24,128]{1,0:T(8,128)S(1)}, f32[24,128]{1,0:T(8,128)S(1)}, u32[]{:S(2)}, u32[]{:S(2)}) %collective-permute-start.16) | collective-permute-done | bytes 12320 | tf_op jit(solution)/shard_map/ppermute | solution.py:43
  55.3 2.6 %collective-permute-start.20 = (f32[24,128]{1,0:T(8,128)S(1)}, f32[24,128]{1,0:T(8,128)S(1)}, u32[]{:S(2)}, u32[]{:S(2)}) collective-permute-start(f32[24,128]{1,0:T(8,128)S(1)} %pad_maximum_fusion.2), channel_id=1, source_target_pairs={{0,12},{1,13},{2,14},{3,15},{4,0},{5,1},{6,2},{7,3},{8,4},{9,5},{1... | collective-permute-start | bytes 36872 | tf_op jit(solution)/shard_map/ppermute | solution.py:43
  59.4 3.8 %collective-permute-done.19 = f32[24,128]{1,0:T(8,128)S(1)} collective-permute-done((f32[24,128]{1,0:T(8,128)S(1)}, f32[24,128]{1,0:T(8,128)S(1)}, u32[]{:S(2)}, u32[]{:S(2)}) %collective-permute-start.19) | collective-permute-done | bytes 12320 | tf_op jit(solution)/shard_map/ppermute | solution.py:43
  63.3 1.9 %shard_map.56 = (bf16[1024,2432]{1,0:T(8,128)(2,1)S(1)}, bf16[64,2432]{1,0:T(8,128)(2,1)S(1)}, bf16[64,2432]{1,0:T(8,128)(2,1)S(1)}) custom-call(f32[512,2432]{1,0:T(8,128)S(1)} %get-tuple-element.43.refs_4_.refs_0_, f32[512,2432]{1,0:T(8,128)S(1)} %get-tuple-element.44.refs_5_.refs_1_, bf16[1024,4864]{1,0:T(8,128)(2,1)S(1)} %bitcast.6, ...), custom_call_target="tpu_custom_call" | custom-call | flops 1275068416 | bytes 64 | tf_op jit(solution)/shard_map/pallas_call | solution.py:57
  65.5 2.0 %shard_map.57 = (bf16[1024,2432]{1,0:T(8,128)(2,1)S(1)}, bf16[64,2432]{1,0:T(8,128)(2,1)S(1)}, bf16[64,2432]{1,0:T(8,128)(2,1)S(1)}) custom-call(f32[512,2432]{1,0:T(8,128)S(1)} %bitcast.8, f32[512,2432]{1,0:T(8,128)S(1)} %get-tuple-element.50.refs_1_, bf16[1024,4864]{1,0:T(8,128)(2,1)S(1)} %bitcast.6, f32[8,128]{1,0:T(8,128)S(1)} %get-tuple-element.64.refs_3_, ...), custom_call_target="tpu_custom_call" | custom-call | flops 1275068416 | bytes 64 | tf_op jit(solution)/shard_map/pallas_call | solution.py:57
  69.4 2.4 %collective-permute-start.33 = (bf16[32,4864]{1,0:T(8,128)(2,1)S(1)}, bf16[32,4864]{1,0:T(8,128)(2,1)S(1)}, u32[]{:S(2)}, u32[]{:S(2)}) collective-permute-start(bf16[32,4864]{1,0:T(8,128)(2,1)S(1)} %get-tuple-element.61), channel_id=1, source_target_pairs={{0,96},{16,112},{32,0},{48,16},{64,32},{80,48},{96,64},{112,80},{1... | collective-permute-start | bytes 933896 | tf_op jit(solution)/shard_map/ppermute | solution.py:30
  71.9 4.3 %shard_map.59 = (bf16[192,4864]{1,0:T(8,128)(2,1)S(1)}, bf16[64,4864]{1,0:T(8,128)(2,1)S(1)}, bf16[64,4864]{1,0:T(8,128)(2,1)S(1)}, bf16[64,4864]{1,0:T(8,128)(2,1)S(1)}) custom-call(bf16[512,1024]{1,0:T(8,128)(2,1)S(1)} %get-tuple-element.38.refs_3_.refs_4_.refs_0_, bf16[1024,2432]{1,0:T(8,128)(2,1)S(1)} %get-tuple-element.48.refs_5_.refs_1_.refs_2_, ...), custom_call_target="tpu_custom_call" | custom-call | flops 3825205248 | bytes 64 | tf_op jit(solution)/shard_map/pallas_call | solution.py:57
  76.9 5.8 %shard_map.60 = bf16[512,1024]{1,0:T(8,128)(2,1)S(1)} custom-call(bf16[512,2432]{1,0:T(8,128)(2,1)S(1)} %copy-done.3, bf16[512,2432]{1,0:T(8,128)(2,1)S(1)} %copy-done.2, bf16[1024,2432]{1,0:T(8,128)(2,1)S(1)} %get-tuple-element.48.refs_5_.refs_1_.refs_2_, bf16[1024,2432]{1,0:T(8,128)(2,1)S(1)} %get-tuple-element.51.refs_2_.refs_3_, ...), custom_call_target="tpu_custom_call" | custom-call | flops 5100273664 | bytes 64 | tf_op jit(solution)/shard_map/pallas_call | solution.py:57
  84.8 2.0 %collective-permute-start.24 = (bf16[128,1024]{1,0:T(8,128)(2,1)S(1)}, bf16[128,1024]{1,0:T(8,128)(2,1)S(1)}, u32[]{:S(2)}, u32[]{:S(2)}) collective-permute-start(bf16[128,1024]{1,0:T(8,128)(2,1)S(1)} %get-tuple-element.73), channel_id=1, source_target_pairs={{0,8},{1,9},{2,10},{3,11},{4,12},{5,13},{6,14},{7,15},{8,0},{9,1},... | collective-permute-start | bytes 786440 | tf_op jit(solution)/shard_map/ppermute | solution.py:43
  87.3 3.3 %collective-permute-start.35 = (bf16[64,4864]{1,0:T(8,128)(2,1)S(1)}, bf16[64,4864]{1,0:T(8,128)(2,1)S(1)}, u32[]{:S(2)}, u32[]{:S(2)}) collective-permute-start(bf16[64,4864]{1,0:T(8,128)(2,1)S(1)} %get-tuple-element.63), channel_id=1, source_target_pairs={{0,96},{16,112},{32,0},{48,16},{64,32},{80,48},{96,64},{112,80},{1... | collective-permute-start | bytes 1867784 | tf_op jit(solution)/shard_map/ppermute | solution.py:30
  91.1 2.9 %collective-permute-done.24 = bf16[128,1024]{1,0:T(8,128)(2,1)S(1)} collective-permute-done((bf16[128,1024]{1,0:T(8,128)(2,1)S(1)}, bf16[128,1024]{1,0:T(8,128)(2,1)S(1)}, u32[]{:S(2)}, u32[]{:S(2)}) %collective-permute-start.24) | collective-permute-done | bytes 262176 | tf_op jit(solution)/shard_map/ppermute | solution.py:43
  94.2 2.1 %collective-permute-start.26 = (bf16[32,1024]{1,0:T(8,128)(2,1)S(1)}, bf16[32,1024]{1,0:T(8,128)(2,1)S(1)}, u32[]{:S(2)}, u32[]{:S(2)}) collective-permute-start(bf16[32,1024]{1,0:T(8,128)(2,1)S(1)} %get-tuple-element.74), channel_id=1, source_target_pairs={{0,3},{1,0},{2,1},{3,2},{4,7},{5,4},{6,5},{7,6},{8,11},{9,8},{10,9... | collective-permute-start | bytes 196616 | tf_op jit(solution)/shard_map/ppermute | solution.py:43
  98.6 3.9 %collective-permute-done.28 = bf16[32,1024]{1,0:T(8,128)(2,1)S(1)} collective-permute-done((bf16[32,1024]{1,0:T(8,128)(2,1)S(1)}, bf16[32,1024]{1,0:T(8,128)(2,1)S(1)}, u32[]{:S(2)}, u32[]{:S(2)}) %collective-permute-start.28) | collective-permute-done | bytes 65568 | tf_op jit(solution)/shard_map/ppermute | solution.py:43
  (94 shorter events, 25.2 us)
Async XLA Ops:
  0.6 21.9 %collective-permute-start.2 = (bf16[64,4864]{1,0:T(8,128)(2,1)}, bf16[64,4864]{1,0:T(8,128)(2,1)S(1)}, u32[]{:S(2)}, u32[]{:S(2)}) collective-permute-start(bf16[64,4864]{1,0:T(8,128)(2,1)} %bitcast.9), channel_id=1, source_target_pairs={{0,96},{16,112},{32,0},{48,16},{64,32},{80,48},{96,64},{112,80},{1... | collective-permute-start | bytes 1867784 | tf_op jit(solution)/shard_map/ppermute | solution.py:30
  3.5 19.0 %collective-permute-start.1 = (bf16[64,4864]{1,0:T(8,128)(2,1)}, bf16[64,4864]{1,0:T(8,128)(2,1)S(1)}, u32[]{:S(2)}, u32[]{:S(2)}) collective-permute-start(bf16[64,4864]{1,0:T(8,128)(2,1)} %bitcast.10), channel_id=1, source_target_pairs={{0,32},{16,48},{32,64},{48,80},{64,96},{80,112},{96,0},{112,16},{1... | collective-permute-start | bytes 1867784 | tf_op jit(solution)/shard_map/ppermute | solution.py:30
  6.6 6.0 %collective-permute-start.4 = (bf16[32,1024]{1,0:T(8,128)(2,1)}, bf16[32,1024]{1,0:T(8,128)(2,1)S(1)}, u32[]{:S(2)}, u32[]{:S(2)}) collective-permute-start(bf16[32,1024]{1,0:T(8,128)(2,1)} %bitcast.14), channel_id=1, source_target_pairs={{0,2},{1,3},{2,0},{3,1},{4,6},{5,7},{6,4},{7,5},{8,10},{9,11},{10,... | collective-permute-start | bytes 196616 | tf_op jit(solution)/shard_map/ppermute | solution.py:43
  7.2 6.1 %collective-permute-start.3 = (bf16[32,1024]{1,0:T(8,128)(2,1)}, bf16[32,1024]{1,0:T(8,128)(2,1)S(1)}, u32[]{:S(2)}, u32[]{:S(2)}) collective-permute-start(bf16[32,1024]{1,0:T(8,128)(2,1)} %bitcast.15), channel_id=1, source_target_pairs={{0,1},{1,2},{2,3},{3,0},{4,5},{5,6},{6,7},{7,4},{8,9},{9,10},{10,1... | collective-permute-start | bytes 196616 | tf_op jit(solution)/shard_map/ppermute | solution.py:43
  14.1 8.5 %collective-permute-start.6 = (bf16[128,1024]{1,0:T(8,128)(2,1)S(1)}, bf16[128,1024]{1,0:T(8,128)(2,1)S(1)}, u32[]{:S(2)}, u32[]{:S(2)}) collective-permute-start(bf16[128,1024]{1,0:T(8,128)(2,1)S(1)} %pad_maximum_fusion), channel_id=1, source_target_pairs={{0,4},{1,5},{2,6},{3,7},{4,8},{5,9},{6,10},{7,11},{8,12},{9,13},{1... | collective-permute-start | bytes 786440 | tf_op jit(solution)/shard_map/ppermute | solution.py:43
  16.1 10.5 %collective-permute-start = (bf16[64,4864]{1,0:T(8,128)(2,1)}, bf16[64,4864]{1,0:T(8,128)(2,1)S(1)}, u32[]{:S(2)}, u32[]{:S(2)}) collective-permute-start(bf16[64,4864]{1,0:T(8,128)(2,1)} %bitcast.11), channel_id=1, source_target_pairs={{0,16},{16,0},{32,48},{48,32},{64,80},{80,64},{96,112},{112,96},{1... | collective-permute-start | bytes 1867784 | tf_op jit(solution)/shard_map/ppermute | solution.py:26
  22.7 6.0 %collective-permute-start.7 = (bf16[64,4864]{1,0:T(8,128)(2,1)S(1)}, bf16[64,4864]{1,0:T(8,128)(2,1)S(1)}, u32[]{:S(2)}, u32[]{:S(2)}) collective-permute-start(bf16[64,4864]{1,0:T(8,128)(2,1)S(1)} %get-tuple-element.33.refs_3_), channel_id=1, source_target_pairs={{0,16},{16,0},{32,48},{48,32},{64,80},{80,64},{96,112},{112,96},{1... | collective-permute-start | bytes 1867784 | tf_op jit(solution)/shard_map/ppermute | solution.py:26
  23.3 13.8 %collective-permute-start.12 = (bf16[32,4864]{1,0:T(8,128)(2,1)S(1)}, bf16[32,4864]{1,0:T(8,128)(2,1)S(1)}, u32[]{:S(2)}, u32[]{:S(2)}) collective-permute-start(bf16[32,4864]{1,0:T(8,128)(2,1)S(1)} %slice.99), channel_id=1, source_target_pairs={{0,96},{16,112},{32,0},{48,16},{64,32},{80,48},{96,64},{112,80},{1... | collective-permute-start | bytes 933896 | tf_op jit(solution)/shard_map/ppermute | solution.py:30
  26.6 10.5 %collective-permute-start.11 = (bf16[32,4864]{1,0:T(8,128)(2,1)S(1)}, bf16[32,4864]{1,0:T(8,128)(2,1)S(1)}, u32[]{:S(2)}, u32[]{:S(2)}) collective-permute-start(bf16[32,4864]{1,0:T(8,128)(2,1)S(1)} %slice.98), channel_id=1, source_target_pairs={{0,32},{16,48},{32,64},{48,80},{64,96},{80,112},{96,0},{112,16},{1... | collective-permute-start | bytes 933896 | tf_op jit(solution)/shard_map/ppermute | solution.py:30
  26.6 8.8 %collective-permute-start.10 = (bf16[128,1024]{1,0:T(8,128)(2,1)S(1)}, bf16[128,1024]{1,0:T(8,128)(2,1)S(1)}, u32[]{:S(2)}, u32[]{:S(2)}) collective-permute-start(bf16[128,1024]{1,0:T(8,128)(2,1)S(1)} %pad_maximum_fusion), channel_id=1, source_target_pairs={{0,12},{1,13},{2,14},{3,15},{4,0},{5,1},{6,2},{7,3},{8,4},{9,5},{1... | collective-permute-start | bytes 786440 | tf_op jit(solution)/shard_map/ppermute | solution.py:43
  28.6 7.9 %collective-permute-start.9 = (bf16[128,1024]{1,0:T(8,128)(2,1)S(1)}, bf16[128,1024]{1,0:T(8,128)(2,1)S(1)}, u32[]{:S(2)}, u32[]{:S(2)}) collective-permute-start(bf16[128,1024]{1,0:T(8,128)(2,1)S(1)} %pad_maximum_fusion), channel_id=1, source_target_pairs={{0,8},{1,9},{2,10},{3,11},{4,12},{5,13},{6,14},{7,15},{8,0},{9,1},... | collective-permute-start | bytes 786440 | tf_op jit(solution)/shard_map/ppermute | solution.py:43
  37.3 5.9 %collective-permute-start.14 = (bf16[64,2432]{1,0:T(8,128)(2,1)S(1)}, bf16[64,2432]{1,0:T(8,128)(2,1)S(1)}, u32[]{:S(2)}, u32[]{:S(2)}) collective-permute-start(bf16[64,2432]{1,0:T(8,128)(2,1)S(1)} %get-tuple-element.42.refs_2_), channel_id=1, source_target_pairs={{0,16},{16,0},{32,48},{48,32},{64,80},{80,64},{96,112},{112,96},{1... | collective-permute-start | bytes 933896 | tf_op jit(solution)/shard_map/ppermute | solution.py:26
  69.4 13.3 %collective-permute-start.33 = (bf16[32,4864]{1,0:T(8,128)(2,1)S(1)}, bf16[32,4864]{1,0:T(8,128)(2,1)S(1)}, u32[]{:S(2)}, u32[]{:S(2)}) collective-permute-start(bf16[32,4864]{1,0:T(8,128)(2,1)S(1)} %get-tuple-element.61), channel_id=1, source_target_pairs={{0,96},{16,112},{32,0},{48,16},{64,32},{80,48},{96,64},{112,80},{1... | collective-permute-start | bytes 933896 | tf_op jit(solution)/shard_map/ppermute | solution.py:30
  71.9 11.6 %collective-permute-start.32 = (bf16[32,4864]{1,0:T(8,128)(2,1)S(1)}, bf16[32,4864]{1,0:T(8,128)(2,1)S(1)}, u32[]{:S(2)}, u32[]{:S(2)}) collective-permute-start(bf16[32,4864]{1,0:T(8,128)(2,1)S(1)} %get-tuple-element.56.refs_3_), channel_id=1, source_target_pairs={{0,32},{16,48},{32,64},{48,80},{64,96},{80,112},{96,0},{112,16},{1... | collective-permute-start | bytes 933896 | tf_op jit(solution)/shard_map/ppermute | solution.py:30
  76.2 8.7 %collective-permute-start.29 = (bf16[64,4864]{1,0:T(8,128)(2,1)S(1)}, bf16[64,4864]{1,0:T(8,128)(2,1)S(1)}, u32[]{:S(2)}, u32[]{:S(2)}) collective-permute-start(bf16[64,4864]{1,0:T(8,128)(2,1)S(1)} %get-tuple-element.58), channel_id=1, source_target_pairs={{0,16},{16,0},{32,48},{48,32},{64,80},{80,64},{96,112},{112,96},{1... | collective-permute-start | bytes 1867784 | tf_op jit(solution)/shard_map/ppermute | solution.py:26
  76.3 10.6 %collective-permute-start.30 = (bf16[64,4864]{1,0:T(8,128)(2,1)S(1)}, bf16[64,4864]{1,0:T(8,128)(2,1)S(1)}, u32[]{:S(2)}, u32[]{:S(2)}) collective-permute-start(bf16[64,4864]{1,0:T(8,128)(2,1)S(1)} %get-tuple-element.59), channel_id=1, source_target_pairs={{0,16},{16,0},{32,48},{48,32},{64,80},{80,64},{96,112},{112,96},{1... | collective-permute-start | bytes 1867784 | tf_op jit(solution)/shard_map/ppermute | solution.py:26
  76.8 10.1 %collective-permute-start.31 = (bf16[64,4864]{1,0:T(8,128)(2,1)S(1)}, bf16[64,4864]{1,0:T(8,128)(2,1)S(1)}, u32[]{:S(2)}, u32[]{:S(2)}) collective-permute-start(bf16[64,4864]{1,0:T(8,128)(2,1)S(1)} %get-tuple-element.60), channel_id=1, source_target_pairs={{0,16},{16,0},{32,48},{48,32},{64,80},{80,64},{96,112},{112,96},{1... | collective-permute-start | bytes 1867784 | tf_op jit(solution)/shard_map/ppermute | solution.py:26
  82.7 7.9 %collective-permute-start.23 = (bf16[128,1024]{1,0:T(8,128)(2,1)S(1)}, bf16[128,1024]{1,0:T(8,128)(2,1)S(1)}, u32[]{:S(2)}, u32[]{:S(2)}) collective-permute-start(bf16[128,1024]{1,0:T(8,128)(2,1)S(1)} %get-tuple-element.71), channel_id=1, source_target_pairs={{0,12},{1,13},{2,14},{3,15},{4,0},{5,1},{6,2},{7,3},{8,4},{9,5},{1... | collective-permute-start | bytes 786440 | tf_op jit(solution)/shard_map/ppermute | solution.py:43
  83.5 7.6 %collective-permute-start.25 = (bf16[128,1024]{1,0:T(8,128)(2,1)S(1)}, bf16[128,1024]{1,0:T(8,128)(2,1)S(1)}, u32[]{:S(2)}, u32[]{:S(2)}) collective-permute-start(bf16[128,1024]{1,0:T(8,128)(2,1)S(1)} %get-tuple-element.72), channel_id=1, source_target_pairs={{0,4},{1,5},{2,6},{3,7},{4,8},{5,9},{6,10},{7,11},{8,12},{9,13},{1... | collective-permute-start | bytes 786440 | tf_op jit(solution)/shard_map/ppermute | solution.py:43
  84.8 9.2 %collective-permute-start.24 = (bf16[128,1024]{1,0:T(8,128)(2,1)S(1)}, bf16[128,1024]{1,0:T(8,128)(2,1)S(1)}, u32[]{:S(2)}, u32[]{:S(2)}) collective-permute-start(bf16[128,1024]{1,0:T(8,128)(2,1)S(1)} %get-tuple-element.73), channel_id=1, source_target_pairs={{0,8},{1,9},{2,10},{3,11},{4,12},{5,13},{6,14},{7,15},{8,0},{9,1},... | collective-permute-start | bytes 786440 | tf_op jit(solution)/shard_map/ppermute | solution.py:43
  87.3 16.9 %collective-permute-start.34 = (bf16[64,4864]{1,0:T(8,128)(2,1)S(1)}, bf16[64,4864]{1,0:T(8,128)(2,1)S(1)}, u32[]{:S(2)}, u32[]{:S(2)}) collective-permute-start(bf16[64,4864]{1,0:T(8,128)(2,1)S(1)} %get-tuple-element.62), channel_id=1, source_target_pairs={{0,32},{16,48},{32,64},{48,80},{64,96},{80,112},{96,0},{112,16},{1... | collective-permute-start | bytes 1867784 | tf_op jit(solution)/shard_map/ppermute | solution.py:30
  87.3 16.8 %collective-permute-start.35 = (bf16[64,4864]{1,0:T(8,128)(2,1)S(1)}, bf16[64,4864]{1,0:T(8,128)(2,1)S(1)}, u32[]{:S(2)}, u32[]{:S(2)}) collective-permute-start(bf16[64,4864]{1,0:T(8,128)(2,1)S(1)} %get-tuple-element.63), channel_id=1, source_target_pairs={{0,96},{16,112},{32,0},{48,16},{64,32},{80,48},{96,64},{112,80},{1... | collective-permute-start | bytes 1867784 | tf_op jit(solution)/shard_map/ppermute | solution.py:30
  96.3 6.2 %collective-permute-start.28 = (bf16[32,1024]{1,0:T(8,128)(2,1)S(1)}, bf16[32,1024]{1,0:T(8,128)(2,1)S(1)}, u32[]{:S(2)}, u32[]{:S(2)}) collective-permute-start(bf16[32,1024]{1,0:T(8,128)(2,1)S(1)} %get-tuple-element.75), channel_id=1, source_target_pairs={{0,1},{1,2},{2,3},{3,0},{4,5},{5,6},{6,7},{7,4},{8,9},{9,10},{10,1... | collective-permute-start | bytes 196616 | tf_op jit(solution)/shard_map/ppermute | solution.py:43
  96.3 6.2 %collective-permute-start.27 = (bf16[32,1024]{1,0:T(8,128)(2,1)S(1)}, bf16[32,1024]{1,0:T(8,128)(2,1)S(1)}, u32[]{:S(2)}, u32[]{:S(2)}) collective-permute-start(bf16[32,1024]{1,0:T(8,128)(2,1)S(1)} %get-tuple-element.76), channel_id=1, source_target_pairs={{0,2},{1,3},{2,0},{3,1},{4,6},{5,7},{6,4},{7,5},{8,10},{9,11},{10,... | collective-permute-start | bytes 196616 | tf_op jit(solution)/shard_map/ppermute | solution.py:43
  (21 other events, 162.7 us)
